TPU v7x, 32 devices: a whole 2x2x4 slice. The times are simulated.
32 devices in a mesh: pop: 2 (over y), ctx: 4 (over z), exp: 2 (over x), tp: 2 (over core).
Axes of the slice: x: 2, y: 2, z: 4, core: 2. Of those that a mesh axis runs over, the one named last changes fastest.
Arguments:
- tokens: bfloat16 [2048, 2688], P(('pop', 'ctx', 'tp')), parts along dimension 0, may hold values from -6 to 6
- routes: int32 [2048, 6], P(('pop', 'ctx', 'tp')), parts along dimension 0, may hold values from 0 to 15, all different within a row; in each aligned block of 128 rows (0 to 127, 128 to 255, ...) at most 64 rows name the same one
- route_gates: float32 [2048, 6], P(('pop', 'ctx', 'tp')), parts along dimension 0, may hold values from 0.05 to 1
- up_weight: bfloat16 [16, 2688, 1536], P(('ctx', 'tp'), None, 'exp'), may hold values from -0.125 to 0.125
- down_weight: bfloat16 [16, 1536, 2688], P(('ctx', 'tp'), None, 'exp'), may hold values from -0.15625 to 0.15625
- factor_seeds: int32 [32, 4], P(('pop', 'ctx', 'tp')), parts along dimension 0, may hold values from 0 to 15
- up_left: bfloat16 [16, 2688], replicated, may hold values from -0.125 to 0.125
- up_right: bfloat16 [16, 1536], P(None, 'exp'), may hold values from -3 to 3
- down_left: bfloat16 [16, 1536], replicated, may hold values from -0.15625 to 0.15625
- down_right: bfloat16 [16, 2688], P(None, 'exp'), may hold values from -3 to 3
Outputs:
- moe_output: bfloat16 [2048, 2688], P(('pop', 'ctx', 'tp'), 'exp'), parts along dimension 0
There are 2 independent parts, one for each index of `pop`. A program takes and returns all parts, laid end to end along the dimension named above; an argument that names none is the same for every part. Nothing has to cross between parts.
Inputs may be any that keep to these rules, and one draw needn't show every extreme that they name: `routes`: each row names 6 different experts. Among the 128 rows of one device (aligned blocks of 128 rows) no expert is named more than 64 times, and in every draw some expert is named exactly 64 times in some block.
All inputs are finite; a program needn't handle non-finite values.
Results may differ from a plain program's by a relative error of at most 0.0057.
Values may be sent and summed in bfloat16 or wider, within the bound.
No kernel may reach another device: no remote copies, remote signals or barrier semaphores. Data moves between devices by JAX's collectives and lax.ppermute only.
A program may use at most 64 MiB of HBM per device.

v0:
```python
import jax
import jax.numpy as jnp
from jax import lax
from jax.sharding import PartitionSpec as P


def pick_rows(factor_table, indices):
    chooser = (
        indices[:, None] == jnp.arange(factor_table.shape[0], dtype=jnp.int32)[None, :]
    ).astype(factor_table.dtype)
    return jnp.dot(chooser, factor_table, preferred_element_type=jnp.float32).astype(
        factor_table.dtype
    )


def on_device(
    tokens,
    routes,
    route_gates,
    up_weight,
    down_weight,
    factor_seeds,
    up_left,
    up_right,
    down_left,
    down_right,
):
    dest_count = lax.axis_size("ctx") * lax.axis_size("tp")
    local_experts = up_weight.shape[0]
    experts_all = dest_count * local_experts
    tok_count, top_count = routes.shape
    capacity = 4 * tok_count * top_count // (3 * experts_all)
    model_width = tokens.shape[1]
    flat_routes = routes.reshape(-1)
    chooser = (flat_routes[:, None] == jnp.arange(experts_all, dtype=jnp.int32)[None, :]).astype(
        jnp.int32
    )
    earlier = jnp.cumsum(chooser, axis=0) - chooser
    slot_index = jnp.sum(earlier * chooser, axis=1)
    target = flat_routes * capacity + slot_index
    pair_token = jnp.arange(tok_count * top_count, dtype=jnp.int32) // top_count + 1
    owner_token = jnp.zeros((experts_all * capacity,), jnp.int32).at[target].set(pair_token)
    source_row = jnp.where(owner_token > 0, owner_token - 1, tok_count)
    padded_tokens = jnp.concatenate([tokens, jnp.zeros((1, model_width), tokens.dtype)], axis=0)
    token_rows = padded_tokens[source_row]
    outgoing = token_rows.reshape(dest_count, local_experts, capacity, model_width)
    left_up = pick_rows(up_left, factor_seeds[:, 0])
    right_up = pick_rows(up_right, factor_seeds[:, 1])
    left_down = pick_rows(down_left, factor_seeds[:, 2])
    right_down = pick_rows(down_right, factor_seeds[:, 3])
    buffer = lax.all_to_all(outgoing, ("ctx", "tp"), split_axis=0, concat_axis=0, tiled=True)
    up_act = jnp.einsum("slcd,ldh->slch", buffer, up_weight, preferred_element_type=jnp.float32)
    low_rank = jnp.einsum("slcd,ld->slc", buffer, left_up, preferred_element_type=jnp.float32)
    up_act = up_act + low_rank[..., None] * right_up[None, :, None, :].astype(jnp.float32)
    hidden = (jnp.maximum(up_act, 0.0) ** 2).astype(jnp.bfloat16)
    full_hidden = lax.all_gather(hidden, "exp", axis=3, tiled=True)
    summed = jnp.einsum(
        "slch,lhd->slcd", full_hidden, down_weight, preferred_element_type=jnp.float32
    )
    rank_sum = jnp.einsum(
        "slch,lh->slc", full_hidden, left_down, preferred_element_type=jnp.float32
    )
    result = (
        summed + rank_sum[..., None] * right_down[None, :, None, :].astype(jnp.float32)
    ).astype(jnp.bfloat16)
    returned = lax.all_to_all(result, ("ctx", "tp"), split_axis=0, concat_axis=0, tiled=True)
    back_rows = returned.reshape(experts_all * capacity, -1)
    picked = back_rows[target]
    normed = (route_gates / jnp.sum(route_gates, axis=1, keepdims=True)).reshape(-1)
    weighted = picked.astype(jnp.float32) * normed[:, None]
    moe_output = jnp.sum(weighted.reshape(tok_count, top_count, -1), axis=1)
    return moe_output.astype(jnp.bfloat16)


def solution(mesh):
    in_specs = (
        P(("pop", "ctx", "tp"), None),
        P(("pop", "ctx", "tp"), None),
        P(("pop", "ctx", "tp"), None),
        P(("ctx", "tp"), None, "exp"),
        P(("ctx", "tp"), None, "exp"),
        P(("pop", "ctx", "tp"), None),
        P(),
        P(None, "exp"),
        P(),
        P(None, "exp"),
    )
    out_specs = P(("pop", "ctx", "tp"), "exp")
    return jax.shard_map(
        on_device, mesh=mesh, in_specs=in_specs, out_specs=out_specs, check_vma=False
    )
```

profile of v0, /device:TPU:0, one launch (start us, length us, event | category | flops | bytes accessed | tf_op | source)
XLA Modules:
  0.0 316.3 jit_solution(15399134807292461094)
XLA Ops:
  6.5 0.0 copy-start
  6.5 0.8 copy.28
  7.4 0.1 eq.89
  7.5 0.1 eq.85
  7.6 0.7 broadcast_multiply_fusion
  8.4 1.7 reduce-window.6
  10.1 0.3 slice_reduce_fusion
  10.4 0.1 copy.27
  10.5 0.1 mul.56
  10.6 0.1 fusion.23
  10.7 3.4 %scatter_custom_fusion = s32[1024]{0:T(1024)S(1)} fusion(s32[768]{0:T(1024)S(1)} %fusion.33, s32[768]{0:T(1024)S(1)} %fusion.28, s32[]{:T(128)} %constant.11.clone.1), kind=kCustom, calls=%fused_computation.52 | custom fusion | bytes 4100 | tf_op jit(solution)/shard_map/scatter | solution.py:42
  14.1 1.2 concatenate.3
  15.3 6.6 %gather_fusion = bf16[1024,2688]{1,0:T(8,128)(2,1)} fusion(bf16[129,2688]{1,0:T(8,128)(2,1)S(1)} %concatenate.3, s32[1024]{0:T(1024)S(1)} %fusion.31), kind=kCustom, calls=%fused_computation | custom fusion | bytes 11014144 | tf_op jit(solution)/shard_map/gather | solution.py:45
  21.9 0.0 copy-start.2
  21.9 0.0 copy-start.5
  21.9 6.5 %all-to-all-start = ((bf16[8,2,64,2688]{3,2,1,0:T(8,128)(2,1)}), bf16[8,2,64,2688]{3,2,1,0:T(8,128)(2,1)}, u32[]{:S(2)}, u32[]{:S(2)}) async-start(bf16[8,2,64,2688]{3,2,1,0:T(8,128)(2,1)} %bitcast.67), calls=%async_computation | async-start | bytes 11010048 | tf_op jit(solution)/shard_map/all_to_all | solution.py:51
  28.3 0.0 all-gather.2.cloned.1.call-start
  28.4 0.0 copy-done.2
  28.4 0.2 slice_reduce_fusion.2
  28.6 0.0 copy-done
  28.6 0.2 fusion.10
  28.8 0.0 copy-done.5
  28.8 0.2 fusion.20
  29.0 121.5 %all-to-all-done = bf16[8,2,64,2688]{3,2,1,0:T(8,128)(2,1)} async-done(((bf16[8,2,64,2688]{3,2,1,0:T(8,128)(2,1)}), bf16[8,2,64,2688]{3,2,1,0:T(8,128)(2,1)}, u32[]{:S(2)}, u32[]{:S(2)}) %all-to-all-start) | async-done | bytes 5505056 | tf_op jit(solution)/shard_map/all_to_all | solution.py:51
  150.5 4.9 %fusion.5 = f32[2,1,8,64]{3,1,2,0:T(1,128)S(1)} fusion(bf16[8,2,64,2688]{3,2,1,0:T(8,128)(2,1)} %all-to-all-done, bf16[2,2688,1,1]{1,0,2,3:T(2,128)(2,1)S(1)} %fusion.10), kind=kOutput, calls=%fused_computation.10 | convolution fusion | flops 5505024 | bytes 5519872 | tf_op jit(solution)/shard_map/slcd,ld->slc/dot_general | solution.py:53
  155.4 0.0 copy-start.3
  155.4 0.0 copy-start.4
  155.4 10.8 %fusion.13 = bf16[8,2,64,768]{3,2,0,1:T(8,128)(2,1)} fusion(bf16[2,2688,768]{2,1,0:T(8,128)(2,1)} %param.13, bf16[8,2,64,2688]{3,2,1,0:T(8,128)(2,1)} %all-to-all-done, f32[2,768]{1,0:T(2,128)S(1)} %fusion.20, f32[8,2,64]{2,0,1:T(8,128)S(1)} %bitcast.70), kind=kOutput, calls=%fused_computation.18 | convolution fusion | flops 4231790592 | bytes 15345664 | tf_op jit(solution)/shard_map/slcd,ldh->slch/dot_general | solution.py:52
  166.3 0.0 all-gather.2.cloned.1.call-update
  166.3 0.0 copy-done.3
  166.3 0.2 fusion.15
  166.5 0.0 copy-done.4
  166.5 0.2 fusion.14
  166.7 43.6 %all-gather.2.cloned.1.call-done = bf16[8,2,64,1536]{3,2,0,1:T(8,128)(2,1)} async-done(((bf16[8,2,64,768]{3,2,0,1:T(8,128)(2,1)}), bf16[8,2,64,1536]{3,2,0,1:T(8,128)(2,1)}) %all-gather.2.cloned.1.call-update) | async-done | bytes 3145744 | tf_op jit(solution)/shard_map/all_gather | solution.py:56
  210.3 3.2 %fusion.26 = f32[2,1,8,64]{3,1,2,0:T(1,128)S(1)} fusion(bf16[8,2,64,1536]{3,2,0,1:T(8,128)(2,1)} %all-gather.2.cloned.1.call-done, bf16[2,1536,1,1]{1,0,2,3:T(2,128)(2,1)S(1)} %fusion.15), kind=kOutput, calls=%fused_computation.36 | convolution fusion | flops 3145728 | bytes 3155968 | tf_op jit(solution)/shard_map/slch,lh->slc/dot_general | solution.py:60
  213.5 9.2 %fusion.4 = bf16[8,2,64,1344]{3,2,0,1:T(8,128)(2,1)S(1)} fusion(bf16[8,2,64,1536]{3,2,0,1:T(8,128)(2,1)} %all-gather.2.cloned.1.call-done, bf16[2,1536,1344]{1,2,0:T(8,128)(2,1)} %param.14, f32[2,1344]{1,0:T(2,128)S(1)} %fusion.14, f32[8,2,64]{2,0,1:T(8,128)S(1)} %bitcast.69), kind=kOutput, calls=%fused_computation.8 | convolution fusion | flops 4231987200 | bytes 14170624 | tf_op jit(solution)/shard_map/slch,lhd->slcd/dot_general | solution.py:57
  222.7 0.0 copy-start.1
  222.7 1.8 copy.32
  224.5 4.6 %all-to-all-start.1 = ((bf16[8,2,64,1344]{3,2,1,0:T(8,128)(2,1)}), bf16[8,2,64,1344]{3,2,1,0:T(8,128)(2,1)S(1)}, u32[]{:S(2)}, u32[]{:S(2)}) async-start(bf16[8,2,64,1344]{3,2,1,0:T(8,128)(2,1)} %copy.32), calls=%async_computation.1 | async-start | bytes 5767168 | tf_op jit(solution)/shard_map/all_to_all | solution.py:66
  229.1 0.0 copy-done.1
  229.1 0.1 copy.33
  229.3 65.8 %all-to-all-done.1 = bf16[8,2,64,1344]{3,2,1,0:T(8,128)(2,1)S(1)} async-done(((bf16[8,2,64,1344]{3,2,1,0:T(8,128)(2,1)}), bf16[8,2,64,1344]{3,2,1,0:T(8,128)(2,1)S(1)}, u32[]{:S(2)}, u32[]{:S(2)}) %all-to-all-start.1) | async-done | bytes 2752544 | tf_op jit(solution)/shard_map/all_to_all | solution.py:66
  295.0 3.7 %gather_fusion.1 = bf16[768,1344]{1,0:T(8,128)(2,1)} fusion(bf16[1024,1344]{1,0:T(8,128)(2,1)S(1)} %bitcast.66, s32[1024]{0:T(1024)S(1)} %pad_clamp_fusion), kind=kCustom, calls=%fused_computation.1 | custom fusion | bytes 4131840 | tf_op jit(solution)/shard_map/gather | solution.py:68
  298.8 5.0 %reshape.72 = f32[128,6,1344]{2,1,0:T(8,128)} reshape(bf16[768,1344]{1,0:T(8,128)(2,1)} %gather_fusion.1) | data formatting | bytes 6193152 | tf_op jit(solution)/shard_map/convert_element_type | solution.py:70
  303.8 4.7 %multiply_reduce_fusion = bf16[128,1344]{1,0:T(8,128)(2,1)S(1)} fusion(f32[128,6,1344]{2,1,0:T(8,128)} %reshape.72, f32[128,6]{1,0:T(8,128)S(1)} %copy.33), kind=kLoop, calls=%fused_computation.9 | loop fusion | flops 1892352 | bytes 4475904 | tf_op jit(solution)/shard_map/reduce_sum | solution.py:71
  308.5 0.9 copy.34
  (8 shorter events, 0.1 us)
Async XLA Ops:
  6.5 22.1 %copy-start = (bf16[16,2688]{1,0:T(8,128)(2,1)S(1)}, bf16[16,2688]{1,0:T(8,128)(2,1)}, u32[]{:S(2)}) copy-start(bf16[16,2688]{1,0:T(8,128)(2,1)} %param.16) | copy-start | bytes 258052
  21.9 6.5 %copy-start.2 = (s32[2,4]{1,0:T(2,128)S(1)}, s32[2,4]{1,0:T(2,128)}, u32[]{:S(2)}) copy-start(s32[2,4]{1,0:T(2,128)} %param.15) | copy-start | bytes 100
  21.9 6.9 %copy-start.5 = (bf16[16,768]{1,0:T(8,128)(2,1)S(1)}, bf16[16,768]{1,0:T(8,128)(2,1)}, u32[]{:S(2)}) copy-start(bf16[16,768]{1,0:T(8,128)(2,1)} %param.17) | copy-start | bytes 73732
  21.9 128.7 %all-to-all-start = ((bf16[8,2,64,2688]{3,2,1,0:T(8,128)(2,1)}), bf16[8,2,64,2688]{3,2,1,0:T(8,128)(2,1)}, u32[]{:S(2)}, u32[]{:S(2)}) async-start(bf16[8,2,64,2688]{3,2,1,0:T(8,128)(2,1)} %bitcast.67), calls=%async_computation | async-start | bytes 11010048 | tf_op jit(solution)/shard_map/all_to_all | solution.py:51
  28.3 182.0 %all-gather.2.cloned.1.call-start = ((), (), s32[]{:S(2)}) async-start(), calls=%async_computation.2 | async-start | bytes 4718592 | tf_op jit(solution)/shard_map/all_gather | solution.py:56
  155.4 10.9 %copy-start.3 = (bf16[16,1536]{1,0:T(8,128)(2,1)S(1)}, bf16[16,1536]{1,0:T(8,128)(2,1)}, u32[]{:S(2)}) copy-start(bf16[16,1536]{1,0:T(8,128)(2,1)} %param.18) | copy-start | bytes 147460
  155.4 11.1 %copy-start.4 = (bf16[16,1344]{1,0:T(8,128)(2,1)S(1)}, bf16[16,1344]{1,0:T(8,128)(2,1)}, u32[]{:S(2)}) copy-start(bf16[16,1344]{1,0:T(8,128)(2,1)} %param.19) | copy-start | bytes 129028
  222.7 6.4 %copy-start.1 = (f32[128,6]{0,1:T(8,128)S(1)}, f32[128,6]{0,1:T(8,128)}, u32[]{:S(2)}) copy-start(f32[128,6]{0,1:T(8,128)} %param.12) | copy-start | bytes 9220
  224.5 70.5 %all-to-all-start.1 = ((bf16[8,2,64,1344]{3,2,1,0:T(8,128)(2,1)}), bf16[8,2,64,1344]{3,2,1,0:T(8,128)(2,1)S(1)}, u32[]{:S(2)}, u32[]{:S(2)}) async-start(bf16[8,2,64,1344]{3,2,1,0:T(8,128)(2,1)} %copy.32), calls=%async_computation.1 | async-start | bytes 5767168 | tf_op jit(solution)/shard_map/all_to_all | solution.py:66
Sparse Core Ops, SparseCore 0:
  166.4 43.8 all-gather.1
where the time goes:
time: 317 us; the launch traced here: 316 us
  waiting for transfers between devices  231 us (73%)
  matrix products  28.9 us (9%)
  local copies, waits for them, and re-layouts  24.5 us (8%)
  between operations  13.5 us (4%)
  starting transfers between devices  11.1 us (4%)
  other arithmetic  7.34 us (2%)
    all_to_all x1, waiting for transfers between devices, on_device(): lax.all_to_all(outgoing, ('ctx', 'tp'), split_axis=0, concat_axis=0, tile...  122 us
    all_to_all x1, waiting for transfers between devices, on_device(): lax.all_to_all(result, ('ctx', 'tp'), split_axis=0, concat_axis=0, tiled=...  65.8 us
    all_gather x1, waiting for transfers between devices, on_device(): full_hidden = lax.all_gather(hidden, 'exp', axis=3, tiled=True)  43.6 us
    dot_general x1, matrix products, on_device(): jnp.einsum('slcd,ldh->slch', buffer, up_weight, preferred_element_type=jn...  10.8 us
    dot_general x1, matrix products, on_device(): jnp.einsum('slch,lhd->slcd', full_hidden, down_weight, preferred_element_...  9.18 us
    gather x1, local copies, waits for them, and re-layouts, on_device(): token_rows = padded_tokens[source_row]  6.58 us
    all_to_all x1, starting transfers between devices, on_device(): lax.all_to_all(outgoing, ('ctx', 'tp'), split_axis=0, concat_axis=0, tile...  6.45 us
  transfers between devices with their start and end apart: 3, of which 3 were waited for; matrix products, arithmetic and copies ran while one was open for 0% of the time, Pallas kernels for 0%

commit v1 on v0

v1 whole, which is shorter than its diff:
```python
import functools

import jax
import jax.numpy as jnp
from jax import lax
from jax.experimental import pallas as pl
from jax.experimental.pallas import tpu as pltpu
from jax.sharding import PartitionSpec as P

LANES = 128
VMEM_LIMIT = 48 * 1024 * 1024


def shift(value, axis, by):
    size = lax.axis_size(axis)
    return lax.ppermute(value, axis, [(i, (i + by) % size) for i in range(size)])


def iota(shape, dim):
    return lax.broadcasted_iota(jnp.int32, shape, dim)


def prep_kernel(experts_all, parts, scalars, tokens, routes, gates, up_left, *refs):
    pieces, info = refs[:-1], refs[-1]
    count, model_width = tokens.shape
    width = info.shape[1]
    factors = up_left.shape[0]
    rows = count // parts
    lane = iota((count, width), 1)
    expert = lax.rem(lane, experts_all)
    gate_all = gates[...]
    normed = gate_all / jnp.sum(gate_all, axis=1, keepdims=True)
    named = jnp.zeros((count, width), jnp.float32)
    gate = jnp.zeros((count, width), jnp.float32)
    for k in range(routes.shape[1]):
        hit = routes[:, k : k + 1] == expert
        named = jnp.where(hit, 1.0, named)
        gate = jnp.where(hit, normed[:, k : k + 1], gate)
    before = (iota((count, count), 1) < iota((count, count), 0)).astype(jnp.bfloat16)
    slot = jnp.dot(before, named.astype(jnp.bfloat16), preferred_element_type=jnp.float32)
    slot = jnp.where(named > 0.0, slot, -1.0)
    row = iota((width, factors), 0) - 3 * experts_all
    pick = (row >= 0) & (row < 2 * factors) & (lax.rem(row, factors) == iota((width, factors), 1))
    left = jnp.dot(
        pick.astype(jnp.bfloat16), up_left[...], preferred_element_type=jnp.float32
    ).astype(jnp.bfloat16)
    low_rank = lax.dot_general(
        tokens[...], left, (((1,), (1,)), ((), ())), preferred_element_type=jnp.float32
    )
    value = jnp.where(lane < 3 * experts_all, gate, low_rank)
    high = value.astype(jnp.bfloat16).astype(jnp.float32)
    is_low = ((lane >= 2 * experts_all) & (lane < 3 * experts_all)) | (
        lane >= 3 * experts_all + factors
    )
    value = jnp.where(is_low, value - high, high)
    info[...] = jnp.where(lane < experts_all, slot, value).astype(jnp.bfloat16)
    for j, piece in enumerate(pieces):
        at = pl.multiple_of(lax.rem(scalars[0] - j + parts, parts) * rows, rows)
        piece[:, :model_width] = tokens[pl.ds(at, rows), :]
        piece[:, model_width:] = info[pl.ds(at, rows), :]


def up_kernel(
    experts_all, parts, cores, capacity, factors, scalars, *refs
):
    pieces = refs[: parts * cores]
    weight, right, hidden, gate_out, block, slots = refs[parts * cores :]
    rows = pieces[0].shape[0]
    tok_count = rows * parts
    model_width = weight.shape[1]
    width = block.shape[1] - model_width
    local_experts = slots.shape[0]
    slot_count = local_experts * capacity
    local = pl.program_id(0)

    @pl.when((local == 0) & (pl.program_id(1) == 0))
    def dispatch():
        column = iota((width, 2 * slot_count), 0)
        slot = iota((width, 2 * slot_count), 1)
        owner = scalars[1] + lax.rem(slot, slot_count) // capacity
        place_of = (column == owner).astype(jnp.bfloat16)
        gate_of = (
            column == owner + jnp.where(slot < slot_count, experts_all, 2 * experts_all)
        ).astype(jnp.bfloat16)
        wanted = lax.rem(iota((tok_count, 2 * slot_count), 1), capacity).astype(jnp.float32)
        for b in range(cores):
            for j in range(parts):
                block[j * rows : (j + 1) * rows, :] = pieces[b * parts + j][...]
            info = block[:, model_width:]
            place = jnp.dot(info, place_of, preferred_element_type=jnp.float32)
            gate = jnp.dot(info, gate_of, preferred_element_type=jnp.float32)
            here = place == wanted
            gate = jnp.where(here, gate, 0.0).astype(jnp.bfloat16)
            for j in range(parts):
                at = pl.multiple_of(lax.rem(scalars[0] - j + parts, parts) * rows, rows)
                gate_out[b, pl.ds(at, rows), :] = gate[j * rows : (j + 1) * rows, :]
            chooser = here[:, :slot_count].astype(jnp.bfloat16)
            chosen = lax.dot_general(
                chooser, block[...], (((0,), (0,)), ((), ())), preferred_element_type=jnp.float32
            ).astype(jnp.bfloat16)
            for l in range(local_experts):
                slots[l, b * capacity : (b + 1) * capacity, :] = chosen[
                    l * capacity : (l + 1) * capacity, :
                ]

    seed_left, seed_right = scalars[2 + 4 * local], scalars[3 + 4 * local]
    extra = slots[local, :, model_width:].astype(jnp.float32)
    lane = iota(extra.shape, 1) - 3 * experts_all
    low_rank = jnp.sum(
        jnp.where((lane == seed_left) | (lane == factors + seed_left), extra, 0.0),
        axis=1,
        keepdims=True,
    )
    table = right[...].astype(jnp.float32)
    right_row = jnp.sum(
        jnp.where(iota(table.shape, 0) == seed_right, table, 0.0), axis=0, keepdims=True
    )
    up_act = jnp.dot(
        slots[local, :, :model_width], weight[0], preferred_element_type=jnp.float32
    )
    up_act = jnp.maximum(up_act + low_rank * right_row, 0.0)
    hidden[0] = (up_act * up_act).astype(jnp.bfloat16)


def down_kernel(parts, cores, capacity, scalars, *refs):
    hiddens = refs[:parts]
    weight, left, right, gate, own, others, total, rank, results = refs[parts:]
    local, part = pl.program_id(0), pl.program_id(1)
    local_experts = pl.num_programs(0)
    slot_count = results.shape[1] // 2
    seed_left, seed_right = scalars[4 + 4 * local], scalars[5 + 4 * local]
    left_table = left[0].astype(jnp.float32)
    left_row = jnp.sum(
        jnp.where(iota(left_table.shape, 0) == seed_left, left_table, 0.0), axis=0, keepdims=True
    )
    for j in range(parts):

        @pl.when(part == j)
        def add(j=j):
            value = hiddens[j][0]
            product = jnp.dot(value, weight[0], preferred_element_type=jnp.float32)
            low_rank = jnp.sum(value.astype(jnp.float32) * left_row, axis=1, keepdims=True)
            if j:
                product = product + total[...]
                low_rank = low_rank + rank[:, :1]
            if j < parts - 1:
                total[...] = product
                rank[...] = jnp.broadcast_to(low_rank, rank.shape)
            else:
                table = right[...].astype(jnp.float32)
                right_row = jnp.sum(
                    jnp.where(iota(table.shape, 0) == seed_right, table, 0.0),
                    axis=0,
                    keepdims=True,
                )
                result = (product + low_rank * right_row).astype(jnp.bfloat16)
                for b in range(cores):
                    for half in range(2):
                        at = pl.multiple_of(half * slot_count + local * capacity, capacity)
                        results[b, pl.ds(at, capacity), :] = result[
                            b * capacity : (b + 1) * capacity, :
                        ]

    @pl.when((local == local_experts - 1) & (part == parts - 1))
    def combine():
        for b in range(cores):
            summed = jnp.dot(gate[b], results[b], preferred_element_type=jnp.float32)
            if b == 0:
                own[...] = summed
            else:
                others[b - 1] = summed.astype(jnp.bfloat16)


def on_device(
    tokens,
    routes,
    route_gates,
    up_weight,
    down_weight,
    factor_seeds,
    up_left,
    up_right,
    down_left,
    down_right,
):
    chips, cores, parts = lax.axis_size("ctx"), lax.axis_size("tp"), lax.axis_size("exp")
    local_experts, model_width, hid = up_weight.shape
    out_width = down_weight.shape[2]
    experts_all = chips * cores * local_experts
    tok_count, top_count = routes.shape
    factors = up_left.shape[0]
    capacity = 4 * tok_count * top_count // (3 * experts_all)
    rows = tok_count // parts
    width = -(-(3 * experts_all + 2 * factors) // LANES) * LANES
    packed = model_width + width
    slot_count = local_experts * capacity
    expert_rows = cores * capacity
    first_expert = (lax.axis_index("ctx") * cores + lax.axis_index("tp")) * local_experts
    scalars = jnp.concatenate(
        [
            jnp.stack([lax.axis_index("exp"), first_expert]).astype(jnp.int32),
            factor_seeds.reshape(-1),
        ]
    )
    left_parts = down_left.reshape(factors, parts, hid).transpose(1, 0, 2)
    params = pltpu.CompilerParams(vmem_limit_bytes=VMEM_LIMIT)

    prep = pl.pallas_call(
        functools.partial(prep_kernel, experts_all, parts),
        out_shape=[jax.ShapeDtypeStruct((rows, packed), jnp.bfloat16)] * parts,
        grid_spec=pltpu.PrefetchScalarGridSpec(
            num_scalar_prefetch=1,
            grid=(1,),
            in_specs=[
                pl.BlockSpec(shape, lambda i, s: (0, 0))
                for shape in (tokens.shape, routes.shape, routes.shape, up_left.shape)
            ],
            out_specs=[pl.BlockSpec((rows, packed), lambda i, s: (0, 0))] * parts,
            scratch_shapes=[pltpu.VMEM((tok_count, width), jnp.bfloat16)],
        ),
        compiler_params=params,
        name="pack_tokens",
    )

    up_tile = 2 * LANES if hid % (2 * LANES) == 0 else hid
    up = pl.pallas_call(
        functools.partial(up_kernel, experts_all, parts, cores, capacity, factors),
        out_shape=[
            jax.ShapeDtypeStruct((local_experts, expert_rows, hid), jnp.bfloat16),
            jax.ShapeDtypeStruct((cores, tok_count, 2 * slot_count), jnp.bfloat16),
        ],
        grid_spec=pltpu.PrefetchScalarGridSpec(
            num_scalar_prefetch=1,
            grid=(local_experts, hid // up_tile),
            in_specs=[pl.BlockSpec((rows, packed), lambda l, n, s: (0, 0))] * (parts * cores)
            + [
                pl.BlockSpec((1, model_width, up_tile), lambda l, n, s: (l, 0, n)),
                pl.BlockSpec((factors, up_tile), lambda l, n, s: (0, n)),
            ],
            out_specs=[
                pl.BlockSpec((1, expert_rows, up_tile), lambda l, n, s: (l, 0, n)),
                pl.BlockSpec((cores, tok_count, 2 * slot_count), lambda l, n, s: (0, 0, 0)),
            ],
            scratch_shapes=[
                pltpu.VMEM((tok_count, packed), jnp.bfloat16),
                pltpu.VMEM((local_experts, expert_rows, packed), jnp.bfloat16),
            ],
        ),
        compiler_params=params,
        cost_estimate=pl.CostEstimate(
            flops=2 * slot_count * cores * model_width * hid,
            bytes_accessed=2 * up_weight.size,
            transcendentals=0,
        ),
        name="up",
    )

    def turned(j, s):
        return lax.rem(s[0] - j + parts, parts)

    down = pl.pallas_call(
        functools.partial(down_kernel, parts, cores, capacity),
        out_shape=[
            jax.ShapeDtypeStruct((tok_count, out_width), jnp.float32),
            jax.ShapeDtypeStruct((cores - 1, tok_count, out_width), jnp.bfloat16),
        ],
        grid_spec=pltpu.PrefetchScalarGridSpec(
            num_scalar_prefetch=1,
            grid=(local_experts, parts),
            in_specs=[pl.BlockSpec((1, expert_rows, hid), lambda l, j, s: (l, 0, 0))] * parts
            + [
                pl.BlockSpec((1, hid, out_width), lambda l, j, s: (l, turned(j, s), 0)),
                pl.BlockSpec((1, factors, hid), lambda l, j, s: (turned(j, s), 0, 0)),
                pl.BlockSpec((factors, out_width), lambda l, j, s: (0, 0)),
                pl.BlockSpec((cores, tok_count, 2 * slot_count), lambda l, j, s: (0, 0, 0)),
            ],
            out_specs=[
                pl.BlockSpec((tok_count, out_width), lambda l, j, s: (0, 0)),
                pl.BlockSpec((cores - 1, tok_count, out_width), lambda l, j, s: (0, 0, 0)),
            ],
            scratch_shapes=[
                pltpu.VMEM((expert_rows, out_width), jnp.float32),
                pltpu.VMEM((expert_rows, LANES), jnp.float32),
                pltpu.VMEM((cores, 2 * slot_count, out_width), jnp.bfloat16),
            ],
        ),
        compiler_params=params,
        cost_estimate=pl.CostEstimate(
            flops=2 * slot_count * cores * parts * hid * out_width,
            bytes_accessed=2 * down_weight.size,
            transcendentals=0,
        ),
        name="down",
    )

    own_pieces = list(prep(scalars, tokens, routes, route_gates, up_left))

    def compute(pieces):
        blocks = list(pieces)
        for b in range(1, cores):
            blocks += [shift(piece, "tp", b) for piece in pieces]
        hidden, gate = up(scalars, *blocks, up_weight, up_right)
        hiddens = [hidden] + [shift(hidden, "exp", j) for j in range(1, parts)]
        own, others = down(scalars, *hiddens, down_weight, left_parts, down_right, gate)
        return own, [shift(others[b - 1], "tp", -b) for b in range(1, cores)]

    sums = [compute(own_pieces)]
    travelling = own_pieces[0]
    for _ in range(1, chips):
        travelling = shift(travelling, "ctx", 1)
        pieces = [travelling] + [shift(travelling, "exp", j) for j in range(1, parts)]
        sums.append(compute(pieces))
    carried = None
    for own, swapped in sums[1:] + sums[:1]:
        total = own
        for value in swapped + ([carried] if carried is not None else []):
            total = total + value.astype(jnp.float32)
        total = total.astype(jnp.bfloat16)
        if own is not sums[0][0]:
            carried = shift(total, "ctx", 1)
    return total


def solution(mesh):
    in_specs = (
        P(("pop", "ctx", "tp"), None),
        P(("pop", "ctx", "tp"), None),
        P(("pop", "ctx", "tp"), None),
        P(("ctx", "tp"), None, "exp"),
        P(("ctx", "tp"), None, "exp"),
        P(("pop", "ctx", "tp"), None),
        P(),
        P(None, "exp"),
        P(),
        P(None, "exp"),
    )
    out_specs = P(("pop", "ctx", "tp"), "exp")
    return jax.shard_map(
        on_device, mesh=mesh, in_specs=in_specs, out_specs=out_specs, check_vma=False
    )
```

time: 317 us -> 158 us (0.50)
  waiting for transfers between devices: 231 us -> 67.2 us
  Pallas kernels: 0 us -> 55.5 us
  matrix products: 28.9 us -> 0 us
  between operations: 13.5 us -> 0.19 us
  local copies, waits for them, and re-layouts: 24.5 us -> 17.5 us
  other arithmetic: 7.34 us -> 0.51 us
  starting transfers between devices: 11.1 us -> 15.9 us
    all_to_all x2 -> x0, waiting for transfers between devices: 187 us -> none  [the longest x1 122 us: on_device(): lax.all_to_all(outgoing, ('ctx', 'tp'), split_axis=0, concat_axis=0, tile...]
    ppermute x0 -> x25, waiting for transfers between devices: none -> 67.2 us  [shift(): lax.ppermute(value, axis, [(i, (i + by) % size) for i in range(size)])]
    pallas_call x0 -> x9, Pallas kernels: none -> 55.5 us  [the longest x4 29.3 us: compute(): hidden, gate = up(scalars, *blocks, up_weight, up_right)]
    all_gather x1 -> x0, waiting for transfers between devices: 43.6 us -> none  [on_device(): full_hidden = lax.all_gather(hidden, 'exp', axis=3, tiled=True)]
    dot_general x8 -> x0, matrix products: 28.9 us -> none  [the longest x1 10.8 us: on_device(): jnp.einsum('slcd,ldh->slch', buffer, up_weight, preferred_element_type=jn...]
    ppermute x0 -> x25, starting transfers between devices: none -> 15.9 us  [shift(): lax.ppermute(value, axis, [(i, (i + by) % size) for i in range(size)])]
    unnamed x13 -> x15, local copies, waits for them, and re-layouts: 0.85 us -> 15.8 us
    all_to_all x2 -> x0, starting transfers between devices: 11.1 us -> none  [the longest x1 6.45 us: on_device(): lax.all_to_all(outgoing, ('ctx', 'tp'), split_axis=0, concat_axis=0, tile...]
  transfers between devices with their start and end apart: 3 -> 25, of which waited for: 3 -> 8; matrix products, arithmetic and copies ran while one was open for 0% -> 8% of each run, Pallas kernels for 0% -> 34%
where the time goes in v1:
time: 158 us; the launch traced here: 157 us
  waiting for transfers between devices  67.2 us (43%)
  Pallas kernels  55.5 us (35%)
  local copies, waits for them, and re-layouts  17.5 us (11%)
  starting transfers between devices  15.9 us (10%)
    ppermute x25, waiting for transfers between devices, shift(): lax.ppermute(value, axis, [(i, (i + by) % size) for i in range(size)])  67.2 us
    pallas_call x4, Pallas kernels, compute(): hidden, gate = up(scalars, *blocks, up_weight, up_right)  29.3 us
    pallas_call x4, Pallas kernels, compute(): down(scalars, *hiddens, down_weight, left_parts, down_right, gate)  24.8 us
    ppermute x25, starting transfers between devices, shift(): lax.ppermute(value, axis, [(i, (i + by) % size) for i in range(size)])  15.9 us
    unnamed x15, local copies, waits for them, and re-layouts  15.8 us
  transfers between devices with their start and end apart: 25, of which 8 were waited for; matrix products, arithmetic and copies ran while one was open for 8% of the time, Pallas kernels for 34%

profile of v1, /device:TPU:0, one launch (start us, length us, event | category | flops | bytes accessed | tf_op | source)
XLA Modules:
  0.0 156.7 jit_solution(13993661166401827565)
XLA Ops:
  0.0 0.8 reshape.6
  0.8 0.8 copy.18.routes
  1.6 0.8 copy.19.gates
  2.3 0.1 pad_add_fusion.scalars
  2.4 1.1 copy-done.1
  3.5 0.9 copy-done.4
  4.4 1.4 pack_tokens.1
  5.8 3.1 %collective-permute-start.4 = (bf16[64,2816]{1,0:T(8,128)(2,1)S(1)}, bf16[64,2816]{1,0:T(8,128)(2,1)S(1)}, u32[]{:S(2)}, u32[]{:S(2)}) collective-permute-start(bf16[64,2816]{1,0:T(8,128)(2,1)S(1)} %get-tuple-element.23.refs_0_), channel_id=1, source_target_pairs={{0,4},{4,8},{8,12},{12,0},{1,5},{5,9},{9,13},{13,1},{2,6},{6,10},{... | collective-permute-start | bytes 1081352 | tf_op jit(solution)/shard_map/ppermute | solution.py:16
  8.9 10.4 %collective-permute-done.4.refs_0_ = bf16[64,2816]{1,0:T(8,128)(2,1)S(1)} collective-permute-done((bf16[64,2816]{1,0:T(8,128)(2,1)S(1)}, bf16[64,2816]{1,0:T(8,128)(2,1)S(1)}, u32[]{:S(2)}, u32[]{:S(2)}) %collective-permute-start.4) | collective-permute-done | bytes 360480 | tf_op jit(solution)/shard_map/ppermute | solution.py:16
  19.3 1.5 collective-permute-start.17
  20.8 0.0 collective-permute-start.18
  20.8 8.1 %collective-permute-done.17.refs_1_ = bf16[64,2816]{1,0:T(8,128)(2,1)S(1)} collective-permute-done((bf16[64,2816]{1,0:T(8,128)(2,1)S(1)}, bf16[64,2816]{1,0:T(8,128)(2,1)S(1)}, u32[]{:S(2)}, u32[]{:S(2)}) %collective-permute-start.17) | collective-permute-done | bytes 360480 | tf_op jit(solution)/shard_map/ppermute | solution.py:16
  28.9 0.0 collective-permute-start.19
  28.9 0.0 collective-permute-start.5
  28.9 0.0 collective-permute-done.18.refs_2_
  28.9 1.7 %collective-permute-done.19.refs_3_ = bf16[64,2816]{1,0:T(8,128)(2,1)S(1)} collective-permute-done((bf16[64,2816]{1,0:T(8,128)(2,1)S(1)}, bf16[64,2816]{1,0:T(8,128)(2,1)S(1)}, u32[]{:S(2)}, u32[]{:S(2)}) %collective-permute-start.19) | collective-permute-done | bytes 360480 | tf_op jit(solution)/shard_map/ppermute | solution.py:16
  30.6 0.7 copy-done.2
  31.3 7.3 %up.7 = (bf16[2,128,768]{2,1,0:T(8,128)(2,1)S(1)}, bf16[2,128,256]{2,1,0:T(8,128)(2,1)S(1)}) custom-call(s32[10]{0:T(128)S(1)} %pad_add_fusion.scalars, bf16[64,2816]{1,0:T(8,128)(2,1)S(1)} %collective-permute-done.4.refs_0_, bf16[64,2816]{1,0:T(8,128)(2,1)S(1)} %collective-permute-done.17.refs_1_, bf16[64,2816]{1,0:T(8,128)(2,1)S(1)} %collective-permute-done.18.refs_2_, ...), custom_call_target="tpu_custom_call" | custom-call | flops 1056964608 | bytes 8257536 | tf_op jit(solution)/shard_map/up/pallas_call | solution.py:302
  38.7 0.0 copy-start.5
  38.7 0.0 copy-start
  38.7 1.3 collective-permute-start.20
  40.0 1.6 collective-permute-done.5.refs_0_
  41.6 1.2 collective-permute-start.12
  42.8 0.0 collective-permute-start.6
  42.8 0.0 collective-permute-start.13
  42.8 14.8 %collective-permute-done.12.refs_1_ = bf16[64,2816]{1,0:T(8,128)(2,1)S(1)} collective-permute-done((bf16[64,2816]{1,0:T(8,128)(2,1)S(1)}, bf16[64,2816]{1,0:T(8,128)(2,1)S(1)}, u32[]{:S(2)}, u32[]{:S(2)}) %collective-permute-start.12) | collective-permute-done | bytes 360480 | tf_op jit(solution)/shard_map/ppermute | solution.py:16
  57.6 0.0 collective-permute-start.14
  57.6 11.5 %copy.21.refs_2_ = bf16[2,1536,1344]{2,1,0:T(8,128)(2,1)} copy(bf16[2,1536,1344]{1,2,0:T(8,128)(2,1)} %param.14) | data formatting | bytes 16515072 | tf_op args[4]
  69.1 0.0 collective-permute-done.6.refs_0_
  69.1 1.3 collective-permute-start.7
  70.4 0.0 collective-permute-done.20.refs_1_
  70.5 6.2 %down.7 = (f32[128,1344]{1,0:T(8,128)S(1)}, bf16[1,128,1344]{2,1,0:T(8,128)(2,1)S(1)}) custom-call(s32[10]{0:T(128)S(1)} %pad_add_fusion.scalars, bf16[2,128,768]{2,1,0:T(8,128)(2,1)S(1)} %get-tuple-element.37.refs_0_, bf16[2,128,768]{2,1,0:T(8,128)(2,1)S(1)} %collective-permute-done.20.refs_1_, bf16[2,1536,1344]{2,1,0:T(8,128)(2,1)} %copy.21.refs_2_, ...), custom_call_target="tpu_custom_call" | custom-call | flops 1056964608 | bytes 8257536 | tf_op jit(solution)/shard_map/down/pallas_call | solution.py:304
  76.6 0.3 collective-permute-start.21
  76.9 0.3 collective-permute-start
  77.2 0.0 collective-permute-done.13.refs_2_
  77.2 0.2 collective-permute-start.1
  77.5 0.0 collective-permute-done.14.refs_3_
  77.5 0.3 collective-permute-start.8
  77.7 7.3 %up.6 = (bf16[2,128,768]{2,1,0:T(8,128)(2,1)S(1)}, bf16[2,128,256]{2,1,0:T(8,128)(2,1)S(1)}) custom-call(s32[10]{0:T(128)S(1)} %pad_add_fusion.scalars, bf16[64,2816]{1,0:T(8,128)(2,1)S(1)} %collective-permute-done.5.refs_0_, bf16[64,2816]{1,0:T(8,128)(2,1)S(1)} %collective-permute-done.12.refs_1_, bf16[64,2816]{1,0:T(8,128)(2,1)S(1)} %collective-permute-done.13.refs_2_, ...), custom_call_target="tpu_custom_call" | custom-call | flops 1056964608 | bytes 8257536 | tf_op jit(solution)/shard_map/up/pallas_call | solution.py:302
  85.1 0.0 collective-permute-done.7.refs_1_
  85.1 0.8 collective-permute-start.15
  85.9 0.0 collective-permute-done.21
  85.9 0.0 collective-permute-start.9
  85.9 0.1 add_convert_fusion.3
  86.0 10.4 %collective-permute-done.15.refs_1_ = bf16[2,128,768]{2,1,0:T(8,128)(2,1)S(1)} collective-permute-done((bf16[2,128,768]{2,1,0:T(8,128)(2,1)S(1)}, bf16[2,128,768]{2,1,0:T(8,128)(2,1)S(1)}, u32[]{:S(2)}, u32[]{:S(2)}) %collective-permute-start.15) | collective-permute-done | bytes 393248 | tf_op jit(solution)/shard_map/ppermute | solution.py:16
  96.4 6.2 %down.6 = (f32[128,1344]{1,0:T(8,128)S(1)}, bf16[1,128,1344]{2,1,0:T(8,128)(2,1)S(1)}) custom-call(s32[10]{0:T(128)S(1)} %pad_add_fusion.scalars, bf16[2,128,768]{2,1,0:T(8,128)(2,1)S(1)} %get-tuple-element.33.refs_0_, bf16[2,128,768]{2,1,0:T(8,128)(2,1)S(1)} %collective-permute-done.15.refs_1_, bf16[2,1536,1344]{2,1,0:T(8,128)(2,1)} %copy.21.refs_2_, ...), custom_call_target="tpu_custom_call" | custom-call | flops 1056964608 | bytes 8257536 | tf_op jit(solution)/shard_map/down/pallas_call | solution.py:304
  102.6 0.0 collective-permute-done.refs_2_
  102.6 0.1 collective-permute-start.16
  102.7 7.3 %up.4 = (bf16[2,128,768]{2,1,0:T(8,128)(2,1)S(1)}, bf16[2,128,256]{2,1,0:T(8,128)(2,1)S(1)}) custom-call(s32[10]{0:T(128)S(1)} %pad_add_fusion.scalars, bf16[64,2816]{1,0:T(8,128)(2,1)S(1)} %get-tuple-element.23.refs_0_, bf16[64,2816]{1,0:T(8,128)(2,1)S(1)} %get-tuple-element.24.refs_1_, bf16[64,2816]{1,0:T(8,128)(2,1)S(1)} %collective-permute-done.refs_2_, ...), custom_call_target="tpu_custom_call" | custom-call | flops 1056964608 | bytes 8257536 | tf_op jit(solution)/shard_map/up/pallas_call | solution.py:302
  110.0 0.8 collective-permute-start.2
  110.9 7.3 %up.5 = (bf16[2,128,768]{2,1,0:T(8,128)(2,1)S(1)}, bf16[2,128,256]{2,1,0:T(8,128)(2,1)S(1)}) custom-call(s32[10]{0:T(128)S(1)} %pad_add_fusion.scalars, bf16[64,2816]{1,0:T(8,128)(2,1)S(1)} %collective-permute-done.6.refs_0_, bf16[64,2816]{1,0:T(8,128)(2,1)S(1)} %collective-permute-done.7.refs_1_, bf16[64,2816]{1,0:T(8,128)(2,1)S(1)} %collective-permute-done.8.refs_2_, ...), custom_call_target="tpu_custom_call" | custom-call | flops 1056964608 | bytes 8257536 | tf_op jit(solution)/shard_map/up/pallas_call | solution.py:302
  118.2 1.3 collective-permute-start.10
  119.5 0.1 add_convert_fusion.2
  119.6 1.4 collective-permute-start.23
  121.1 8.9 %collective-permute-done.10.refs_1_ = bf16[2,128,768]{2,1,0:T(8,128)(2,1)S(1)} collective-permute-done((bf16[2,128,768]{2,1,0:T(8,128)(2,1)S(1)}, bf16[2,128,768]{2,1,0:T(8,128)(2,1)S(1)}, u32[]{:S(2)}, u32[]{:S(2)}) %collective-permute-start.10) | collective-permute-done | bytes 393248 | tf_op jit(solution)/shard_map/ppermute | solution.py:16
  130.0 6.2 %down.5 = (f32[128,1344]{1,0:T(8,128)S(1)}, bf16[1,128,1344]{2,1,0:T(8,128)(2,1)S(1)}) custom-call(s32[10]{0:T(128)S(1)} %pad_add_fusion.scalars, bf16[2,128,768]{2,1,0:T(8,128)(2,1)S(1)} %get-tuple-element.29.refs_0_, bf16[2,128,768]{2,1,0:T(8,128)(2,1)S(1)} %collective-permute-done.10.refs_1_, bf16[2,1536,1344]{2,1,0:T(8,128)(2,1)} %copy.21.refs_2_, ...), custom_call_target="tpu_custom_call" | custom-call | flops 1056964608 | bytes 8257536 | tf_op jit(solution)/shard_map/down/pallas_call | solution.py:304
  136.2 0.1 collective-permute-start.11
  136.3 6.2 %down.4 = (f32[128,1344]{1,0:T(8,128)S(1)}, bf16[1,128,1344]{2,1,0:T(8,128)(2,1)S(1)}) custom-call(s32[10]{0:T(128)S(1)} %pad_add_fusion.scalars, bf16[2,128,768]{2,1,0:T(8,128)(2,1)S(1)} %get-tuple-element.25.refs_0_, bf16[2,128,768]{2,1,0:T(8,128)(2,1)S(1)} %collective-permute-done.2.refs_1_, bf16[2,1536,1344]{2,1,0:T(8,128)(2,1)} %copy.21.refs_2_, ...), custom_call_target="tpu_custom_call" | custom-call | flops 1056964608 | bytes 8257536 | tf_op jit(solution)/shard_map/down/pallas_call | solution.py:304
  142.5 0.6 collective-permute-start.3
  143.1 0.1 add_convert_fusion.1
  143.2 1.3 collective-permute-start.24
  144.5 11.2 %collective-permute-done.24 = bf16[128,1344]{1,0:T(8,128)(2,1)S(1)} collective-permute-done((bf16[128,1344]{1,0:T(8,128)(2,1)S(1)}, bf16[128,1344]{1,0:T(8,128)(2,1)S(1)}, u32[]{:S(2)}, u32[]{:S(2)}) %collective-permute-start.24) | collective-permute-done | bytes 344096 | tf_op jit(solution)/shard_map/ppermute | solution.py:16
  155.7 0.1 add_convert_fusion
  155.8 0.9 copy.25
  (18 shorter events, 0.0 us)
Async XLA Ops:
  2.4 1.1 copy-start.1
  3.5 0.9 copy-start.4
  5.8 13.5 %collective-permute-start.4 = (bf16[64,2816]{1,0:T(8,128)(2,1)S(1)}, bf16[64,2816]{1,0:T(8,128)(2,1)S(1)}, u32[]{:S(2)}, u32[]{:S(2)}) collective-permute-start(bf16[64,2816]{1,0:T(8,128)(2,1)S(1)} %get-tuple-element.23.refs_0_), channel_id=1, source_target_pairs={{0,4},{4,8},{8,12},{12,0},{1,5},{5,9},{9,13},{13,1},{2,6},{6,10},{... | collective-permute-start | bytes 1081352 | tf_op jit(solution)/shard_map/ppermute | solution.py:16
  19.3 9.6 %collective-permute-start.17 = (bf16[64,2816]{1,0:T(8,128)(2,1)S(1)}, bf16[64,2816]{1,0:T(8,128)(2,1)S(1)}, u32[]{:S(2)}, u32[]{:S(2)}) collective-permute-start(bf16[64,2816]{1,0:T(8,128)(2,1)S(1)} %collective-permute-done.4.refs_0_), channel_id=1, source_target_pairs={{0,2},{2,0},{1,3},{3,1},{4,6},{6,4},{5,7},{7,5},{8,10},{10,8},{9,1... | collective-permute-start | bytes 1081352 | tf_op jit(solution)/shard_map/ppermute | solution.py:16
  20.8 8.1 %collective-permute-start.18 = (bf16[64,2816]{1,0:T(8,128)(2,1)S(1)}, bf16[64,2816]{1,0:T(8,128)(2,1)S(1)}, u32[]{:S(2)}, u32[]{:S(2)}) collective-permute-start(bf16[64,2816]{1,0:T(8,128)(2,1)S(1)} %collective-permute-done.4.refs_0_), channel_id=1, source_target_pairs={{0,1},{1,0},{2,3},{3,2},{4,5},{5,4},{6,7},{7,6},{8,9},{9,8},{10,11... | collective-permute-start | bytes 1081352 | tf_op jit(solution)/shard_map/ppermute | solution.py:16
  28.9 1.7 %collective-permute-start.19 = (bf16[64,2816]{1,0:T(8,128)(2,1)S(1)}, bf16[64,2816]{1,0:T(8,128)(2,1)S(1)}, u32[]{:S(2)}, u32[]{:S(2)}) collective-permute-start(bf16[64,2816]{1,0:T(8,128)(2,1)S(1)} %collective-permute-done.17.refs_1_), channel_id=1, source_target_pairs={{0,1},{1,0},{2,3},{3,2},{4,5},{5,4},{6,7},{7,6},{8,9},{9,8},{10,11... | collective-permute-start | bytes 1081352 | tf_op jit(solution)/shard_map/ppermute | solution.py:16
  28.9 12.6 %collective-permute-start.5 = (bf16[64,2816]{1,0:T(8,128)(2,1)S(1)}, bf16[64,2816]{1,0:T(8,128)(2,1)S(1)}, u32[]{:S(2)}, u32[]{:S(2)}) collective-permute-start(bf16[64,2816]{1,0:T(8,128)(2,1)S(1)} %collective-permute-done.4.refs_0_), channel_id=1, source_target_pairs={{0,4},{4,8},{8,12},{12,0},{1,5},{5,9},{9,13},{13,1},{2,6},{6,10},{... | collective-permute-start | bytes 1081352 | tf_op jit(solution)/shard_map/ppermute | solution.py:16
  30.6 0.7 copy-start.2
  38.7 30.4 %copy-start.5 = (bf16[16,1536]{1,0:T(8,128)(2,1)S(1)}, bf16[16,1536]{1,0:T(8,128)(2,1)}, u32[]{:S(2)}) copy-start(bf16[16,1536]{1,0:T(8,128)(2,1)} %param.18) | copy-start | bytes 147460
  38.7 31.8 %copy-start = (bf16[16,1344]{1,0:T(8,128)(2,1)S(1)}, bf16[16,1344]{1,0:T(8,128)(2,1)}, u32[]{:S(2)}) copy-start(bf16[16,1344]{1,0:T(8,128)(2,1)} %refs_4_.15) | copy-start | bytes 129028
  38.7 31.8 %collective-permute-start.20 = (bf16[2,128,768]{2,1,0:T(8,128)(2,1)S(1)}, bf16[2,128,768]{2,1,0:T(8,128)(2,1)S(1)}, u32[]{:S(2)}, u32[]{:S(2)}) collective-permute-start(bf16[2,128,768]{2,1,0:T(8,128)(2,1)S(1)} %get-tuple-element.37.refs_0_), channel_id=1, source_target_pairs={{0,2},{2,0},{1,3},{3,1},{4,6},{6,4},{5,7},{7,5},{8,10},{10,8},{9,1... | collective-permute-start | bytes 1179656 | tf_op jit(solution)/shard_map/ppermute | solution.py:16
  41.6 16.1 %collective-permute-start.12 = (bf16[64,2816]{1,0:T(8,128)(2,1)S(1)}, bf16[64,2816]{1,0:T(8,128)(2,1)S(1)}, u32[]{:S(2)}, u32[]{:S(2)}) collective-permute-start(bf16[64,2816]{1,0:T(8,128)(2,1)S(1)} %collective-permute-done.5.refs_0_), channel_id=1, source_target_pairs={{0,2},{2,0},{1,3},{3,1},{4,6},{6,4},{5,7},{7,5},{8,10},{10,8},{9,1... | collective-permute-start | bytes 1081352 | tf_op jit(solution)/shard_map/ppermute | solution.py:16
  42.8 26.3 %collective-permute-start.6 = (bf16[64,2816]{1,0:T(8,128)(2,1)S(1)}, bf16[64,2816]{1,0:T(8,128)(2,1)S(1)}, u32[]{:S(2)}, u32[]{:S(2)}) collective-permute-start(bf16[64,2816]{1,0:T(8,128)(2,1)S(1)} %collective-permute-done.5.refs_0_), channel_id=1, source_target_pairs={{0,4},{4,8},{8,12},{12,0},{1,5},{5,9},{9,13},{13,1},{2,6},{6,10},{... | collective-permute-start | bytes 1081352 | tf_op jit(solution)/shard_map/ppermute | solution.py:16
  42.8 34.4 %collective-permute-start.13 = (bf16[64,2816]{1,0:T(8,128)(2,1)S(1)}, bf16[64,2816]{1,0:T(8,128)(2,1)S(1)}, u32[]{:S(2)}, u32[]{:S(2)}) collective-permute-start(bf16[64,2816]{1,0:T(8,128)(2,1)S(1)} %collective-permute-done.5.refs_0_), channel_id=1, source_target_pairs={{0,1},{1,0},{2,3},{3,2},{4,5},{5,4},{6,7},{7,6},{8,9},{9,8},{10,11... | collective-permute-start | bytes 1081352 | tf_op jit(solution)/shard_map/ppermute | solution.py:16
  57.6 19.8 %collective-permute-start.14 = (bf16[64,2816]{1,0:T(8,128)(2,1)S(1)}, bf16[64,2816]{1,0:T(8,128)(2,1)S(1)}, u32[]{:S(2)}, u32[]{:S(2)}) collective-permute-start(bf16[64,2816]{1,0:T(8,128)(2,1)S(1)} %collective-permute-done.12.refs_1_), channel_id=1, source_target_pairs={{0,1},{1,0},{2,3},{3,2},{4,5},{5,4},{6,7},{7,6},{8,9},{9,8},{10,11... | collective-permute-start | bytes 1081352 | tf_op jit(solution)/shard_map/ppermute | solution.py:16
  69.1 8.6 %copy-start.3 = (bf16[16,768]{1,0:T(8,128)(2,1)S(1)}, bf16[16,768]{1,0:T(8,128)(2,1)}, u32[]{:S(2)}) copy-start(bf16[16,768]{1,0:T(8,128)(2,1)} %refs_5_.7) | copy-start | bytes 73732
  69.1 15.9 %collective-permute-start.7 = (bf16[64,2816]{1,0:T(8,128)(2,1)S(1)}, bf16[64,2816]{1,0:T(8,128)(2,1)S(1)}, u32[]{:S(2)}, u32[]{:S(2)}) collective-permute-start(bf16[64,2816]{1,0:T(8,128)(2,1)S(1)} %collective-permute-done.6.refs_0_), channel_id=1, source_target_pairs={{0,2},{2,0},{1,3},{3,1},{4,6},{6,4},{5,7},{7,5},{8,10},{10,8},{9,1... | collective-permute-start | bytes 1081352 | tf_op jit(solution)/shard_map/ppermute | solution.py:16
  76.6 9.3 %collective-permute-start.21 = (bf16[128,1344]{1,0:T(8,128)(2,1)S(1)}, bf16[128,1344]{1,0:T(8,128)(2,1)S(1)}, u32[]{:S(2)}, u32[]{:S(2)}) collective-permute-start(bf16[128,1344]{1,0:T(8,128)(2,1)S(1)} %bitcast.18), channel_id=1, source_target_pairs={{0,1},{1,0},{2,3},{3,2},{4,5},{5,4},{6,7},{7,6},{8,9},{9,8},{10,11... | collective-permute-start | bytes 1032200 | tf_op jit(solution)/shard_map/ppermute | solution.py:16
  76.9 25.7 %collective-permute-start = (bf16[64,2816]{1,0:T(8,128)(2,1)S(1)}, bf16[64,2816]{1,0:T(8,128)(2,1)S(1)}, u32[]{:S(2)}, u32[]{:S(2)}) collective-permute-start(bf16[64,2816]{1,0:T(8,128)(2,1)S(1)} %get-tuple-element.23.refs_0_), channel_id=1, source_target_pairs={{0,1},{1,0},{2,3},{3,2},{4,5},{5,4},{6,7},{7,6},{8,9},{9,8},{10,11... | collective-permute-start | bytes 1081352 | tf_op jit(solution)/shard_map/ppermute | solution.py:16
  77.2 25.5 %collective-permute-start.1 = (bf16[64,2816]{1,0:T(8,128)(2,1)S(1)}, bf16[64,2816]{1,0:T(8,128)(2,1)S(1)}, u32[]{:S(2)}, u32[]{:S(2)}) collective-permute-start(bf16[64,2816]{1,0:T(8,128)(2,1)S(1)} %get-tuple-element.24.refs_1_), channel_id=1, source_target_pairs={{0,1},{1,0},{2,3},{3,2},{4,5},{5,4},{6,7},{7,6},{8,9},{9,8},{10,11... | collective-permute-start | bytes 1081352 | tf_op jit(solution)/shard_map/ppermute | solution.py:16
  77.5 33.4 %collective-permute-start.8 = (bf16[64,2816]{1,0:T(8,128)(2,1)S(1)}, bf16[64,2816]{1,0:T(8,128)(2,1)S(1)}, u32[]{:S(2)}, u32[]{:S(2)}) collective-permute-start(bf16[64,2816]{1,0:T(8,128)(2,1)S(1)} %collective-permute-done.6.refs_0_), channel_id=1, source_target_pairs={{0,1},{1,0},{2,3},{3,2},{4,5},{5,4},{6,7},{7,6},{8,9},{9,8},{10,11... | collective-permute-start | bytes 1081352 | tf_op jit(solution)/shard_map/ppermute | solution.py:16
  85.1 11.3 %collective-permute-start.15 = (bf16[2,128,768]{2,1,0:T(8,128)(2,1)S(1)}, bf16[2,128,768]{2,1,0:T(8,128)(2,1)S(1)}, u32[]{:S(2)}, u32[]{:S(2)}) collective-permute-start(bf16[2,128,768]{2,1,0:T(8,128)(2,1)S(1)} %get-tuple-element.33.refs_0_), channel_id=1, source_target_pairs={{0,2},{2,0},{1,3},{3,1},{4,6},{6,4},{5,7},{7,5},{8,10},{10,8},{9,1... | collective-permute-start | bytes 1179656 | tf_op jit(solution)/shard_map/ppermute | solution.py:16
  85.9 25.0 %collective-permute-start.9 = (bf16[64,2816]{1,0:T(8,128)(2,1)S(1)}, bf16[64,2816]{1,0:T(8,128)(2,1)S(1)}, u32[]{:S(2)}, u32[]{:S(2)}) collective-permute-start(bf16[64,2816]{1,0:T(8,128)(2,1)S(1)} %collective-permute-done.7.refs_1_), channel_id=1, source_target_pairs={{0,1},{1,0},{2,3},{3,2},{4,5},{5,4},{6,7},{7,6},{8,9},{9,8},{10,11... | collective-permute-start | bytes 1081352 | tf_op jit(solution)/shard_map/ppermute | solution.py:16
  96.4 23.1 %collective-permute-start.22 = (bf16[128,1344]{1,0:T(8,128)(2,1)S(1)}, bf16[128,1344]{1,0:T(8,128)(2,1)S(1)}, u32[]{:S(2)}, u32[]{:S(2)}) collective-permute-start(bf16[128,1344]{1,0:T(8,128)(2,1)S(1)} %add_convert_fusion.3), channel_id=1, source_target_pairs={{0,4},{4,8},{8,12},{12,0},{1,5},{5,9},{9,13},{13,1},{2,6},{6,10},{... | collective-permute-start | bytes 1032200 | tf_op jit(solution)/shard_map/ppermute | solution.py:16
  102.6 16.9 %collective-permute-start.16 = (bf16[128,1344]{1,0:T(8,128)(2,1)S(1)}, bf16[128,1344]{1,0:T(8,128)(2,1)S(1)}, u32[]{:S(2)}, u32[]{:S(2)}) collective-permute-start(bf16[128,1344]{1,0:T(8,128)(2,1)S(1)} %bitcast.17), channel_id=1, source_target_pairs={{0,1},{1,0},{2,3},{3,2},{4,5},{5,4},{6,7},{7,6},{8,9},{9,8},{10,11... | collective-permute-start | bytes 1032200 | tf_op jit(solution)/shard_map/ppermute | solution.py:16
  110.0 26.3 %collective-permute-start.2 = (bf16[2,128,768]{2,1,0:T(8,128)(2,1)S(1)}, bf16[2,128,768]{2,1,0:T(8,128)(2,1)S(1)}, u32[]{:S(2)}, u32[]{:S(2)}) collective-permute-start(bf16[2,128,768]{2,1,0:T(8,128)(2,1)S(1)} %get-tuple-element.25.refs_0_), channel_id=1, source_target_pairs={{0,2},{2,0},{1,3},{3,1},{4,6},{6,4},{5,7},{7,5},{8,10},{10,8},{9,1... | collective-permute-start | bytes 1179656 | tf_op jit(solution)/shard_map/ppermute | solution.py:16
  118.2 11.8 %collective-permute-start.10 = (bf16[2,128,768]{2,1,0:T(8,128)(2,1)S(1)}, bf16[2,128,768]{2,1,0:T(8,128)(2,1)S(1)}, u32[]{:S(2)}, u32[]{:S(2)}) collective-permute-start(bf16[2,128,768]{2,1,0:T(8,128)(2,1)S(1)} %get-tuple-element.29.refs_0_), channel_id=1, source_target_pairs={{0,2},{2,0},{1,3},{3,1},{4,6},{6,4},{5,7},{7,5},{8,10},{10,8},{9,1... | collective-permute-start | bytes 1179656 | tf_op jit(solution)/shard_map/ppermute | solution.py:16
  119.6 23.4 %collective-permute-start.23 = (bf16[128,1344]{1,0:T(8,128)(2,1)S(1)}, bf16[128,1344]{1,0:T(8,128)(2,1)S(1)}, u32[]{:S(2)}, u32[]{:S(2)}) collective-permute-start(bf16[128,1344]{1,0:T(8,128)(2,1)S(1)} %add_convert_fusion.2), channel_id=1, source_target_pairs={{0,4},{4,8},{8,12},{12,0},{1,5},{5,9},{9,13},{13,1},{2,6},{6,10},{... | collective-permute-start | bytes 1032200 | tf_op jit(solution)/shard_map/ppermute | solution.py:16
  136.2 6.9 %collective-permute-start.11 = (bf16[128,1344]{1,0:T(8,128)(2,1)S(1)}, bf16[128,1344]{1,0:T(8,128)(2,1)S(1)}, u32[]{:S(2)}, u32[]{:S(2)}) collective-permute-start(bf16[128,1344]{1,0:T(8,128)(2,1)S(1)} %bitcast.19), channel_id=1, source_target_pairs={{0,1},{1,0},{2,3},{3,2},{4,5},{5,4},{6,7},{7,6},{8,9},{9,8},{10,11... | collective-permute-start | bytes 1032200 | tf_op jit(solution)/shard_map/ppermute | solution.py:16
  142.5 2.0 %collective-permute-start.3 = (bf16[128,1344]{1,0:T(8,128)(2,1)S(1)}, bf16[128,1344]{1,0:T(8,128)(2,1)S(1)}, u32[]{:S(2)}, u32[]{:S(2)}) collective-permute-start(bf16[128,1344]{1,0:T(8,128)(2,1)S(1)} %bitcast.20), channel_id=1, source_target_pairs={{0,1},{1,0},{2,3},{3,2},{4,5},{5,4},{6,7},{7,6},{8,9},{9,8},{10,11... | collective-permute-start | bytes 1032200 | tf_op jit(solution)/shard_map/ppermute | solution.py:16
  143.2 12.5 %collective-permute-start.24 = (bf16[128,1344]{1,0:T(8,128)(2,1)S(1)}, bf16[128,1344]{1,0:T(8,128)(2,1)S(1)}, u32[]{:S(2)}, u32[]{:S(2)}) collective-permute-start(bf16[128,1344]{1,0:T(8,128)(2,1)S(1)} %add_convert_fusion.1), channel_id=1, source_target_pairs={{0,4},{4,8},{8,12},{12,0},{1,5},{5,9},{9,13},{13,1},{2,6},{6,10},{... | collective-permute-start | bytes 1032200 | tf_op jit(solution)/shard_map/ppermute | solution.py:16

commit v2 on v0

v2 whole, which is shorter than its diff:
```python
import functools

import jax
import jax.numpy as jnp
from jax import lax
from jax.experimental import pallas as pl
from jax.experimental.pallas import tpu as pltpu
from jax.sharding import PartitionSpec as P

LANES = 128
VMEM_LIMIT = 24 * 1024 * 1024
NT = (((1,), (1,)), ((), ()))
TN = (((0,), (0,)), ((), ()))


def shift(value, axis, by):
    size = lax.axis_size(axis)
    return lax.ppermute(value, axis, [(i, (i + by) % size) for i in range(size)])


in_memory = pltpu.with_memory_space_constraint


def after(value, earlier):
    return lax.optimization_barrier((value, earlier))[0]


def iota(shape, dim):
    return lax.broadcasted_iota(jnp.int32, shape, dim)


def prep_kernel(experts_all, parts, place, routes, gates, tokens, up_left, *refs):
    pieces, (routes_in, gates_in, rows_in, table_in, info, sems) = refs[:parts], refs[parts:]
    count, model_width = tokens.shape
    width = info.shape[1]
    factors = up_left.shape[0]
    rows = count // parts
    copies = [
        pltpu.make_async_copy(source, target, sems.at[i])
        for i, (source, target) in enumerate(
            ((routes, routes_in), (gates, gates_in), (up_left, table_in), (tokens, rows_in))
        )
    ]
    for copy in copies:
        copy.start()
    line = iota((width, count), 0)
    expert = lax.rem(line, experts_all)
    after_it = (iota((count, count), 0) < iota((count, count), 1)).astype(jnp.bfloat16)
    row = iota((width, factors), 0) - 3 * experts_all
    pick = (row >= 0) & (row < 2 * factors) & (lax.rem(row, factors) == iota((width, factors), 1))
    for copy in copies[:2]:
        copy.wait()
    gate_all = gates_in[...]
    normed = gate_all / jnp.sum(gate_all, axis=0, keepdims=True)
    named = jnp.zeros((width, count), jnp.float32)
    gate = jnp.zeros((width, count), jnp.float32)
    for k in range(routes.shape[0]):
        hit = routes_in[k : k + 1, :] == expert
        named = jnp.where(hit, 1.0, named)
        gate = jnp.where(hit, normed[k : k + 1, :], gate)
    slot = jnp.dot(named.astype(jnp.bfloat16), after_it, preferred_element_type=jnp.float32)
    slot = jnp.where(named > 0.0, slot, -1.0)
    copies[2].wait()
    left = jnp.dot(
        pick.astype(jnp.bfloat16), table_in[...], preferred_element_type=jnp.float32
    ).astype(jnp.bfloat16)
    copies[3].wait()
    low_rank = lax.dot_general(left, rows_in[...], NT, preferred_element_type=jnp.float32)
    value = jnp.where(line < 3 * experts_all, gate, low_rank)
    high = value.astype(jnp.bfloat16).astype(jnp.float32)
    is_low = ((line >= 2 * experts_all) & (line < 3 * experts_all)) | (
        line >= 3 * experts_all + factors
    )
    value = jnp.where(is_low, value - high, high)
    info[...] = jnp.where(line < experts_all, slot, value).T.astype(jnp.bfloat16)
    for j, piece in enumerate(pieces):
        at = pl.multiple_of(lax.rem(place[0] - j + parts, parts) * rows, rows)
        piece[:, :model_width] = rows_in[pl.ds(at, rows), :]
        piece[:, model_width:] = info[pl.ds(at, rows), :]


def up_kernel(first, experts_all, parts, cores, splits, capacity, factors, place, seeds, *refs):
    count = parts * (1 + (cores - 1) * splits)
    pieces = refs[:count]
    weight, right, hidden, gate_out, *tiles, block, slots, right_in, sems = refs[count:]
    rows = pieces[0].shape[0]
    tok_count = rows * parts
    tiles = tiles[0] if first else weight
    local_experts, _, hid = hidden.shape
    steps = tiles.shape[0] // local_experts
    model_width, tile = tiles.shape[1:]
    width = block.shape[1] - model_width
    expert_rows = cores * capacity
    slot_count = local_experts * expert_rows

    right_copy = pltpu.make_async_copy(right, right_in, sems.at[0])
    right_copy.start()
    copies = []
    if first:
        copies = [
            pltpu.make_async_copy(
                weight.at[l, :, pl.ds(n * tile, tile)],
                tiles.at[l * steps + n],
                sems.at[1 + l * steps + n],
            )
            for l in range(local_experts)
            for n in range(steps)
        ]
    for copy in copies:
        copy.start()

    column = iota((width, 2 * slot_count), 0)
    slot = iota((width, 2 * slot_count), 1)
    owner = place[1] + lax.rem(slot, slot_count) // expert_rows
    place_of = (column == owner).astype(jnp.bfloat16)
    gate_of = (
        column == owner + jnp.where(slot < slot_count, experts_all, 2 * experts_all)
    ).astype(jnp.bfloat16)
    lane = iota((tok_count, 2 * slot_count), 1)
    wanted = lax.rem(lane, capacity).astype(jnp.float32)
    base = 0
    for piece in pieces:
        block[base : base + piece.shape[0], :] = piece[...]
        base += piece.shape[0]
    choosers = []
    for b in range(cores):
        base = b * tok_count
        info = block[base : base + tok_count, model_width:]
        slot_of = jnp.dot(info, place_of, preferred_element_type=jnp.float32)
        gate = jnp.dot(info, gate_of, preferred_element_type=jnp.float32)
        here = (slot_of == wanted) & (lax.rem(lane, expert_rows) // capacity == b)
        gate = jnp.where(here, gate, 0.0).astype(jnp.bfloat16)
        for j in range(parts):
            at = lax.rem(place[0] - j + parts, parts) * rows
            gate_out[pl.ds(pl.multiple_of(base + at, rows), rows), :] = gate[
                j * rows : (j + 1) * rows, :
            ]
        choosers.append(here[:, :slot_count].astype(jnp.bfloat16))
    slots[...] = lax.dot_general(
        jnp.concatenate(choosers, axis=0), block[...], TN, preferred_element_type=jnp.float32
    ).astype(jnp.bfloat16)

    right_copy.wait()
    table = right_in[...].astype(jnp.float32)
    for l in range(local_experts):
        mine = slice(l * expert_rows, (l + 1) * expert_rows)
        extra = slots[mine, model_width:].astype(jnp.float32)
        at = iota(extra.shape, 1) - 3 * experts_all
        low_rank = jnp.sum(
            jnp.where((at == seeds[l, 0]) | (at == factors + seeds[l, 0]), extra, 0.0),
            axis=1,
            keepdims=True,
        )
        right_row = jnp.sum(
            jnp.where(iota(table.shape, 0) == seeds[l, 1], table, 0.0), axis=0, keepdims=True
        )
        for n in range(steps):
            if first:
                copies[l * steps + n].wait()
            up_act = jnp.dot(
                slots[mine, :model_width],
                tiles[l * steps + n],
                preferred_element_type=jnp.float32,
            )
            here = slice(n * tile, (n + 1) * tile)
            up_act = jnp.maximum(up_act + low_rank * right_row[:, here], 0.0)
            hidden[l, :, here] = (up_act * up_act).astype(jnp.bfloat16)


def down_kernel(first, parts, cores, pieces_out, place, seeds, *refs):
    pieces = refs[:parts]
    weight, left, right, gate, own, *rest = refs[parts:]
    others, rest = rest[: (cores - 1) * pieces_out], rest[(cores - 1) * pieces_out :]
    *tiles, results, left_in, right_in, sems = rest
    tiles = tiles[0] if first else weight
    local_experts, expert_rows, depth = pieces[0].shape
    steps = tiles.shape[0] // local_experts
    tile = tiles.shape[1]
    slot_count = local_experts * expert_rows
    tok_count = gate.shape[0] // cores

    tables = [
        pltpu.make_async_copy(left, left_in, sems.at[0]),
        pltpu.make_async_copy(right, right_in, sems.at[1]),
    ]
    copies = []
    if first:
        copies = [
            pltpu.make_async_copy(
                weight.at[l, pl.ds(n * tile, tile), :],
                tiles.at[l * steps + n],
                sems.at[2 + l * steps + n],
            )
            for l in range(local_experts)
            for n in range(steps)
        ]
    for copy in tables + copies:
        copy.start()

    columns = [slice(None)]
    if parts > 1:
        columns = [
            pl.ds(pl.multiple_of(lax.rem(place[0] - j + parts, parts) * depth, depth), depth)
            for j in range(parts)
        ]
    for copy in tables:
        copy.wait()
    for l in range(local_experts):
        rank_all = sum(
            lax.dot_general(left_in[:, at], piece[l], NT, preferred_element_type=jnp.float32)
            for at, piece in zip(columns, pieces)
        )
        rank = jnp.sum(
            jnp.where(iota(rank_all.shape, 0) == seeds[l, 2], rank_all, 0.0),
            axis=0,
            keepdims=True,
        )
        chosen = (iota((right.shape[0], expert_rows), 0) == seeds[l, 3]).astype(jnp.bfloat16)
        for n in range(steps):
            if first:
                copies[l * steps + n].wait()
            result = sum(
                lax.dot_general(
                    tiles[l * steps + n, :, at], piece[l], NT, preferred_element_type=jnp.float32
                )
                for at, piece in zip(columns, pieces)
            )
            here = slice(n * tile, (n + 1) * tile)
            right_column = lax.dot_general(
                right_in[:, here], chosen, TN, preferred_element_type=jnp.float32
            )
            result = (result + right_column * rank).astype(jnp.bfloat16)
            for half in range(2):
                at = half * slot_count + l * expert_rows
                results[here, at : at + expert_rows] = result
    summed = lax.dot_general(results[...], gate[...], NT, preferred_element_type=jnp.float32)
    own[...] = summed[:, :tok_count]
    step = summed.shape[0] // pieces_out
    for b in range(1, cores):
        for i in range(pieces_out):
            others[(b - 1) * pieces_out + i][...] = summed[
                i * step : (i + 1) * step, b * tok_count : (b + 1) * tok_count
            ].astype(jnp.bfloat16)


def on_device(
    tokens,
    routes,
    route_gates,
    up_weight,
    down_weight,
    factor_seeds,
    up_left,
    up_right,
    down_left,
    down_right,
):
    chips, cores, parts = lax.axis_size("ctx"), lax.axis_size("tp"), lax.axis_size("exp")
    local_experts, model_width, hid = up_weight.shape
    hid_all, out_width = down_weight.shape[1:]
    experts_all = chips * cores * local_experts
    tok_count, top_count = routes.shape
    factors = up_left.shape[0]
    capacity = 4 * tok_count * top_count // (3 * experts_all)
    rows = tok_count // parts
    width = -(-(3 * experts_all + 2 * factors) // LANES) * LANES
    packed = model_width + width
    expert_rows = cores * capacity
    slot_count = local_experts * expert_rows
    all_tokens = cores * tok_count
    first_expert = (lax.axis_index("ctx") * cores + lax.axis_index("tp")) * local_experts
    place = jnp.stack([lax.axis_index("exp"), first_expert]).astype(jnp.int32)
    whole_tiles = hid % LANES == 0
    params = pltpu.CompilerParams(vmem_limit_bytes=VMEM_LIMIT)
    smem, vmem, hbm = (
        pl.BlockSpec(memory_space=space) for space in (pltpu.SMEM, pltpu.VMEM, pltpu.HBM)
    )

    prep = pl.pallas_call(
        functools.partial(prep_kernel, experts_all, parts),
        out_shape=[jax.ShapeDtypeStruct((rows, packed), jnp.bfloat16)] * parts,
        in_specs=[smem, hbm, hbm, hbm, hbm],
        out_specs=[vmem] * parts,
        scratch_shapes=[
            pltpu.VMEM((top_count, tok_count), jnp.int32),
            pltpu.VMEM((top_count, tok_count), jnp.float32),
            pltpu.VMEM(tokens.shape, jnp.bfloat16),
            pltpu.VMEM(up_left.shape, jnp.bfloat16),
            pltpu.VMEM((tok_count, width), jnp.bfloat16),
            pltpu.SemaphoreType.DMA((4,)),
        ],
        compiler_params=params,
        name="pack_tokens",
    )

    splits = 2 if rows % 32 == 0 else 1
    up_steps = 3 if hid % (3 * LANES) == 0 else 1
    up_tiles = (local_experts * up_steps, model_width, hid // up_steps)

    def up(first):
        return pl.pallas_call(
            functools.partial(
                up_kernel, first, experts_all, parts, cores, splits, capacity, factors
            ),
            out_shape=[
                jax.ShapeDtypeStruct((local_experts, expert_rows, hid), jnp.bfloat16),
                jax.ShapeDtypeStruct((all_tokens, 2 * slot_count), jnp.bfloat16),
            ]
            + [jax.ShapeDtypeStruct(up_tiles, jnp.bfloat16)] * first,
            in_specs=[smem, smem] + [vmem] * (parts * (1 + (cores - 1) * splits)) + [hbm if first else vmem, hbm],
            out_specs=[vmem] * (2 + first),
            scratch_shapes=[
                pltpu.VMEM((all_tokens, packed), jnp.bfloat16),
                pltpu.VMEM((slot_count, packed), jnp.bfloat16),
                pltpu.VMEM(up_right.shape, jnp.bfloat16),
                pltpu.SemaphoreType.DMA((1 + local_experts * up_steps,)),
            ],
            compiler_params=params,
            name="up",
        )

    r_splits = 2 if out_width % 64 == 0 else 1
    down_steps = 3 if out_width % 48 == 0 else 1
    down_tiles = (local_experts * down_steps, out_width // down_steps, hid_all)
    hidden_parts = parts if whole_tiles else 1

    def down(first):
        return pl.pallas_call(
            functools.partial(down_kernel, first, hidden_parts, cores, r_splits),
            out_shape=[
                jax.ShapeDtypeStruct((out_width, tok_count), jnp.float32),
            ]
            + [jax.ShapeDtypeStruct((out_width // r_splits, tok_count), jnp.bfloat16)]
            * ((cores - 1) * r_splits)
            + [jax.ShapeDtypeStruct(down_tiles, jnp.bfloat16)] * first,
            in_specs=[smem, smem]
            + [vmem] * hidden_parts
            + [hbm if first else vmem, hbm, hbm, vmem],
            out_specs=[vmem] * (1 + (cores - 1) * r_splits + first),
            scratch_shapes=[
                pltpu.VMEM((out_width, 2 * slot_count), jnp.bfloat16),
                pltpu.VMEM(down_left.shape, jnp.bfloat16),
                pltpu.VMEM(down_right.shape, jnp.bfloat16),
                pltpu.SemaphoreType.DMA((2 + local_experts * down_steps,)),
            ],
            compiler_params=params,
            name="down",
        )

    place = in_memory(place, pltpu.SMEM)
    seeds = in_memory(factor_seeds, pltpu.SMEM)
    in_hbm = [
        in_memory(value, pltpu.HBM)
        for value in (
            routes.T, route_gates.T, tokens, up_left, up_weight, up_right,
            down_weight.transpose(0, 2, 1), down_left, down_right,
        )
    ]
    up_weight, up_right, down_turned, down_left, down_right = in_hbm[4:]
    pieces = list(prep(place, *in_hbm[:4]))
    kept = {}

    last = [pieces[0]]

    def order(value):
        last[0] = after(value, last[0])
        return last[0]

    def over_cores(piece):
        step = rows // splits
        return [
            [shift(piece[i * step : (i + 1) * step], "tp", b) for i in range(splits)]
            for b in range(1, cores)
        ]

    def over_exp(value):
        return [shift(value, "exp", j) for j in range(1, parts)]

    def run_up(here, there):
        blocks = here + [
            there[j][b][i] for b in range(cores - 1) for j in range(parts) for i in range(splits)
        ]
        first = "up" not in kept
        hidden, gate, *tiles = up(first)(
            place, seeds, order(blocks[0]), *blocks[1:], up_weight if first else kept["up"], up_right
        )
        if first:
            kept["up"] = tiles[0]
        last[0] = gate
        if whole_tiles:
            return [hidden] + over_exp(hidden), gate
        return [lax.all_gather(hidden, "exp", axis=2, tiled=True)], gate

    def run_down(hiddens, gate):
        first = "down" not in kept
        own, *others = down(first)(
            place,
            seeds,
            *hiddens[:-1],
            order(hiddens[-1]),
            down_turned if first else kept["down"],
            down_left,
            down_right,
            gate,
        )
        if first:
            kept["down"] = others.pop()
        last[0] = own
        return own, others

    def back(others):
        return [
            [shift(others[(b - 1) * r_splits + i], "tp", -b) for i in range(r_splits)]
            for b in range(1, cores)
        ]

    def add(own, swapped, *values):
        arrays = [piece for pieces in swapped for piece in pieces]

        def kernel(own, *refs):
            out, refs = refs[-1], refs[:-1]
            step = own.shape[0] // r_splits
            for i in range(r_splits):
                at = slice(i * step, (i + 1) * step)
                total = own[at, :]
                for b in range(cores - 1):
                    total = total + refs[b * r_splits + i][...].astype(jnp.float32)
                for value in refs[len(arrays) :]:
                    total = total + value[at, :].astype(jnp.float32)
                out[at, :] = total.astype(jnp.bfloat16)

        return pl.pallas_call(
            kernel,
            out_shape=jax.ShapeDtypeStruct(own.shape, jnp.bfloat16),
            in_specs=[vmem] * (1 + len(arrays) + len(values)),
            out_specs=vmem,
            compiler_params=params,
            cost_estimate=pl.CostEstimate(flops=1, bytes_accessed=1, transcendentals=0),
            name="add",
        )(own, *arrays, *values)

    def summed(own, others, *more):
        return add(own, back(others), *more)

    returned = {}

    def give_back(k, own, others):
        total = order(summed(own, [after(others[0], last[0])] + others[1:], *([returned[k - 1]] if k > 2 else [])))
        returned[k] = shift(total, "ctx", -1 if k == 1 else 1)

    arriving = shift(pieces[0], "ctx", 1)
    direct = [shift(piece, "ctx", -1) for piece in pieces[1:]]
    work = [run_up(pieces, [over_cores(piece) for piece in pieces])]
    arriving = order(arriving)
    direct = [order(piece) for piece in direct]
    direct_there = [over_cores(piece) for piece in direct]
    for k in range(1, chips):
        here = [arriving] + (over_exp(arriving) if k < chips - 1 else direct)
        there = [over_cores(arriving)]
        if k < chips - 1:
            arriving = shift(arriving, "ctx", 1)
        if k == 1:
            own_sum, own_others = run_down(*work[0])
            arriving = order(arriving)
        if k < chips - 1:
            here[1:] = [order(piece) for piece in here[1:]]
            there += [over_cores(piece) for piece in here[1:]]
        else:
            there += direct_there
        work.append(run_up(here, there))
        if 1 < k < chips - 1:
            arriving = order(arriving)
    for k in range(1, chips):
        sums = run_down(*work[k])
        give_back(k, *sums)
        if 1 < k == chips - 2:
            returned[1] = order(returned[1])
    homeward = {1, chips - 1}
    return add(own_sum, back(own_others), *(returned[k] for k in sorted(homeward))).T


def solution(mesh):
    in_specs = (
        P(("pop", "ctx", "tp"), None),
        P(("pop", "ctx", "tp"), None),
        P(("pop", "ctx", "tp"), None),
        P(("ctx", "tp"), None, "exp"),
        P(("ctx", "tp"), None, "exp"),
        P(("pop", "ctx", "tp"), None),
        P(),
        P(None, "exp"),
        P(),
        P(None, "exp"),
    )
    out_specs = P(("pop", "ctx", "tp"), "exp")
    return jax.shard_map(
        on_device, mesh=mesh, in_specs=in_specs, out_specs=out_specs, check_vma=False
    )
```

time: 317 us -> 97.3 us (0.31)
  waiting for transfers between devices: 231 us -> 34.8 us
  Pallas kernels: 0 us -> 38.5 us
  matrix products: 28.9 us -> 0 us
  local copies, waits for them, and re-layouts: 24.5 us -> 0.88 us
  between operations: 13.5 us -> 0.3 us
  starting transfers between devices: 11.1 us -> 22.1 us
  other arithmetic: 7.34 us -> 0.07 us
    all_to_all x2 -> x0, waiting for transfers between devices: 187 us -> none  [the longest x1 122 us: on_device(): lax.all_to_all(outgoing, ('ctx', 'tp'), split_axis=0, concat_axis=0, tile...]
    all_gather x1 -> x0, waiting for transfers between devices: 43.6 us -> none  [on_device(): full_hidden = lax.all_gather(hidden, 'exp', axis=3, tiled=True)]
    pallas_call x0 -> x13, Pallas kernels: none -> 38.5 us  [the longest x4 19.6 us: run_down(): down(first)]
    ppermute x0 -> x37, waiting for transfers between devices: none -> 34.8 us  [shift(): lax.ppermute(value, axis, [(i, (i + by) % size) for i in range(size)])]
    dot_general x8 -> x0, matrix products: 28.9 us -> none  [the longest x1 10.8 us: on_device(): jnp.einsum('slcd,ldh->slch', buffer, up_weight, preferred_element_type=jn...]
    ppermute x0 -> x37, starting transfers between devices: none -> 22.1 us  [shift(): lax.ppermute(value, axis, [(i, (i + by) % size) for i in range(size)])]
    all_to_all x2 -> x0, starting transfers between devices: 11.1 us -> none  [the longest x1 6.45 us: on_device(): lax.all_to_all(outgoing, ('ctx', 'tp'), split_axis=0, concat_axis=0, tile...]
    gather x2 -> x0, local copies, waits for them, and re-layouts: 10.3 us -> none  [the longest x1 6.58 us: on_device(): token_rows = padded_tokens[source_row]]
  transfers between devices with their start and end apart: 3 -> 37, of which waited for: 3 -> 20; matrix products, arithmetic and copies ran while one was open for 0% -> 0% of each run, Pallas kernels for 0% -> 36%
where the time goes in v2:
time: 97.3 us; the launch traced here: 96.8 us
  Pallas kernels  38.5 us (40%)
  waiting for transfers between devices  34.8 us (36%)
  starting transfers between devices  22.1 us (23%)
    ppermute x37, waiting for transfers between devices, shift(): lax.ppermute(value, axis, [(i, (i + by) % size) for i in range(size)])  34.8 us
    ppermute x37, starting transfers between devices, shift(): lax.ppermute(value, axis, [(i, (i + by) % size) for i in range(size)])  22.1 us
    pallas_call x4, Pallas kernels, run_down(): down(first)  19.6 us
    pallas_call x4, Pallas kernels, run_up(): up(first)  15.3 us
    pallas_call x1, Pallas kernels, on_device(): pieces = list(prep(place, *in_hbm[:4]))  2.51 us
  transfers between devices with their start and end apart: 37, of which 20 were waited for; matrix products, arithmetic and copies ran while one was open for 0% of the time, Pallas kernels for 36%

profile of v2, /device:TPU:0, one launch (start us, length us, event | category | flops | bytes accessed | tf_op | source)
XLA Modules:
  0.0 96.8 jit_solution(5416227835803011917)
XLA Ops:
  0.0 0.1 pad_add_fusion.place
  0.1 2.5 %pack_tokens.1 = (bf16[64,2816]{1,0:T(8,128)(2,1)S(1)}, bf16[64,2816]{1,0:T(8,128)(2,1)S(1)}) custom-call(s32[2]{0:T(128)S(1)} %pad_add_fusion.place, s32[6,128]{1,0:T(8,128)} %bitcast.7, f32[6,128]{1,0:T(8,128)} %bitcast.8, bf16[128,2688]{1,0:T(8,128)(2,1)} %tokens.1, bf16[16,2688]{1,0:T(8,128)(2,1)} %up_left.1), custom_call_target="tpu_custom_call" | custom-call | tf_op jit(solution)/shard_map/pack_tokens/pallas_call | solution.py:360
  2.6 3.1 %collective-permute-start.6 = (bf16[64,2816]{1,0:T(8,128)(2,1)S(1)}, bf16[64,2816]{1,0:T(8,128)(2,1)S(1)}, u32[]{:S(2)}, u32[]{:S(2)}) collective-permute-start(bf16[64,2816]{1,0:T(8,128)(2,1)S(1)} %get-tuple-element.51.refs_0_), channel_id=1, source_target_pairs={{0,4},{4,8},{8,12},{12,0},{1,5},{5,9},{9,13},{13,1},{2,6},{6,10},{... | collective-permute-start | bytes 1081352 | tf_op jit(solution)/shard_map/ppermute | solution.py:18
  5.8 0.5 collective-permute-start.1
  6.3 2.0 %collective-permute-start.5 = (bf16[64,2816]{1,0:T(8,128)(2,1)S(1)}, bf16[64,2816]{1,0:T(8,128)(2,1)S(1)}, u32[]{:S(2)}, u32[]{:S(2)}) collective-permute-start(bf16[64,2816]{1,0:T(8,128)(2,1)S(1)} %get-tuple-element.52.refs_1_), channel_id=1, source_target_pairs={{0,12},{4,0},{8,4},{12,8},{1,13},{5,1},{9,5},{13,9},{2,14},{6,2},{... | collective-permute-start | bytes 1081352 | tf_op jit(solution)/shard_map/ppermute | solution.py:18
  8.4 0.5 collective-permute-start.3
  8.9 0.9 collective-permute-done.2.refs_4_
  9.8 0.3 collective-permute-done.3.refs_5_
  10.1 0.7 copy-done
  10.8 5.6 %up.4 = (bf16[2,128,768]{2,1,0:T(8,128)(2,1)S(1)}, bf16[256,512]{1,0:T(8,128)(2,1)S(1)}, bf16[6,2688,256]{2,1,0:T(8,128)(2,1)S(1)}) custom-call(s32[2]{0:T(128)S(1)} %pad_add_fusion.place, s32[2,4]{1,0:T(2,128)S(1)} %copy-done, bf16[64,2816]{1,0:T(8,128)(2,1)S(1)} %get-tuple-element.51.refs_0_, bf16[64,2816]{1,0:T(8,128)(2,1)S(1)} %get-tuple-element.52.refs_1_, ...), custom_call_target="tpu_custom_call" | custom-call | tf_op jit(solution)/shard_map/up/pallas_call | solution.py:384
  16.4 1.8 %collective-permute-start.4 = (bf16[2,128,768]{2,1,0:T(8,128)(2,1)S(1)}, bf16[2,128,768]{2,1,0:T(8,128)(2,1)S(1)}, u32[]{:S(2)}, u32[]{:S(2)}) collective-permute-start(bf16[2,128,768]{2,1,0:T(8,128)(2,1)S(1)} %get-tuple-element.53.refs_0_), channel_id=1, source_target_pairs={{0,2},{2,0},{1,3},{3,1},{4,6},{6,4},{5,7},{7,5},{8,10},{10,8},{9,1... | collective-permute-start | bytes 1179656 | tf_op jit(solution)/shard_map/ppermute | solution.py:18
  18.2 0.5 collective-permute-start.9
  18.7 5.9 %collective-permute-done.5.refs_1_ = bf16[64,2816]{1,0:T(8,128)(2,1)S(1)} collective-permute-done((bf16[64,2816]{1,0:T(8,128)(2,1)S(1)}, bf16[64,2816]{1,0:T(8,128)(2,1)S(1)}, u32[]{:S(2)}, u32[]{:S(2)}) %collective-permute-start.5) | collective-permute-done | bytes 360480 | tf_op jit(solution)/shard_map/ppermute | solution.py:18
  24.7 0.5 collective-permute-start.12
  25.2 3.2 %collective-permute-done.4.refs_1_ = bf16[2,128,768]{2,1,0:T(8,128)(2,1)S(1)} collective-permute-done((bf16[2,128,768]{2,1,0:T(8,128)(2,1)S(1)}, bf16[2,128,768]{2,1,0:T(8,128)(2,1)S(1)}, u32[]{:S(2)}, u32[]{:S(2)}) %collective-permute-start.4) | collective-permute-done | bytes 393248 | tf_op jit(solution)/shard_map/ppermute | solution.py:18
  28.4 6.1 %down.4 = (f32[1344,128]{1,0:T(8,128)S(1)}, bf16[672,128]{1,0:T(8,128)(2,1)S(1)}, bf16[672,128]{1,0:T(8,128)(2,1)S(1)}, bf16[6,448,1536]{2,1,0:T(8,128)(2,1)S(1)}) custom-call(s32[2]{0:T(128)S(1)} %pad_add_fusion.place, s32[2,4]{1,0:T(2,128)S(1)} %copy-done, bf16[2,128,768]{2,1,0:T(8,128)(2,1)S(1)} %get-tuple-element.53.refs_0_, ...), custom_call_target="tpu_custom_call" | custom-call | tf_op jit(solution)/shard_map/down/pallas_call | solution.py:396
  34.6 1.8 %collective-permute-start.17 = (bf16[64,2816]{1,0:T(8,128)(2,1)S(1)}, bf16[64,2816]{1,0:T(8,128)(2,1)S(1)}, u32[]{:S(2)}, u32[]{:S(2)}) collective-permute-start(bf16[64,2816]{1,0:T(8,128)(2,1)S(1)} %collective-permute-done.10.refs_0_), channel_id=1, source_target_pairs={{0,2},{2,0},{1,3},{3,1},{4,6},{6,4},{5,7},{7,5},{8,10},{10,8},{9,1... | collective-permute-start | bytes 1081352 | tf_op jit(solution)/shard_map/ppermute | solution.py:18
  36.3 0.1 collective-permute-start.13
  36.4 0.5 collective-permute-start.14
  37.0 0.2 collective-permute-start.16
  37.2 0.1 collective-permute-start.18
  37.4 0.5 collective-permute-done.13.refs_4_
  37.8 0.1 collective-permute-start.19
  38.0 0.1 collective-permute-done.14.refs_5_
  38.1 3.2 %up.5 = (bf16[2,128,768]{2,1,0:T(8,128)(2,1)S(1)}, bf16[256,512]{1,0:T(8,128)(2,1)S(1)}) custom-call(s32[2]{0:T(128)S(1)} %pad_add_fusion.place, s32[2,4]{1,0:T(2,128)S(1)} %copy-done.1, bf16[64,2816]{1,0:T(8,128)(2,1)S(1)} %collective-permute-done.6.refs_0_, bf16[64,2816]{1,0:T(8,128)(2,1)S(1)} %collective-permute-done.9.refs_1_, ...), custom_call_target="tpu_custom_call" | custom-call | tf_op jit(solution)/shard_map/up/pallas_call | solution.py:384
  41.3 2.4 %collective-permute-done.17.refs_1_ = bf16[64,2816]{1,0:T(8,128)(2,1)S(1)} collective-permute-done((bf16[64,2816]{1,0:T(8,128)(2,1)S(1)}, bf16[64,2816]{1,0:T(8,128)(2,1)S(1)}, u32[]{:S(2)}, u32[]{:S(2)}) %collective-permute-start.17) | collective-permute-done | bytes 360480 | tf_op jit(solution)/shard_map/ppermute | solution.py:18
  43.7 0.1 collective-permute-start.20
  43.8 0.5 collective-permute-start.21
  44.3 0.1 collective-permute-start.24
  44.5 0.4 collective-permute-start.25
  44.9 0.3 collective-permute-done.20.refs_4_
  45.2 1.7 %collective-permute-start.15 = (bf16[2,128,768]{2,1,0:T(8,128)(2,1)S(1)}, bf16[2,128,768]{2,1,0:T(8,128)(2,1)S(1)}, u32[]{:S(2)}, u32[]{:S(2)}) collective-permute-start(bf16[2,128,768]{2,1,0:T(8,128)(2,1)S(1)} %get-tuple-element.65.refs_0_), channel_id=1, source_target_pairs={{0,2},{2,0},{1,3},{3,1},{4,6},{6,4},{5,7},{7,5},{8,10},{10,8},{9,1... | collective-permute-start | bytes 1179656 | tf_op jit(solution)/shard_map/ppermute | solution.py:18
  46.9 3.2 %up.6 = (bf16[2,128,768]{2,1,0:T(8,128)(2,1)S(1)}, bf16[256,512]{1,0:T(8,128)(2,1)S(1)}) custom-call(s32[2]{0:T(128)S(1)} %pad_add_fusion.place, s32[2,4]{1,0:T(2,128)S(1)} %copy-done.1, bf16[64,2816]{1,0:T(8,128)(2,1)S(1)} %collective-permute-done.10.refs_0_, bf16[64,2816]{1,0:T(8,128)(2,1)S(1)} %collective-permute-done.17.refs_1_, ...), custom_call_target="tpu_custom_call" | custom-call | tf_op jit(solution)/shard_map/up/pallas_call | solution.py:384
  50.2 0.4 collective-permute-start.29
  50.6 0.1 collective-permute-start.22
  50.7 0.5 collective-permute-start.23
  51.1 0.9 collective-permute-done.22.refs_2_
  52.0 0.3 collective-permute-done.23.refs_3_
  52.3 3.2 %up.7 = (bf16[2,128,768]{2,1,0:T(8,128)(2,1)S(1)}, bf16[256,512]{1,0:T(8,128)(2,1)S(1)}) custom-call(s32[2]{0:T(128)S(1)} %pad_add_fusion.place, s32[2,4]{1,0:T(2,128)S(1)} %copy-done.1, bf16[64,2816]{1,0:T(8,128)(2,1)S(1)} %collective-permute-done.16.refs_0_, bf16[64,2816]{1,0:T(8,128)(2,1)S(1)} %collective-permute-done.5.refs_1_, ...), custom_call_target="tpu_custom_call" | custom-call | tf_op jit(solution)/shard_map/up/pallas_call | solution.py:384
  55.5 1.6 %collective-permute-done.15.refs_1_ = bf16[2,128,768]{2,1,0:T(8,128)(2,1)S(1)} collective-permute-done((bf16[2,128,768]{2,1,0:T(8,128)(2,1)S(1)}, bf16[2,128,768]{2,1,0:T(8,128)(2,1)S(1)}, u32[]{:S(2)}, u32[]{:S(2)}) %collective-permute-start.15) | collective-permute-done | bytes 393248 | tf_op jit(solution)/shard_map/ppermute | solution.py:18
  57.2 4.5 %down.5 = (f32[1344,128]{1,0:T(8,128)S(1)}, bf16[672,128]{1,0:T(8,128)(2,1)S(1)}, bf16[672,128]{1,0:T(8,128)(2,1)S(1)}) custom-call(s32[2]{0:T(128)S(1)} %pad_add_fusion.place, s32[2,4]{1,0:T(2,128)S(1)} %copy-done.1, bf16[2,128,768]{2,1,0:T(8,128)(2,1)S(1)} %get-tuple-element.65.refs_0_, bf16[2,128,768]{2,1,0:T(8,128)(2,1)S(1)} %collective-permute-done.15.refs_1_, ...), custom_call_target="tpu_custom_call" | custom-call | tf_op jit(solution)/shard_map/down/pallas_call | solution.py:396
  61.7 0.1 collective-permute-start.26
  61.8 0.5 collective-permute-start.27
  62.3 1.7 %collective-permute-start.32 = (bf16[2,128,768]{2,1,0:T(8,128)(2,1)S(1)}, bf16[2,128,768]{2,1,0:T(8,128)(2,1)S(1)}, u32[]{:S(2)}, u32[]{:S(2)}) collective-permute-start(bf16[2,128,768]{2,1,0:T(8,128)(2,1)S(1)} %get-tuple-element.88.refs_0_), channel_id=1, source_target_pairs={{0,2},{2,0},{1,3},{3,1},{4,6},{6,4},{5,7},{7,5},{8,10},{10,8},{9,1... | collective-permute-start | bytes 1179656 | tf_op jit(solution)/shard_map/ppermute | solution.py:18
  64.0 0.1 add.10
  64.1 2.1 %collective-permute-start.28 = (bf16[1344,128]{1,0:T(8,128)(2,1)S(1)}, bf16[1344,128]{1,0:T(8,128)(2,1)S(1)}, u32[]{:S(2)}, u32[]{:S(2)}) collective-permute-start(bf16[1344,128]{1,0:T(8,128)(2,1)S(1)} %add.10), channel_id=1, source_target_pairs={{0,12},{4,0},{8,4},{12,8},{1,13},{5,1},{9,5},{13,9},{2,14},{6,2},{... | collective-permute-start | bytes 1032200 | tf_op jit(solution)/shard_map/ppermute | solution.py:18
  66.1 4.5 %down.6 = (f32[1344,128]{1,0:T(8,128)S(1)}, bf16[672,128]{1,0:T(8,128)(2,1)S(1)}, bf16[672,128]{1,0:T(8,128)(2,1)S(1)}) custom-call(s32[2]{0:T(128)S(1)} %pad_add_fusion.place, s32[2,4]{1,0:T(2,128)S(1)} %copy-done.1, bf16[2,128,768]{2,1,0:T(8,128)(2,1)S(1)} %get-tuple-element.80.refs_0_, bf16[2,128,768]{2,1,0:T(8,128)(2,1)S(1)} %collective-permute-done.29.refs_1_, ...), custom_call_target="tpu_custom_call" | custom-call | tf_op jit(solution)/shard_map/down/pallas_call | solution.py:396
  70.7 0.5 collective-permute-start.31
  71.2 0.9 collective-permute-done.30.refs_0_
  72.1 0.2 collective-permute-done.31.refs_1_
  72.4 0.3 collective-permute-start.35
  72.7 1.4 %collective-permute-done.28.refs_2_ = bf16[1344,128]{1,0:T(8,128)(2,1)S(1)} collective-permute-done((bf16[1344,128]{1,0:T(8,128)(2,1)S(1)}, bf16[1344,128]{1,0:T(8,128)(2,1)S(1)}, u32[]{:S(2)}, u32[]{:S(2)}) %collective-permute-start.28) | collective-permute-done | bytes 344096 | tf_op jit(solution)/shard_map/ppermute | solution.py:18
  74.1 4.5 %down.7 = (f32[1344,128]{1,0:T(8,128)S(1)}, bf16[672,128]{1,0:T(8,128)(2,1)S(1)}, bf16[672,128]{1,0:T(8,128)(2,1)S(1)}) custom-call(s32[2]{0:T(128)S(1)} %pad_add_fusion.place, s32[2,4]{1,0:T(2,128)S(1)} %copy-done.1, bf16[2,128,768]{2,1,0:T(8,128)(2,1)S(1)} %get-tuple-element.88.refs_0_, bf16[2,128,768]{2,1,0:T(8,128)(2,1)S(1)} %collective-permute-done.32.refs_1_, ...), custom_call_target="tpu_custom_call" | custom-call | tf_op jit(solution)/shard_map/down/pallas_call | solution.py:396
  78.6 0.1 collective-permute-start.33
  78.7 0.5 collective-permute-start.34
  79.2 0.9 collective-permute-done.33.refs_0_
  80.1 0.2 collective-permute-done.34.refs_1_
  80.3 4.2 %collective-permute-done.35.refs_2_ = bf16[1344,128]{1,0:T(8,128)(2,1)S(1)} collective-permute-done((bf16[1344,128]{1,0:T(8,128)(2,1)S(1)}, bf16[1344,128]{1,0:T(8,128)(2,1)S(1)}, u32[]{:S(2)}, u32[]{:S(2)}) %collective-permute-start.35) | collective-permute-done | bytes 344096 | tf_op jit(solution)/shard_map/ppermute | solution.py:18
  84.5 0.1 add.12
  84.8 0.5 collective-permute-start.8
  85.3 0.9 collective-permute-done.7.refs_0_
  86.2 0.2 collective-permute-done.8.refs_1_
  86.4 9.5 %collective-permute-done.36.refs_3_ = bf16[1344,128]{1,0:T(8,128)(2,1)S(1)} collective-permute-done((bf16[1344,128]{1,0:T(8,128)(2,1)S(1)}, bf16[1344,128]{1,0:T(8,128)(2,1)S(1)}, u32[]{:S(2)}, u32[]{:S(2)}) %collective-permute-start.36) | collective-permute-done | bytes 344096 | tf_op jit(solution)/shard_map/ppermute | solution.py:18
  95.9 0.9 add.13
  (36 shorter events, 0.7 us)
Async XLA Ops:
  2.6 15.6 %collective-permute-start.6 = (bf16[64,2816]{1,0:T(8,128)(2,1)S(1)}, bf16[64,2816]{1,0:T(8,128)(2,1)S(1)}, u32[]{:S(2)}, u32[]{:S(2)}) collective-permute-start(bf16[64,2816]{1,0:T(8,128)(2,1)S(1)} %get-tuple-element.51.refs_0_), channel_id=1, source_target_pairs={{0,4},{4,8},{8,12},{12,0},{1,5},{5,9},{9,13},{13,1},{2,6},{6,10},{... | collective-permute-start | bytes 1081352 | tf_op jit(solution)/shard_map/ppermute | solution.py:18
  5.7 2.7 %collective-permute-start = (bf16[32,2816]{1,0:T(8,128)(2,1)S(1)}, bf16[32,2816]{1,0:T(8,128)(2,1)S(1)}, u32[]{:S(2)}, u32[]{:S(2)}) collective-permute-start(bf16[32,2816]{1,0:T(8,128)(2,1)S(1)} %get-tuple-element.110), channel_id=1, source_target_pairs={{0,1},{1,0},{2,3},{3,2},{4,5},{5,4},{6,7},{7,6},{8,9},{9,8},{10,11... | collective-permute-start | bytes 540680 | tf_op jit(solution)/shard_map/ppermute | solution.py:18
  5.8 3.2 %collective-permute-start.1 = (bf16[32,2816]{1,0:T(8,128)(2,1)S(1)}, bf16[32,2816]{1,0:T(8,128)(2,1)S(1)}, u32[]{:S(2)}, u32[]{:S(2)}) collective-permute-start(bf16[32,2816]{1,0:T(8,128)(2,1)S(1)} %get-tuple-element.109), channel_id=1, source_target_pairs={{0,1},{1,0},{2,3},{3,2},{4,5},{5,4},{6,7},{7,6},{8,9},{9,8},{10,11... | collective-permute-start | bytes 540680 | tf_op jit(solution)/shard_map/ppermute | solution.py:18
  6.3 18.3 %collective-permute-start.5 = (bf16[64,2816]{1,0:T(8,128)(2,1)S(1)}, bf16[64,2816]{1,0:T(8,128)(2,1)S(1)}, u32[]{:S(2)}, u32[]{:S(2)}) collective-permute-start(bf16[64,2816]{1,0:T(8,128)(2,1)S(1)} %get-tuple-element.52.refs_1_), channel_id=1, source_target_pairs={{0,12},{4,0},{8,4},{12,8},{1,13},{5,1},{9,5},{13,9},{2,14},{6,2},{... | collective-permute-start | bytes 1081352 | tf_op jit(solution)/shard_map/ppermute | solution.py:18
  8.3 1.5 %collective-permute-start.2 = (bf16[32,2816]{1,0:T(8,128)(2,1)S(1)}, bf16[32,2816]{1,0:T(8,128)(2,1)S(1)}, u32[]{:S(2)}, u32[]{:S(2)}) collective-permute-start(bf16[32,2816]{1,0:T(8,128)(2,1)S(1)} %get-tuple-element.108), channel_id=1, source_target_pairs={{0,1},{1,0},{2,3},{3,2},{4,5},{5,4},{6,7},{7,6},{8,9},{9,8},{10,11... | collective-permute-start | bytes 540680 | tf_op jit(solution)/shard_map/ppermute | solution.py:18
  8.4 29.7 %copy-start.1 = (s32[2,4]{1,0:T(2,128)S(1)}, s32[2,4]{1,0:T(2,128)}, u32[]{:S(2)}) copy-start(s32[2,4]{1,0:T(2,128)} %seeds.15) | copy-start | bytes 100
  8.4 1.6 %collective-permute-start.3 = (bf16[32,2816]{1,0:T(8,128)(2,1)S(1)}, bf16[32,2816]{1,0:T(8,128)(2,1)S(1)}, u32[]{:S(2)}, u32[]{:S(2)}) collective-permute-start(bf16[32,2816]{1,0:T(8,128)(2,1)S(1)} %get-tuple-element.107), channel_id=1, source_target_pairs={{0,1},{1,0},{2,3},{3,2},{4,5},{5,4},{6,7},{7,6},{8,9},{9,8},{10,11... | collective-permute-start | bytes 540680 | tf_op jit(solution)/shard_map/ppermute | solution.py:18
  10.1 0.7 copy-start
  16.4 12.0 %collective-permute-start.4 = (bf16[2,128,768]{2,1,0:T(8,128)(2,1)S(1)}, bf16[2,128,768]{2,1,0:T(8,128)(2,1)S(1)}, u32[]{:S(2)}, u32[]{:S(2)}) collective-permute-start(bf16[2,128,768]{2,1,0:T(8,128)(2,1)S(1)} %get-tuple-element.53.refs_0_), channel_id=1, source_target_pairs={{0,2},{2,0},{1,3},{3,1},{4,6},{6,4},{5,7},{7,5},{8,10},{10,8},{9,1... | collective-permute-start | bytes 1179656 | tf_op jit(solution)/shard_map/ppermute | solution.py:18
  18.2 16.4 %collective-permute-start.10 = (bf16[64,2816]{1,0:T(8,128)(2,1)S(1)}, bf16[64,2816]{1,0:T(8,128)(2,1)S(1)}, u32[]{:S(2)}, u32[]{:S(2)}) collective-permute-start(bf16[64,2816]{1,0:T(8,128)(2,1)S(1)} %collective-permute-done.6.refs_0_), channel_id=1, source_target_pairs={{0,4},{4,8},{8,12},{12,0},{1,5},{5,9},{9,13},{13,1},{2,6},{6,10},{... | collective-permute-start | bytes 1081352 | tf_op jit(solution)/shard_map/ppermute | solution.py:18
  18.2 18.1 %collective-permute-start.9 = (bf16[64,2816]{1,0:T(8,128)(2,1)S(1)}, bf16[64,2816]{1,0:T(8,128)(2,1)S(1)}, u32[]{:S(2)}, u32[]{:S(2)}) collective-permute-start(bf16[64,2816]{1,0:T(8,128)(2,1)S(1)} %collective-permute-done.6.refs_0_), channel_id=1, source_target_pairs={{0,2},{2,0},{1,3},{3,1},{4,6},{6,4},{5,7},{7,5},{8,10},{10,8},{9,1... | collective-permute-start | bytes 1081352 | tf_op jit(solution)/shard_map/ppermute | solution.py:18
  24.6 12.3 %collective-permute-start.11 = (bf16[32,2816]{1,0:T(8,128)(2,1)S(1)}, bf16[32,2816]{1,0:T(8,128)(2,1)S(1)}, u32[]{:S(2)}, u32[]{:S(2)}) collective-permute-start(bf16[32,2816]{1,0:T(8,128)(2,1)S(1)} %get-tuple-element.106), channel_id=1, source_target_pairs={{0,1},{1,0},{2,3},{3,2},{4,5},{5,4},{6,7},{7,6},{8,9},{9,8},{10,11... | collective-permute-start | bytes 540680 | tf_op jit(solution)/shard_map/ppermute | solution.py:18
  24.7 12.5 %collective-permute-start.12 = (bf16[32,2816]{1,0:T(8,128)(2,1)S(1)}, bf16[32,2816]{1,0:T(8,128)(2,1)S(1)}, u32[]{:S(2)}, u32[]{:S(2)}) collective-permute-start(bf16[32,2816]{1,0:T(8,128)(2,1)S(1)} %get-tuple-element.105), channel_id=1, source_target_pairs={{0,1},{1,0},{2,3},{3,2},{4,5},{5,4},{6,7},{7,6},{8,9},{9,8},{10,11... | collective-permute-start | bytes 540680 | tf_op jit(solution)/shard_map/ppermute | solution.py:18
  34.6 9.1 %collective-permute-start.17 = (bf16[64,2816]{1,0:T(8,128)(2,1)S(1)}, bf16[64,2816]{1,0:T(8,128)(2,1)S(1)}, u32[]{:S(2)}, u32[]{:S(2)}) collective-permute-start(bf16[64,2816]{1,0:T(8,128)(2,1)S(1)} %collective-permute-done.10.refs_0_), channel_id=1, source_target_pairs={{0,2},{2,0},{1,3},{3,1},{4,6},{6,4},{5,7},{7,5},{8,10},{10,8},{9,1... | collective-permute-start | bytes 1081352 | tf_op jit(solution)/shard_map/ppermute | solution.py:18
  36.3 1.5 %collective-permute-start.13 = (bf16[32,2816]{1,0:T(8,128)(2,1)S(1)}, bf16[32,2816]{1,0:T(8,128)(2,1)S(1)}, u32[]{:S(2)}, u32[]{:S(2)}) collective-permute-start(bf16[32,2816]{1,0:T(8,128)(2,1)S(1)} %get-tuple-element.104), channel_id=1, source_target_pairs={{0,1},{1,0},{2,3},{3,2},{4,5},{5,4},{6,7},{7,6},{8,9},{9,8},{10,11... | collective-permute-start | bytes 540680 | tf_op jit(solution)/shard_map/ppermute | solution.py:18
  36.4 1.7 %collective-permute-start.14 = (bf16[32,2816]{1,0:T(8,128)(2,1)S(1)}, bf16[32,2816]{1,0:T(8,128)(2,1)S(1)}, u32[]{:S(2)}, u32[]{:S(2)}) collective-permute-start(bf16[32,2816]{1,0:T(8,128)(2,1)S(1)} %get-tuple-element.103), channel_id=1, source_target_pairs={{0,1},{1,0},{2,3},{3,2},{4,5},{5,4},{6,7},{7,6},{8,9},{9,8},{10,11... | collective-permute-start | bytes 540680 | tf_op jit(solution)/shard_map/ppermute | solution.py:18
  37.0 13.2 %collective-permute-start.16 = (bf16[64,2816]{1,0:T(8,128)(2,1)S(1)}, bf16[64,2816]{1,0:T(8,128)(2,1)S(1)}, u32[]{:S(2)}, u32[]{:S(2)}) collective-permute-start(bf16[64,2816]{1,0:T(8,128)(2,1)S(1)} %collective-permute-done.10.refs_0_), channel_id=1, source_target_pairs={{0,4},{4,8},{8,12},{12,0},{1,5},{5,9},{9,13},{13,1},{2,6},{6,10},{... | collective-permute-start | bytes 1081352 | tf_op jit(solution)/shard_map/ppermute | solution.py:18
  37.2 7.1 %collective-permute-start.18 = (bf16[32,2816]{1,0:T(8,128)(2,1)S(1)}, bf16[32,2816]{1,0:T(8,128)(2,1)S(1)}, u32[]{:S(2)}, u32[]{:S(2)}) collective-permute-start(bf16[32,2816]{1,0:T(8,128)(2,1)S(1)} %get-tuple-element.102), channel_id=1, source_target_pairs={{0,1},{1,0},{2,3},{3,2},{4,5},{5,4},{6,7},{7,6},{8,9},{9,8},{10,11... | collective-permute-start | bytes 540680 | tf_op jit(solution)/shard_map/ppermute | solution.py:18
  37.8 6.7 %collective-permute-start.19 = (bf16[32,2816]{1,0:T(8,128)(2,1)S(1)}, bf16[32,2816]{1,0:T(8,128)(2,1)S(1)}, u32[]{:S(2)}, u32[]{:S(2)}) collective-permute-start(bf16[32,2816]{1,0:T(8,128)(2,1)S(1)} %get-tuple-element.101), channel_id=1, source_target_pairs={{0,1},{1,0},{2,3},{3,2},{4,5},{5,4},{6,7},{7,6},{8,9},{9,8},{10,11... | collective-permute-start | bytes 540680 | tf_op jit(solution)/shard_map/ppermute | solution.py:18
  43.7 1.5 %collective-permute-start.20 = (bf16[32,2816]{1,0:T(8,128)(2,1)S(1)}, bf16[32,2816]{1,0:T(8,128)(2,1)S(1)}, u32[]{:S(2)}, u32[]{:S(2)}) collective-permute-start(bf16[32,2816]{1,0:T(8,128)(2,1)S(1)} %get-tuple-element.100), channel_id=1, source_target_pairs={{0,1},{1,0},{2,3},{3,2},{4,5},{5,4},{6,7},{7,6},{8,9},{9,8},{10,11... | collective-permute-start | bytes 540680 | tf_op jit(solution)/shard_map/ppermute | solution.py:18
  43.8 3.1 %collective-permute-start.21 = (bf16[32,2816]{1,0:T(8,128)(2,1)S(1)}, bf16[32,2816]{1,0:T(8,128)(2,1)S(1)}, u32[]{:S(2)}, u32[]{:S(2)}) collective-permute-start(bf16[32,2816]{1,0:T(8,128)(2,1)S(1)} %get-tuple-element.99), channel_id=1, source_target_pairs={{0,1},{1,0},{2,3},{3,2},{4,5},{5,4},{6,7},{7,6},{8,9},{9,8},{10,11... | collective-permute-start | bytes 540680 | tf_op jit(solution)/shard_map/ppermute | solution.py:18
  44.3 6.3 %collective-permute-start.24 = (bf16[32,2816]{1,0:T(8,128)(2,1)S(1)}, bf16[32,2816]{1,0:T(8,128)(2,1)S(1)}, u32[]{:S(2)}, u32[]{:S(2)}) collective-permute-start(bf16[32,2816]{1,0:T(8,128)(2,1)S(1)} %get-tuple-element.96), channel_id=1, source_target_pairs={{0,1},{1,0},{2,3},{3,2},{4,5},{5,4},{6,7},{7,6},{8,9},{9,8},{10,11... | collective-permute-start | bytes 540680 | tf_op jit(solution)/shard_map/ppermute | solution.py:18
  44.5 6.6 %collective-permute-start.25 = (bf16[32,2816]{1,0:T(8,128)(2,1)S(1)}, bf16[32,2816]{1,0:T(8,128)(2,1)S(1)}, u32[]{:S(2)}, u32[]{:S(2)}) collective-permute-start(bf16[32,2816]{1,0:T(8,128)(2,1)S(1)} %get-tuple-element.95), channel_id=1, source_target_pairs={{0,1},{1,0},{2,3},{3,2},{4,5},{5,4},{6,7},{7,6},{8,9},{9,8},{10,11... | collective-permute-start | bytes 540680 | tf_op jit(solution)/shard_map/ppermute | solution.py:18
  45.2 12.0 %collective-permute-start.15 = (bf16[2,128,768]{2,1,0:T(8,128)(2,1)S(1)}, bf16[2,128,768]{2,1,0:T(8,128)(2,1)S(1)}, u32[]{:S(2)}, u32[]{:S(2)}) collective-permute-start(bf16[2,128,768]{2,1,0:T(8,128)(2,1)S(1)} %get-tuple-element.65.refs_0_), channel_id=1, source_target_pairs={{0,2},{2,0},{1,3},{3,1},{4,6},{6,4},{5,7},{7,5},{8,10},{10,8},{9,1... | collective-permute-start | bytes 1179656 | tf_op jit(solution)/shard_map/ppermute | solution.py:18
  50.2 16.0 %collective-permute-start.29 = (bf16[2,128,768]{2,1,0:T(8,128)(2,1)S(1)}, bf16[2,128,768]{2,1,0:T(8,128)(2,1)S(1)}, u32[]{:S(2)}, u32[]{:S(2)}) collective-permute-start(bf16[2,128,768]{2,1,0:T(8,128)(2,1)S(1)} %get-tuple-element.80.refs_0_), channel_id=1, source_target_pairs={{0,2},{2,0},{1,3},{3,1},{4,6},{6,4},{5,7},{7,5},{8,10},{10,8},{9,1... | collective-permute-start | bytes 1179656 | tf_op jit(solution)/shard_map/ppermute | solution.py:18
  50.6 1.5 %collective-permute-start.22 = (bf16[32,2816]{1,0:T(8,128)(2,1)S(1)}, bf16[32,2816]{1,0:T(8,128)(2,1)S(1)}, u32[]{:S(2)}, u32[]{:S(2)}) collective-permute-start(bf16[32,2816]{1,0:T(8,128)(2,1)S(1)} %get-tuple-element.98), channel_id=1, source_target_pairs={{0,1},{1,0},{2,3},{3,2},{4,5},{5,4},{6,7},{7,6},{8,9},{9,8},{10,11... | collective-permute-start | bytes 540680 | tf_op jit(solution)/shard_map/ppermute | solution.py:18
  50.7 1.7 %collective-permute-start.23 = (bf16[32,2816]{1,0:T(8,128)(2,1)S(1)}, bf16[32,2816]{1,0:T(8,128)(2,1)S(1)}, u32[]{:S(2)}, u32[]{:S(2)}) collective-permute-start(bf16[32,2816]{1,0:T(8,128)(2,1)S(1)} %get-tuple-element.97), channel_id=1, source_target_pairs={{0,1},{1,0},{2,3},{3,2},{4,5},{5,4},{6,7},{7,6},{8,9},{9,8},{10,11... | collective-permute-start | bytes 540680 | tf_op jit(solution)/shard_map/ppermute | solution.py:18
  61.7 2.3 %collective-permute-start.26 = (bf16[672,128]{1,0:T(8,128)(2,1)S(1)}, bf16[672,128]{1,0:T(8,128)(2,1)S(1)}, u32[]{:S(2)}, u32[]{:S(2)}) collective-permute-start(bf16[672,128]{1,0:T(8,128)(2,1)S(1)} %get-tuple-element.77), channel_id=1, source_target_pairs={{0,1},{1,0},{2,3},{3,2},{4,5},{5,4},{6,7},{7,6},{8,9},{9,8},{10,11... | collective-permute-start | bytes 516104 | tf_op jit(solution)/shard_map/ppermute | solution.py:18
  61.8 2.2 %collective-permute-start.27 = (bf16[672,128]{1,0:T(8,128)(2,1)S(1)}, bf16[672,128]{1,0:T(8,128)(2,1)S(1)}, u32[]{:S(2)}, u32[]{:S(2)}) collective-permute-start(bf16[672,128]{1,0:T(8,128)(2,1)S(1)} %get-tuple-element.78), channel_id=1, source_target_pairs={{0,1},{1,0},{2,3},{3,2},{4,5},{5,4},{6,7},{7,6},{8,9},{9,8},{10,11... | collective-permute-start | bytes 516104 | tf_op jit(solution)/shard_map/ppermute | solution.py:18
  62.3 11.8 %collective-permute-start.32 = (bf16[2,128,768]{2,1,0:T(8,128)(2,1)S(1)}, bf16[2,128,768]{2,1,0:T(8,128)(2,1)S(1)}, u32[]{:S(2)}, u32[]{:S(2)}) collective-permute-start(bf16[2,128,768]{2,1,0:T(8,128)(2,1)S(1)} %get-tuple-element.88.refs_0_), channel_id=1, source_target_pairs={{0,2},{2,0},{1,3},{3,1},{4,6},{6,4},{5,7},{7,5},{8,10},{10,8},{9,1... | collective-permute-start | bytes 1179656 | tf_op jit(solution)/shard_map/ppermute | solution.py:18
  64.1 10.0 %collective-permute-start.28 = (bf16[1344,128]{1,0:T(8,128)(2,1)S(1)}, bf16[1344,128]{1,0:T(8,128)(2,1)S(1)}, u32[]{:S(2)}, u32[]{:S(2)}) collective-permute-start(bf16[1344,128]{1,0:T(8,128)(2,1)S(1)} %add.10), channel_id=1, source_target_pairs={{0,12},{4,0},{8,4},{12,8},{1,13},{5,1},{9,5},{13,9},{2,14},{6,2},{... | collective-permute-start | bytes 1032200 | tf_op jit(solution)/shard_map/ppermute | solution.py:18
  70.6 1.5 %collective-permute-start.30 = (bf16[672,128]{1,0:T(8,128)(2,1)S(1)}, bf16[672,128]{1,0:T(8,128)(2,1)S(1)}, u32[]{:S(2)}, u32[]{:S(2)}) collective-permute-start(bf16[672,128]{1,0:T(8,128)(2,1)S(1)} %get-tuple-element.84), channel_id=1, source_target_pairs={{0,1},{1,0},{2,3},{3,2},{4,5},{5,4},{6,7},{7,6},{8,9},{9,8},{10,11... | collective-permute-start | bytes 516104 | tf_op jit(solution)/shard_map/ppermute | solution.py:18
  70.7 1.6 %collective-permute-start.31 = (bf16[672,128]{1,0:T(8,128)(2,1)S(1)}, bf16[672,128]{1,0:T(8,128)(2,1)S(1)}, u32[]{:S(2)}, u32[]{:S(2)}) collective-permute-start(bf16[672,128]{1,0:T(8,128)(2,1)S(1)} %get-tuple-element.85), channel_id=1, source_target_pairs={{0,1},{1,0},{2,3},{3,2},{4,5},{5,4},{6,7},{7,6},{8,9},{9,8},{10,11... | collective-permute-start | bytes 516104 | tf_op jit(solution)/shard_map/ppermute | solution.py:18
  72.4 12.1 %collective-permute-start.35 = (bf16[1344,128]{1,0:T(8,128)(2,1)S(1)}, bf16[1344,128]{1,0:T(8,128)(2,1)S(1)}, u32[]{:S(2)}, u32[]{:S(2)}) collective-permute-start(bf16[1344,128]{1,0:T(8,128)(2,1)S(1)} %add.11), channel_id=1, source_target_pairs={{0,4},{4,8},{8,12},{12,0},{1,5},{5,9},{9,13},{13,1},{2,6},{6,10},{... | collective-permute-start | bytes 1032200 | tf_op jit(solution)/shard_map/ppermute | solution.py:18
  78.6 1.5 %collective-permute-start.33 = (bf16[672,128]{1,0:T(8,128)(2,1)S(1)}, bf16[672,128]{1,0:T(8,128)(2,1)S(1)}, u32[]{:S(2)}, u32[]{:S(2)}) collective-permute-start(bf16[672,128]{1,0:T(8,128)(2,1)S(1)} %get-tuple-element.92), channel_id=1, source_target_pairs={{0,1},{1,0},{2,3},{3,2},{4,5},{5,4},{6,7},{7,6},{8,9},{9,8},{10,11... | collective-permute-start | bytes 516104 | tf_op jit(solution)/shard_map/ppermute | solution.py:18
  78.7 1.6 %collective-permute-start.34 = (bf16[672,128]{1,0:T(8,128)(2,1)S(1)}, bf16[672,128]{1,0:T(8,128)(2,1)S(1)}, u32[]{:S(2)}, u32[]{:S(2)}) collective-permute-start(bf16[672,128]{1,0:T(8,128)(2,1)S(1)} %get-tuple-element.93), channel_id=1, source_target_pairs={{0,1},{1,0},{2,3},{3,2},{4,5},{5,4},{6,7},{7,6},{8,9},{9,8},{10,11... | collective-permute-start | bytes 516104 | tf_op jit(solution)/shard_map/ppermute | solution.py:18
  84.6 11.3 %collective-permute-start.36 = (bf16[1344,128]{1,0:T(8,128)(2,1)S(1)}, bf16[1344,128]{1,0:T(8,128)(2,1)S(1)}, u32[]{:S(2)}, u32[]{:S(2)}) collective-permute-start(bf16[1344,128]{1,0:T(8,128)(2,1)S(1)} %add.12), channel_id=1, source_target_pairs={{0,4},{4,8},{8,12},{12,0},{1,5},{5,9},{9,13},{13,1},{2,6},{6,10},{... | collective-permute-start | bytes 1032200 | tf_op jit(solution)/shard_map/ppermute | solution.py:18
  84.7 1.5 %collective-permute-start.7 = (bf16[672,128]{1,0:T(8,128)(2,1)S(1)}, bf16[672,128]{1,0:T(8,128)(2,1)S(1)}, u32[]{:S(2)}, u32[]{:S(2)}) collective-permute-start(bf16[672,128]{1,0:T(8,128)(2,1)S(1)} %get-tuple-element.59), channel_id=1, source_target_pairs={{0,1},{1,0},{2,3},{3,2},{4,5},{5,4},{6,7},{7,6},{8,9},{9,8},{10,11... | collective-permute-start | bytes 516104 | tf_op jit(solution)/shard_map/ppermute | solution.py:18
  84.8 1.6 %collective-permute-start.8 = (bf16[672,128]{1,0:T(8,128)(2,1)S(1)}, bf16[672,128]{1,0:T(8,128)(2,1)S(1)}, u32[]{:S(2)}, u32[]{:S(2)}) collective-permute-start(bf16[672,128]{1,0:T(8,128)(2,1)S(1)} %get-tuple-element.60), channel_id=1, source_target_pairs={{0,1},{1,0},{2,3},{3,2},{4,5},{5,4},{6,7},{7,6},{8,9},{9,8},{10,11... | collective-permute-start | bytes 516104 | tf_op jit(solution)/shard_map/ppermute | solution.py:18

commit v3 on v2

--- a/solution.py
+++ b/solution.py
@@ -29,8 +29,17 @@
     return lax.broadcasted_iota(jnp.int32, shape, dim)
 
 
-def prep_kernel(experts_all, parts, place, routes, gates, tokens, up_left, *refs):
-    pieces, (routes_in, gates_in, rows_in, table_in, info, sems) = refs[:parts], refs[parts:]
+def my_part():
+    return lax.axis_index("exp")
+
+
+def first_expert(local_experts):
+    return (lax.axis_index("ctx") * lax.axis_size("tp") + lax.axis_index("tp")) * local_experts
+
+
+def prep_kernel(experts_all, parts, routes, gates, tokens, up_left, weight, *refs):
+    pieces, tiles = refs[:parts], refs[parts]
+    routes_in, gates_in, rows_in, table_in, info, sems = refs[parts + 1 :]
     count, model_width = tokens.shape
     width = info.shape[1]
     factors = up_left.shape[0]
@@ -41,7 +50,14 @@
             ((routes, routes_in), (gates, gates_in), (up_left, table_in), (tokens, rows_in))
         )
     ]
-    for copy in copies:
+    steps, _, tile = tiles.shape
+    loads = [
+        pltpu.make_async_copy(
+            weight.at[0, :, pl.ds(n * tile, tile)], tiles.at[n], sems.at[len(copies) + n]
+        )
+        for n in range(steps)
+    ]
+    for copy in copies + loads:
         copy.start()
     line = iota((width, count), 0)
     expert = lax.rem(line, experts_all)
@@ -74,44 +90,64 @@
     value = jnp.where(is_low, value - high, high)
     info[...] = jnp.where(line < experts_all, slot, value).T.astype(jnp.bfloat16)
     for j, piece in enumerate(pieces):
-        at = pl.multiple_of(lax.rem(place[0] - j + parts, parts) * rows, rows)
+        at = pl.multiple_of(lax.rem(my_part() - j + parts, parts) * rows, rows)
         piece[:, :model_width] = rows_in[pl.ds(at, rows), :]
         piece[:, model_width:] = info[pl.ds(at, rows), :]
-
-
-def up_kernel(first, experts_all, parts, cores, splits, capacity, factors, place, seeds, *refs):
+    for copy in loads:
+        copy.wait()
+
+
+def up_kernel(first, load, experts_all, parts, cores, splits, capacity, factors, *refs):
     count = parts * (1 + (cores - 1) * splits)
     pieces = refs[:count]
-    weight, right, hidden, gate_out, *tiles, block, slots, right_in, sems = refs[count:]
+    tiles_first, weight, right, seeds_in, *rest = refs[count:-5]
+    down_weight = rest.pop(0) if load else None
+    hidden, gate_out, *tiles_rest = rest
+    down_tiles = tiles_rest.pop() if load else None
+    block, slots, right_in, seeds, sems = refs[-5:]
     rows = pieces[0].shape[0]
     tok_count = rows * parts
-    tiles = tiles[0] if first else weight
+    tiles_rest = tiles_rest[0] if first else weight
     local_experts, _, hid = hidden.shape
-    steps = tiles.shape[0] // local_experts
-    model_width, tile = tiles.shape[1:]
+    steps, model_width, tile = tiles_first.shape
     width = block.shape[1] - model_width
     expert_rows = cores * capacity
     slot_count = local_experts * expert_rows
 
-    right_copy = pltpu.make_async_copy(right, right_in, sems.at[0])
-    right_copy.start()
+    tables = [
+        pltpu.make_async_copy(right, right_in, sems.at[0]),
+        pltpu.make_async_copy(seeds_in, seeds, sems.at[1]),
+    ]
     copies = []
     if first:
         copies = [
             pltpu.make_async_copy(
                 weight.at[l, :, pl.ds(n * tile, tile)],
-                tiles.at[l * steps + n],
-                sems.at[1 + l * steps + n],
+                tiles_rest.at[(l - 1) * steps + n],
+                sems.at[2 + (l - 1) * steps + n],
+            )
+            for l in range(1, local_experts)
+            for n in range(steps)
+        ]
+    loads = []
+    if load:
+        down_steps = down_tiles.shape[0] // local_experts
+        down_tile = down_tiles.shape[1]
+        loads = [
+            pltpu.make_async_copy(
+                down_weight.at[l, pl.ds(n * down_tile, down_tile), :],
+                down_tiles.at[l * down_steps + n],
+                sems.at[2 + len(copies) + l * down_steps + n],
             )
             for l in range(local_experts)
-            for n in range(steps)
+            for n in range(down_steps)
         ]
-    for copy in copies:
+    for copy in tables + copies + loads:
         copy.start()
 
     column = iota((width, 2 * slot_count), 0)
     slot = iota((width, 2 * slot_count), 1)
-    owner = place[1] + lax.rem(slot, slot_count) // expert_rows
+    owner = first_expert(local_experts) + lax.rem(slot, slot_count) // expert_rows
     place_of = (column == owner).astype(jnp.bfloat16)
     gate_of = (
         column == owner + jnp.where(slot < slot_count, experts_all, 2 * experts_all)
@@ -131,7 +167,7 @@
         here = (slot_of == wanted) & (lax.rem(lane, expert_rows) // capacity == b)
         gate = jnp.where(here, gate, 0.0).astype(jnp.bfloat16)
         for j in range(parts):
-            at = lax.rem(place[0] - j + parts, parts) * rows
+            at = lax.rem(my_part() - j + parts, parts) * rows
             gate_out[pl.ds(pl.multiple_of(base + at, rows), rows), :] = gate[
                 j * rows : (j + 1) * rows, :
             ]
@@ -140,7 +176,8 @@
         jnp.concatenate(choosers, axis=0), block[...], TN, preferred_element_type=jnp.float32
     ).astype(jnp.bfloat16)
 
-    right_copy.wait()
+    for copy in tables:
+        copy.wait()
     table = right_in[...].astype(jnp.float32)
     for l in range(local_experts):
         mine = slice(l * expert_rows, (l + 1) * expert_rows)
@@ -155,24 +192,23 @@
             jnp.where(iota(table.shape, 0) == seeds[l, 1], table, 0.0), axis=0, keepdims=True
         )
         for n in range(steps):
-            if first:
-                copies[l * steps + n].wait()
+            if first and l > 0:
+                copies[(l - 1) * steps + n].wait()
+            tile_in = tiles_rest[(l - 1) * steps + n] if l > 0 else tiles_first[n]
             up_act = jnp.dot(
-                slots[mine, :model_width],
-                tiles[l * steps + n],
-                preferred_element_type=jnp.float32,
+                slots[mine, :model_width], tile_in, preferred_element_type=jnp.float32
             )
             here = slice(n * tile, (n + 1) * tile)
             up_act = jnp.maximum(up_act + low_rank * right_row[:, here], 0.0)
             hidden[l, :, here] = (up_act * up_act).astype(jnp.bfloat16)
-
-
-def down_kernel(first, parts, cores, pieces_out, place, seeds, *refs):
+    for copy in loads:
+        copy.wait()
+
+
+def down_kernel(parts, cores, pieces_out, *refs):
     pieces = refs[:parts]
-    weight, left, right, gate, own, *rest = refs[parts:]
-    others, rest = rest[: (cores - 1) * pieces_out], rest[(cores - 1) * pieces_out :]
-    *tiles, results, left_in, right_in, sems = rest
-    tiles = tiles[0] if first else weight
+    tiles, left, right, seeds_in, gate, own, *rest = refs[parts:]
+    others, (results, left_in, right_in, seeds, sems) = rest[:-5], rest[-5:]
     local_experts, expert_rows, depth = pieces[0].shape
     steps = tiles.shape[0] // local_experts
     tile = tiles.shape[1]
@@ -182,25 +218,15 @@
     tables = [
         pltpu.make_async_copy(left, left_in, sems.at[0]),
         pltpu.make_async_copy(right, right_in, sems.at[1]),
+        pltpu.make_async_copy(seeds_in, seeds, sems.at[2]),
     ]
-    copies = []
-    if first:
-        copies = [
-            pltpu.make_async_copy(
-                weight.at[l, pl.ds(n * tile, tile), :],
-                tiles.at[l * steps + n],
-                sems.at[2 + l * steps + n],
-            )
-            for l in range(local_experts)
-            for n in range(steps)
-        ]
-    for copy in tables + copies:
+    for copy in tables:
         copy.start()
 
     columns = [slice(None)]
     if parts > 1:
         columns = [
-            pl.ds(pl.multiple_of(lax.rem(place[0] - j + parts, parts) * depth, depth), depth)
+            pl.ds(pl.multiple_of(lax.rem(my_part() - j + parts, parts) * depth, depth), depth)
             for j in range(parts)
         ]
     for copy in tables:
@@ -217,8 +243,6 @@
         )
         chosen = (iota((right.shape[0], expert_rows), 0) == seeds[l, 3]).astype(jnp.bfloat16)
         for n in range(steps):
-            if first:
-                copies[l * steps + n].wait()
             result = sum(
                 lax.dot_general(
                     tiles[l * steps + n, :, at], piece[l], NT, preferred_element_type=jnp.float32
@@ -268,96 +292,92 @@
     expert_rows = cores * capacity
     slot_count = local_experts * expert_rows
     all_tokens = cores * tok_count
-    first_expert = (lax.axis_index("ctx") * cores + lax.axis_index("tp")) * local_experts
-    place = jnp.stack([lax.axis_index("exp"), first_expert]).astype(jnp.int32)
     whole_tiles = hid % LANES == 0
     params = pltpu.CompilerParams(vmem_limit_bytes=VMEM_LIMIT)
-    smem, vmem, hbm = (
-        pl.BlockSpec(memory_space=space) for space in (pltpu.SMEM, pltpu.VMEM, pltpu.HBM)
-    )
+    vmem, hbm = (pl.BlockSpec(memory_space=space) for space in (pltpu.VMEM, pltpu.HBM))
+    up_steps = 3 if hid % (3 * LANES) == 0 else 1
+    up_tiles = (up_steps, model_width, hid // up_steps)
 
     prep = pl.pallas_call(
         functools.partial(prep_kernel, experts_all, parts),
-        out_shape=[jax.ShapeDtypeStruct((rows, packed), jnp.bfloat16)] * parts,
-        in_specs=[smem, hbm, hbm, hbm, hbm],
-        out_specs=[vmem] * parts,
+        out_shape=[jax.ShapeDtypeStruct((rows, packed), jnp.bfloat16)] * parts
+        + [jax.ShapeDtypeStruct(up_tiles, jnp.bfloat16)],
+        in_specs=[hbm] * 5,
+        out_specs=[vmem] * (parts + 1),
         scratch_shapes=[
             pltpu.VMEM((top_count, tok_count), jnp.int32),
             pltpu.VMEM((top_count, tok_count), jnp.float32),
             pltpu.VMEM(tokens.shape, jnp.bfloat16),
             pltpu.VMEM(up_left.shape, jnp.bfloat16),
             pltpu.VMEM((tok_count, width), jnp.bfloat16),
-            pltpu.SemaphoreType.DMA((4,)),
+            pltpu.SemaphoreType.DMA((4 + up_steps,)),
         ],
         compiler_params=params,
         name="pack_tokens",
     )
 
     splits = 2 if rows % 32 == 0 else 1
-    up_steps = 3 if hid % (3 * LANES) == 0 else 1
-    up_tiles = (local_experts * up_steps, model_width, hid // up_steps)
-
-    def up(first):
+    up_rest = ((local_experts - 1) * up_steps,) + up_tiles[1:]
+
+    down_steps = 3 if out_width % 48 == 0 else 1
+    down_tiles = (local_experts * down_steps, out_width // down_steps, hid_all)
+
+    def up(first, load):
         return pl.pallas_call(
             functools.partial(
-                up_kernel, first, experts_all, parts, cores, splits, capacity, factors
+                up_kernel, first, load, experts_all, parts, cores, splits, capacity, factors
             ),
             out_shape=[
                 jax.ShapeDtypeStruct((local_experts, expert_rows, hid), jnp.bfloat16),
                 jax.ShapeDtypeStruct((all_tokens, 2 * slot_count), jnp.bfloat16),
             ]
-            + [jax.ShapeDtypeStruct(up_tiles, jnp.bfloat16)] * first,
-            in_specs=[smem, smem] + [vmem] * (parts * (1 + (cores - 1) * splits)) + [hbm if first else vmem, hbm],
-            out_specs=[vmem] * (2 + first),
+            + [jax.ShapeDtypeStruct(up_rest, jnp.bfloat16)] * first
+            + [jax.ShapeDtypeStruct(down_tiles, jnp.bfloat16)] * load,
+            in_specs=[vmem] * (parts * (1 + (cores - 1) * splits))
+            + [vmem, hbm if first else vmem, hbm, hbm]
+            + [hbm] * load,
+            out_specs=[vmem] * (2 + first + load),
             scratch_shapes=[
                 pltpu.VMEM((all_tokens, packed), jnp.bfloat16),
                 pltpu.VMEM((slot_count, packed), jnp.bfloat16),
                 pltpu.VMEM(up_right.shape, jnp.bfloat16),
-                pltpu.SemaphoreType.DMA((1 + local_experts * up_steps,)),
+                pltpu.SMEM(factor_seeds.shape, jnp.int32),
+                pltpu.SemaphoreType.DMA((2 + (local_experts - 1) * up_steps + down_tiles[0],)),
             ],
             compiler_params=params,
             name="up",
         )
 
     r_splits = 2 if out_width % 64 == 0 else 1
-    down_steps = 3 if out_width % 48 == 0 else 1
-    down_tiles = (local_experts * down_steps, out_width // down_steps, hid_all)
     hidden_parts = parts if whole_tiles else 1
 
-    def down(first):
-        return pl.pallas_call(
-            functools.partial(down_kernel, first, hidden_parts, cores, r_splits),
-            out_shape=[
-                jax.ShapeDtypeStruct((out_width, tok_count), jnp.float32),
-            ]
-            + [jax.ShapeDtypeStruct((out_width // r_splits, tok_count), jnp.bfloat16)]
-            * ((cores - 1) * r_splits)
-            + [jax.ShapeDtypeStruct(down_tiles, jnp.bfloat16)] * first,
-            in_specs=[smem, smem]
-            + [vmem] * hidden_parts
-            + [hbm if first else vmem, hbm, hbm, vmem],
-            out_specs=[vmem] * (1 + (cores - 1) * r_splits + first),
-            scratch_shapes=[
-                pltpu.VMEM((out_width, 2 * slot_count), jnp.bfloat16),
-                pltpu.VMEM(down_left.shape, jnp.bfloat16),
-                pltpu.VMEM(down_right.shape, jnp.bfloat16),
-                pltpu.SemaphoreType.DMA((2 + local_experts * down_steps,)),
-            ],
-            compiler_params=params,
-            name="down",
-        )
-
-    place = in_memory(place, pltpu.SMEM)
-    seeds = in_memory(factor_seeds, pltpu.SMEM)
+    down = pl.pallas_call(
+        functools.partial(down_kernel, hidden_parts, cores, r_splits),
+        out_shape=[jax.ShapeDtypeStruct((out_width, tok_count), jnp.float32)]
+        + [jax.ShapeDtypeStruct((out_width // r_splits, tok_count), jnp.bfloat16)]
+        * ((cores - 1) * r_splits),
+        in_specs=[vmem] * (hidden_parts + 1) + [hbm, hbm, hbm, vmem],
+        out_specs=[vmem] * (1 + (cores - 1) * r_splits),
+        scratch_shapes=[
+            pltpu.VMEM((out_width, 2 * slot_count), jnp.bfloat16),
+            pltpu.VMEM(down_left.shape, jnp.bfloat16),
+            pltpu.VMEM(down_right.shape, jnp.bfloat16),
+            pltpu.SMEM(factor_seeds.shape, jnp.int32),
+            pltpu.SemaphoreType.DMA((3,)),
+        ],
+        compiler_params=params,
+        name="down",
+    )
+
     in_hbm = [
         in_memory(value, pltpu.HBM)
         for value in (
             routes.T, route_gates.T, tokens, up_left, up_weight, up_right,
-            down_weight.transpose(0, 2, 1), down_left, down_right,
+            down_weight.transpose(0, 2, 1), down_left, down_right, factor_seeds,
         )
     ]
-    up_weight, up_right, down_turned, down_left, down_right = in_hbm[4:]
-    pieces = list(prep(place, *in_hbm[:4]))
+    up_weight, up_right, down_turned, down_left, down_right, seeds = in_hbm[4:]
+    *pieces, tiles_first = prep(*in_hbm[:5])
     kept = {}
 
     last = [pieces[0]]
@@ -376,35 +396,42 @@
     def over_exp(value):
         return [shift(value, "exp", j) for j in range(1, parts)]
 
-    def run_up(here, there):
+    def up_only(here, there, load=False):
         blocks = here + [
             there[j][b][i] for b in range(cores - 1) for j in range(parts) for i in range(splits)
         ]
         first = "up" not in kept
-        hidden, gate, *tiles = up(first)(
-            place, seeds, order(blocks[0]), *blocks[1:], up_weight if first else kept["up"], up_right
-        )
+        hidden, gate, *tiles = up(first, load)(
+            order(blocks[0]),
+            *blocks[1:],
+            tiles_first,
+            up_weight if first else kept["up"],
+            up_right,
+            seeds,
+            *([down_turned] if load else []),
+        )
+        if load:
+            kept["down"] = tiles.pop()
         if first:
             kept["up"] = tiles[0]
         last[0] = gate
+        return hidden, gate
+
+    def exchanged(hidden):
         if whole_tiles:
-            return [hidden] + over_exp(hidden), gate
-        return [lax.all_gather(hidden, "exp", axis=2, tiled=True)], gate
+            return [hidden] + over_exp(hidden)
+        return [lax.all_gather(hidden, "exp", axis=2, tiled=True)]
 
     def run_down(hiddens, gate):
-        first = "down" not in kept
-        own, *others = down(first)(
-            place,
-            seeds,
+        own, *others = down(
             *hiddens[:-1],
             order(hiddens[-1]),
-            down_turned if first else kept["down"],
+            kept["down"],
             down_left,
             down_right,
+            seeds,
             gate,
         )
-        if first:
-            kept["down"] = others.pop()
         last[0] = own
         return own, others
 
@@ -445,36 +472,47 @@
     returned = {}
 
     def give_back(k, own, others):
-        total = order(summed(own, [after(others[0], last[0])] + others[1:], *([returned[k - 1]] if k > 2 else [])))
+        total = order(
+            summed(own, [after(others[0], last[0])] + others[1:], *([returned[k - 1]] if k > 2 else []))
+        )
         returned[k] = shift(total, "ctx", -1 if k == 1 else 1)
+
+    def send_direct(earlier):
+        return [shift(after(piece, earlier), "ctx", -1) for piece in pieces[1:]]
 
     arriving = shift(pieces[0], "ctx", 1)
     direct = [shift(piece, "ctx", -1) for piece in pieces[1:]]
-    work = [run_up(pieces, [over_cores(piece) for piece in pieces])]
+    hidden_own, gate_own = up_only(pieces, [over_cores(piece) for piece in pieces], load=True)
     arriving = order(arriving)
     direct = [order(piece) for piece in direct]
-    direct_there = [over_cores(piece) for piece in direct]
+    mine_there = over_cores(arriving)
+    work = [None]
     for k in range(1, chips):
         here = [arriving] + (over_exp(arriving) if k < chips - 1 else direct)
-        there = [over_cores(arriving)]
+        there = [mine_there]
         if k < chips - 1:
             arriving = shift(arriving, "ctx", 1)
         if k == 1:
-            own_sum, own_others = run_down(*work[0])
             arriving = order(arriving)
-        if k < chips - 1:
-            here[1:] = [order(piece) for piece in here[1:]]
-            there += [over_cores(piece) for piece in here[1:]]
-        else:
-            there += direct_there
-        work.append(run_up(here, there))
+        here[1:] = [order(piece) for piece in here[1:]]
+        there += [over_cores(piece) for piece in here[1:]]
+        if k < chips - 2:
+            mine_there = over_cores(arriving)
+            mine_there = [[order(half) for half in halves] for halves in mine_there]
+        hidden, gate = up_only(here, there)
+        work.append((exchanged(hidden), gate))
         if 1 < k < chips - 1:
             arriving = order(arriving)
+            if k == chips - 2:
+                mine_there = over_cores(arriving)
+    hidden_own = after(hidden_own, gate)
+    work[0] = (exchanged(hidden_own), gate_own)
     for k in range(1, chips):
         sums = run_down(*work[k])
         give_back(k, *sums)
         if 1 < k == chips - 2:
             returned[1] = order(returned[1])
+    own_sum, own_others = run_down(*work[0])
     homeward = {1, chips - 1}
     return add(own_sum, back(own_others), *(returned[k] for k in sorted(homeward))).T
 

time: 97.3 us -> 90.8 us (0.933)
  Pallas kernels: 38.5 us -> 32.7 us
    pallas_call x9, Pallas kernels: 37.4 us -> 31.6 us  [the longest x4 15.6 us: run_down(): down(*hiddens[:-1], order(hiddens[-1]), kept['down'], down_left, down_rig...]
  transfers between devices with their start and end apart: 37 -> 37, of which waited for: 20 -> 23; matrix products, arithmetic and copies ran while one was open for 0% -> 0% of each run, Pallas kernels for 36% -> 32%
where the time goes in v3:
time: 90.8 us; the launch traced here: 90.3 us
  waiting for transfers between devices  35.3 us (39%)
  Pallas kernels  32.7 us (36%)
  starting transfers between devices  21.8 us (24%)
    ppermute x37, waiting for transfers between devices, shift(): lax.ppermute(value, axis, [(i, (i + by) % size) for i in range(size)])  35.3 us
    ppermute x37, starting transfers between devices, shift(): lax.ppermute(value, axis, [(i, (i + by) % size) for i in range(size)])  21.8 us
    pallas_call x4, Pallas kernels, run_down(): down(*hiddens[:-1], order(hiddens[-1]), kept['down'], down_left, down_rig...  15.6 us
    pallas_call x4, Pallas kernels, up_only(): up(first, load)  13.4 us
    pallas_call x1, Pallas kernels, on_device(): *pieces, tiles_first = prep(*in_hbm[:5])  2.55 us
  transfers between devices with their start and end apart: 37, of which 23 were waited for; matrix products, arithmetic and copies ran while one was open for 0% of the time, Pallas kernels for 32%

profile of v3, /device:TPU:0, one launch (start us, length us, event | category | flops | bytes accessed | tf_op | source)
XLA Modules:
  0.0 90.3 jit_solution(9834124461317914184)
XLA Ops:
  0.0 2.6 %pack_tokens.1 = (bf16[64,2816]{1,0:T(8,128)(2,1)S(1)}, bf16[64,2816]{1,0:T(8,128)(2,1)S(1)}, bf16[3,2688,256]{2,1,0:T(8,128)(2,1)S(1)}) custom-call(s32[6,128]{1,0:T(8,128)} %bitcast.5, f32[6,128]{1,0:T(8,128)} %bitcast.6, bf16[128,2688]{1,0:T(8,128)(2,1)} %tokens.1, bf16[16,2688]{1,0:T(8,128)(2,1)} %up_left.1, bf16[2,2688,768]{2,1,0:T(8,128)(2,1)} %refs_7_.1), custom_call_target="tpu_custom_call" | custom-call | tf_op jit(solution)/shard_map/pack_tokens/pallas_call | solution.py:380
  2.6 3.1 %collective-permute-start.4 = (bf16[64,2816]{1,0:T(8,128)(2,1)S(1)}, bf16[64,2816]{1,0:T(8,128)(2,1)S(1)}, u32[]{:S(2)}, u32[]{:S(2)}) collective-permute-start(bf16[64,2816]{1,0:T(8,128)(2,1)S(1)} %get-tuple-element.56.refs_0_), channel_id=1, source_target_pairs={{0,4},{4,8},{8,12},{12,0},{1,5},{5,9},{9,13},{13,1},{2,6},{6,10},{... | collective-permute-start | bytes 1081352 | tf_op jit(solution)/shard_map/ppermute | solution.py:18
  5.7 0.5 collective-permute-start
  6.2 2.0 %collective-permute-start.6 = (bf16[64,2816]{1,0:T(8,128)(2,1)S(1)}, bf16[64,2816]{1,0:T(8,128)(2,1)S(1)}, u32[]{:S(2)}, u32[]{:S(2)}) collective-permute-start(bf16[64,2816]{1,0:T(8,128)(2,1)S(1)} %get-tuple-element.57.refs_1_), channel_id=1, source_target_pairs={{0,12},{4,0},{8,4},{12,8},{1,13},{5,1},{9,5},{13,9},{2,14},{6,2},{... | collective-permute-start | bytes 1081352 | tf_op jit(solution)/shard_map/ppermute | solution.py:18
  8.3 0.1 collective-permute-start.3
  8.4 0.5 collective-permute-start.2
  8.9 0.9 collective-permute-done.3.refs_5_
  9.8 0.3 collective-permute-done.2.refs_4_
  10.1 5.2 %up.4 = (bf16[2,128,768]{2,1,0:T(8,128)(2,1)S(1)}, bf16[256,512]{1,0:T(8,128)(2,1)S(1)}, bf16[3,2688,256]{2,1,0:T(8,128)(2,1)S(1)}, bf16[6,448,1536]{2,1,0:T(8,128)(2,1)S(1)}) custom-call(bf16[64,2816]{1,0:T(8,128)(2,1)S(1)} %get-tuple-element.56.refs_0_, bf16[64,2816]{1,0:T(8,128)(2,1)S(1)} %get-tuple-element.57.refs_1_, ...), custom_call_target="tpu_custom_call" | custom-call | tf_op jit(solution)/shard_map/up/pallas_call | solution.py:404
  15.3 1.7 %collective-permute-done.4.refs_0_ = bf16[64,2816]{1,0:T(8,128)(2,1)S(1)} collective-permute-done((bf16[64,2816]{1,0:T(8,128)(2,1)S(1)}, bf16[64,2816]{1,0:T(8,128)(2,1)S(1)}, u32[]{:S(2)}, u32[]{:S(2)}) %collective-permute-start.4) | collective-permute-done | bytes 360480 | tf_op jit(solution)/shard_map/ppermute | solution.py:18
  16.9 1.7 %collective-permute-start.11 = (bf16[64,2816]{1,0:T(8,128)(2,1)S(1)}, bf16[64,2816]{1,0:T(8,128)(2,1)S(1)}, u32[]{:S(2)}, u32[]{:S(2)}) collective-permute-start(bf16[64,2816]{1,0:T(8,128)(2,1)S(1)} %collective-permute-done.4.refs_0_), channel_id=1, source_target_pairs={{0,2},{2,0},{1,3},{3,1},{4,6},{6,4},{5,7},{7,5},{8,10},{10,8},{9,1... | collective-permute-start | bytes 1081352 | tf_op jit(solution)/shard_map/ppermute | solution.py:18
  18.7 5.9 %collective-permute-done.6.refs_1_ = bf16[64,2816]{1,0:T(8,128)(2,1)S(1)} collective-permute-done((bf16[64,2816]{1,0:T(8,128)(2,1)S(1)}, bf16[64,2816]{1,0:T(8,128)(2,1)S(1)}, u32[]{:S(2)}, u32[]{:S(2)}) %collective-permute-start.6) | collective-permute-done | bytes 360480 | tf_op jit(solution)/shard_map/ppermute | solution.py:18
  24.6 0.1 collective-permute-start.13
  24.7 0.5 collective-permute-start.12
  25.2 6.4 %collective-permute-done.5.refs_0_ = bf16[64,2816]{1,0:T(8,128)(2,1)S(1)} collective-permute-done((bf16[64,2816]{1,0:T(8,128)(2,1)S(1)}, bf16[64,2816]{1,0:T(8,128)(2,1)S(1)}, u32[]{:S(2)}, u32[]{:S(2)}) %collective-permute-start.5) | collective-permute-done | bytes 360480 | tf_op jit(solution)/shard_map/ppermute | solution.py:18
  31.6 1.5 %collective-permute-start.8 = (bf16[64,2816]{1,0:T(8,128)(2,1)S(1)}, bf16[64,2816]{1,0:T(8,128)(2,1)S(1)}, u32[]{:S(2)}, u32[]{:S(2)}) collective-permute-start(bf16[64,2816]{1,0:T(8,128)(2,1)S(1)} %collective-permute-done.5.refs_0_), channel_id=1, source_target_pairs={{0,2},{2,0},{1,3},{3,1},{4,6},{6,4},{5,7},{7,5},{8,10},{10,8},{9,1... | collective-permute-start | bytes 1081352 | tf_op jit(solution)/shard_map/ppermute | solution.py:18
  33.2 0.5 collective-permute-start.9
  33.7 0.9 collective-permute-done.10.refs_2_
  34.6 0.1 collective-permute-start.15
  34.7 0.1 collective-permute-done.9.refs_3_
  34.8 0.3 collective-permute-start.14
  35.1 0.9 collective-permute-done.15.refs_5_
  36.0 0.3 collective-permute-done.14.refs_4_
  36.3 2.7 %up.5 = (bf16[2,128,768]{2,1,0:T(8,128)(2,1)S(1)}, bf16[256,512]{1,0:T(8,128)(2,1)S(1)}) custom-call(bf16[64,2816]{1,0:T(8,128)(2,1)S(1)} %collective-permute-done.4.refs_0_, bf16[64,2816]{1,0:T(8,128)(2,1)S(1)} %collective-permute-done.11.refs_1_, bf16[32,2816]{1,0:T(8,128)(2,1)S(1)} %collective-permute-done.12.refs_2_, ...), custom_call_target="tpu_custom_call" | custom-call | tf_op jit(solution)/shard_map/up/pallas_call | solution.py:404
  39.0 0.3 collective-permute-start.17
  39.4 0.3 collective-permute-start.16
  39.6 1.6 %collective-permute-start.24 = (bf16[2,128,768]{2,1,0:T(8,128)(2,1)S(1)}, bf16[2,128,768]{2,1,0:T(8,128)(2,1)S(1)}, u32[]{:S(2)}, u32[]{:S(2)}) collective-permute-start(bf16[2,128,768]{2,1,0:T(8,128)(2,1)S(1)} %get-tuple-element.79.refs_0_), channel_id=1, source_target_pairs={{0,2},{2,0},{1,3},{3,1},{4,6},{6,4},{5,7},{7,5},{8,10},{10,8},{9,1... | collective-permute-start | bytes 1179656 | tf_op jit(solution)/shard_map/ppermute | solution.py:18
  41.2 2.7 %up.6 = (bf16[2,128,768]{2,1,0:T(8,128)(2,1)S(1)}, bf16[256,512]{1,0:T(8,128)(2,1)S(1)}) custom-call(bf16[64,2816]{1,0:T(8,128)(2,1)S(1)} %collective-permute-done.5.refs_0_, bf16[64,2816]{1,0:T(8,128)(2,1)S(1)} %collective-permute-done.8.refs_1_, bf16[32,2816]{1,0:T(8,128)(2,1)S(1)} %collective-permute-done.10.refs_2_, ...), custom_call_target="tpu_custom_call" | custom-call | tf_op jit(solution)/shard_map/up/pallas_call | solution.py:404
  44.0 3.5 %collective-permute-done.7.refs_0_ = bf16[64,2816]{1,0:T(8,128)(2,1)S(1)} collective-permute-done((bf16[64,2816]{1,0:T(8,128)(2,1)S(1)}, bf16[64,2816]{1,0:T(8,128)(2,1)S(1)}, u32[]{:S(2)}, u32[]{:S(2)}) %collective-permute-start.7) | collective-permute-done | bytes 360480 | tf_op jit(solution)/shard_map/ppermute | solution.py:18
  47.5 0.1 collective-permute-start.21
  47.6 0.6 collective-permute-start.28
  48.2 0.2 collective-permute-start.20
  48.4 0.3 collective-permute-start.19
  48.8 0.2 collective-permute-done.21.refs_5_
  49.0 0.1 collective-permute-start.18
  49.1 0.6 collective-permute-done.20.refs_4_
  49.7 0.3 collective-permute-done.19.refs_3_
  49.9 0.5 collective-permute-done.18.refs_2_
  50.4 2.7 %up.7 = (bf16[2,128,768]{2,1,0:T(8,128)(2,1)S(1)}, bf16[256,512]{1,0:T(8,128)(2,1)S(1)}) custom-call(bf16[64,2816]{1,0:T(8,128)(2,1)S(1)} %collective-permute-done.7.refs_0_, bf16[64,2816]{1,0:T(8,128)(2,1)S(1)} %collective-permute-done.6.refs_1_, bf16[32,2816]{1,0:T(8,128)(2,1)S(1)} %collective-permute-done.18.refs_2_, ...), custom_call_target="tpu_custom_call" | custom-call | tf_op jit(solution)/shard_map/up/pallas_call | solution.py:404
  53.1 3.9 %down.4 = (f32[1344,128]{1,0:T(8,128)S(1)}, bf16[672,128]{1,0:T(8,128)(2,1)S(1)}, bf16[672,128]{1,0:T(8,128)(2,1)S(1)}) custom-call(bf16[2,128,768]{2,1,0:T(8,128)(2,1)S(1)} %get-tuple-element.79.refs_0_, bf16[2,128,768]{2,1,0:T(8,128)(2,1)S(1)} %collective-permute-done.24.refs_1_, bf16[6,448,1536]{2,1,0:T(8,128)(2,1)S(1)} %get-tuple-element.81.refs_2_, ...), custom_call_target="tpu_custom_call" | custom-call | tf_op jit(solution)/shard_map/down/pallas_call | solution.py:426
  57.1 0.2 collective-permute-start.25
  57.3 0.4 collective-permute-start.26
  57.6 1.3 %collective-permute-start.23 = (bf16[2,128,768]{2,1,0:T(8,128)(2,1)S(1)}, bf16[2,128,768]{2,1,0:T(8,128)(2,1)S(1)}, u32[]{:S(2)}, u32[]{:S(2)}) collective-permute-start(bf16[2,128,768]{2,1,0:T(8,128)(2,1)S(1)} %get-tuple-element.78.refs_0_), channel_id=1, source_target_pairs={{0,2},{2,0},{1,3},{3,1},{4,6},{6,4},{5,7},{7,5},{8,10},{10,8},{9,1... | collective-permute-start | bytes 1179656 | tf_op jit(solution)/shard_map/ppermute | solution.py:18
  59.0 1.2 %collective-permute-start.27 = (bf16[1344,128]{1,0:T(8,128)(2,1)S(1)}, bf16[1344,128]{1,0:T(8,128)(2,1)S(1)}, u32[]{:S(2)}, u32[]{:S(2)}) collective-permute-start(bf16[1344,128]{1,0:T(8,128)(2,1)S(1)} %add.4), channel_id=1, source_target_pairs={{0,12},{4,0},{8,4},{12,8},{1,13},{5,1},{9,5},{13,9},{2,14},{6,2},{... | collective-permute-start | bytes 1032200 | tf_op jit(solution)/shard_map/ppermute | solution.py:18
  60.2 3.9 %down.5 = (f32[1344,128]{1,0:T(8,128)S(1)}, bf16[672,128]{1,0:T(8,128)(2,1)S(1)}, bf16[672,128]{1,0:T(8,128)(2,1)S(1)}) custom-call(bf16[2,128,768]{2,1,0:T(8,128)(2,1)S(1)} %get-tuple-element.87.refs_0_, bf16[2,128,768]{2,1,0:T(8,128)(2,1)S(1)} %collective-permute-done.28.refs_1_, bf16[6,448,1536]{2,1,0:T(8,128)(2,1)S(1)} %get-tuple-element.81.refs_2_, ...), custom_call_target="tpu_custom_call" | custom-call | tf_op jit(solution)/shard_map/down/pallas_call | solution.py:426
  64.2 0.1 collective-permute-start.29
  64.2 0.5 collective-permute-start.30
  64.7 0.9 collective-permute-done.29.refs_0_
  65.6 0.2 collective-permute-done.30.refs_1_
  65.9 1.1 %collective-permute-start.33 = (bf16[1344,128]{1,0:T(8,128)(2,1)S(1)}, bf16[1344,128]{1,0:T(8,128)(2,1)S(1)}, u32[]{:S(2)}, u32[]{:S(2)}) collective-permute-start(bf16[1344,128]{1,0:T(8,128)(2,1)S(1)} %add.5), channel_id=1, source_target_pairs={{0,4},{4,8},{8,12},{12,0},{1,5},{5,9},{9,13},{13,1},{2,6},{6,10},{... | collective-permute-start | bytes 1032200 | tf_op jit(solution)/shard_map/ppermute | solution.py:18
  67.1 1.2 %collective-permute-start.22 = (bf16[2,128,768]{2,1,0:T(8,128)(2,1)S(1)}, bf16[2,128,768]{2,1,0:T(8,128)(2,1)S(1)}, u32[]{:S(2)}, u32[]{:S(2)}) collective-permute-start(bf16[2,128,768]{2,1,0:T(8,128)(2,1)S(1)} %get-tuple-element.77.refs_0_), channel_id=1, source_target_pairs={{0,2},{2,0},{1,3},{3,1},{4,6},{6,4},{5,7},{7,5},{8,10},{10,8},{9,1... | collective-permute-start | bytes 1179656 | tf_op jit(solution)/shard_map/ppermute | solution.py:18
  68.3 1.1 %collective-permute-done.27.refs_2_ = bf16[1344,128]{1,0:T(8,128)(2,1)S(1)} collective-permute-done((bf16[1344,128]{1,0:T(8,128)(2,1)S(1)}, bf16[1344,128]{1,0:T(8,128)(2,1)S(1)}, u32[]{:S(2)}, u32[]{:S(2)}) %collective-permute-start.27) | collective-permute-done | bytes 344096 | tf_op jit(solution)/shard_map/ppermute | solution.py:18
  69.4 3.9 %down.6 = (f32[1344,128]{1,0:T(8,128)S(1)}, bf16[672,128]{1,0:T(8,128)(2,1)S(1)}, bf16[672,128]{1,0:T(8,128)(2,1)S(1)}) custom-call(bf16[2,128,768]{2,1,0:T(8,128)(2,1)S(1)} %get-tuple-element.78.refs_0_, bf16[2,128,768]{2,1,0:T(8,128)(2,1)S(1)} %collective-permute-done.23.refs_1_, bf16[6,448,1536]{2,1,0:T(8,128)(2,1)S(1)} %get-tuple-element.81.refs_2_, ...), custom_call_target="tpu_custom_call" | custom-call | tf_op jit(solution)/shard_map/down/pallas_call | solution.py:426
  73.3 0.5 collective-permute-start.32
  73.8 0.9 collective-permute-done.31.refs_0_
  74.7 0.2 collective-permute-done.32.refs_1_
  75.0 3.0 %collective-permute-done.33.refs_2_ = bf16[1344,128]{1,0:T(8,128)(2,1)S(1)} collective-permute-done((bf16[1344,128]{1,0:T(8,128)(2,1)S(1)}, bf16[1344,128]{1,0:T(8,128)(2,1)S(1)}, u32[]{:S(2)}, u32[]{:S(2)}) %collective-permute-start.33) | collective-permute-done | bytes 344096 | tf_op jit(solution)/shard_map/ppermute | solution.py:18
  78.0 0.1 add.6
  78.2 3.9 %down.7 = (f32[1344,128]{1,0:T(8,128)S(1)}, bf16[672,128]{1,0:T(8,128)(2,1)S(1)}, bf16[672,128]{1,0:T(8,128)(2,1)S(1)}) custom-call(bf16[2,128,768]{2,1,0:T(8,128)(2,1)S(1)} %get-tuple-element.77.refs_0_, bf16[2,128,768]{2,1,0:T(8,128)(2,1)S(1)} %collective-permute-done.22.refs_1_, bf16[6,448,1536]{2,1,0:T(8,128)(2,1)S(1)} %get-tuple-element.81.refs_2_, ...), custom_call_target="tpu_custom_call" | custom-call | tf_op jit(solution)/shard_map/down/pallas_call | solution.py:426
  82.2 0.5 collective-permute-start.35
  82.7 0.9 collective-permute-done.34.refs_0_
  83.6 0.2 collective-permute-done.35.refs_1_
  83.8 5.6 %collective-permute-done.36.refs_3_ = bf16[1344,128]{1,0:T(8,128)(2,1)S(1)} collective-permute-done((bf16[1344,128]{1,0:T(8,128)(2,1)S(1)}, bf16[1344,128]{1,0:T(8,128)(2,1)S(1)}, u32[]{:S(2)}, u32[]{:S(2)}) %collective-permute-start.36) | collective-permute-done | bytes 344096 | tf_op jit(solution)/shard_map/ppermute | solution.py:18
  89.4 0.9 add.7
  (31 shorter events, 0.7 us)
Async XLA Ops:
  2.6 14.4 %collective-permute-start.4 = (bf16[64,2816]{1,0:T(8,128)(2,1)S(1)}, bf16[64,2816]{1,0:T(8,128)(2,1)S(1)}, u32[]{:S(2)}, u32[]{:S(2)}) collective-permute-start(bf16[64,2816]{1,0:T(8,128)(2,1)S(1)} %get-tuple-element.56.refs_0_), channel_id=1, source_target_pairs={{0,4},{4,8},{8,12},{12,0},{1,5},{5,9},{9,13},{13,1},{2,6},{6,10},{... | collective-permute-start | bytes 1081352 | tf_op jit(solution)/shard_map/ppermute | solution.py:18
  5.7 2.7 %collective-permute-start.1 = (bf16[32,2816]{1,0:T(8,128)(2,1)S(1)}, bf16[32,2816]{1,0:T(8,128)(2,1)S(1)}, u32[]{:S(2)}, u32[]{:S(2)}) collective-permute-start(bf16[32,2816]{1,0:T(8,128)(2,1)S(1)} %get-tuple-element.119), channel_id=1, source_target_pairs={{0,1},{1,0},{2,3},{3,2},{4,5},{5,4},{6,7},{7,6},{8,9},{9,8},{10,11... | collective-permute-start | bytes 540680 | tf_op jit(solution)/shard_map/ppermute | solution.py:18
  5.7 3.2 %collective-permute-start = (bf16[32,2816]{1,0:T(8,128)(2,1)S(1)}, bf16[32,2816]{1,0:T(8,128)(2,1)S(1)}, u32[]{:S(2)}, u32[]{:S(2)}) collective-permute-start(bf16[32,2816]{1,0:T(8,128)(2,1)S(1)} %get-tuple-element.120), channel_id=1, source_target_pairs={{0,1},{1,0},{2,3},{3,2},{4,5},{5,4},{6,7},{7,6},{8,9},{9,8},{10,11... | collective-permute-start | bytes 540680 | tf_op jit(solution)/shard_map/ppermute | solution.py:18
  6.2 18.3 %collective-permute-start.6 = (bf16[64,2816]{1,0:T(8,128)(2,1)S(1)}, bf16[64,2816]{1,0:T(8,128)(2,1)S(1)}, u32[]{:S(2)}, u32[]{:S(2)}) collective-permute-start(bf16[64,2816]{1,0:T(8,128)(2,1)S(1)} %get-tuple-element.57.refs_1_), channel_id=1, source_target_pairs={{0,12},{4,0},{8,4},{12,8},{1,13},{5,1},{9,5},{13,9},{2,14},{6,2},{... | collective-permute-start | bytes 1081352 | tf_op jit(solution)/shard_map/ppermute | solution.py:18
  8.3 1.5 %collective-permute-start.3 = (bf16[32,2816]{1,0:T(8,128)(2,1)S(1)}, bf16[32,2816]{1,0:T(8,128)(2,1)S(1)}, u32[]{:S(2)}, u32[]{:S(2)}) collective-permute-start(bf16[32,2816]{1,0:T(8,128)(2,1)S(1)} %get-tuple-element.117), channel_id=1, source_target_pairs={{0,1},{1,0},{2,3},{3,2},{4,5},{5,4},{6,7},{7,6},{8,9},{9,8},{10,11... | collective-permute-start | bytes 540680 | tf_op jit(solution)/shard_map/ppermute | solution.py:18
  8.4 1.7 %collective-permute-start.2 = (bf16[32,2816]{1,0:T(8,128)(2,1)S(1)}, bf16[32,2816]{1,0:T(8,128)(2,1)S(1)}, u32[]{:S(2)}, u32[]{:S(2)}) collective-permute-start(bf16[32,2816]{1,0:T(8,128)(2,1)S(1)} %get-tuple-element.118), channel_id=1, source_target_pairs={{0,1},{1,0},{2,3},{3,2},{4,5},{5,4},{6,7},{7,6},{8,9},{9,8},{10,11... | collective-permute-start | bytes 540680 | tf_op jit(solution)/shard_map/ppermute | solution.py:18
  16.9 16.1 %collective-permute-start.11 = (bf16[64,2816]{1,0:T(8,128)(2,1)S(1)}, bf16[64,2816]{1,0:T(8,128)(2,1)S(1)}, u32[]{:S(2)}, u32[]{:S(2)}) collective-permute-start(bf16[64,2816]{1,0:T(8,128)(2,1)S(1)} %collective-permute-done.4.refs_0_), channel_id=1, source_target_pairs={{0,2},{2,0},{1,3},{3,1},{4,6},{6,4},{5,7},{7,5},{8,10},{10,8},{9,1... | collective-permute-start | bytes 1081352 | tf_op jit(solution)/shard_map/ppermute | solution.py:18
  18.7 12.9 %collective-permute-start.5 = (bf16[64,2816]{1,0:T(8,128)(2,1)S(1)}, bf16[64,2816]{1,0:T(8,128)(2,1)S(1)}, u32[]{:S(2)}, u32[]{:S(2)}) collective-permute-start(bf16[64,2816]{1,0:T(8,128)(2,1)S(1)} %collective-permute-done.4.refs_0_), channel_id=1, source_target_pairs={{0,4},{4,8},{8,12},{12,0},{1,5},{5,9},{9,13},{13,1},{2,6},{6,10},{... | collective-permute-start | bytes 1081352 | tf_op jit(solution)/shard_map/ppermute | solution.py:18
  24.6 10.5 %collective-permute-start.13 = (bf16[32,2816]{1,0:T(8,128)(2,1)S(1)}, bf16[32,2816]{1,0:T(8,128)(2,1)S(1)}, u32[]{:S(2)}, u32[]{:S(2)}) collective-permute-start(bf16[32,2816]{1,0:T(8,128)(2,1)S(1)} %get-tuple-element.113), channel_id=1, source_target_pairs={{0,1},{1,0},{2,3},{3,2},{4,5},{5,4},{6,7},{7,6},{8,9},{9,8},{10,11... | collective-permute-start | bytes 540680 | tf_op jit(solution)/shard_map/ppermute | solution.py:18
  24.7 10.4 %collective-permute-start.12 = (bf16[32,2816]{1,0:T(8,128)(2,1)S(1)}, bf16[32,2816]{1,0:T(8,128)(2,1)S(1)}, u32[]{:S(2)}, u32[]{:S(2)}) collective-permute-start(bf16[32,2816]{1,0:T(8,128)(2,1)S(1)} %get-tuple-element.114), channel_id=1, source_target_pairs={{0,1},{1,0},{2,3},{3,2},{4,5},{5,4},{6,7},{7,6},{8,9},{9,8},{10,11... | collective-permute-start | bytes 540680 | tf_op jit(solution)/shard_map/ppermute | solution.py:18
  31.6 7.4 %collective-permute-start.8 = (bf16[64,2816]{1,0:T(8,128)(2,1)S(1)}, bf16[64,2816]{1,0:T(8,128)(2,1)S(1)}, u32[]{:S(2)}, u32[]{:S(2)}) collective-permute-start(bf16[64,2816]{1,0:T(8,128)(2,1)S(1)} %collective-permute-done.5.refs_0_), channel_id=1, source_target_pairs={{0,2},{2,0},{1,3},{3,1},{4,6},{6,4},{5,7},{7,5},{8,10},{10,8},{9,1... | collective-permute-start | bytes 1081352 | tf_op jit(solution)/shard_map/ppermute | solution.py:18
  33.1 1.5 %collective-permute-start.10 = (bf16[32,2816]{1,0:T(8,128)(2,1)S(1)}, bf16[32,2816]{1,0:T(8,128)(2,1)S(1)}, u32[]{:S(2)}, u32[]{:S(2)}) collective-permute-start(bf16[32,2816]{1,0:T(8,128)(2,1)S(1)} %get-tuple-element.115), channel_id=1, source_target_pairs={{0,1},{1,0},{2,3},{3,2},{4,5},{5,4},{6,7},{7,6},{8,9},{9,8},{10,11... | collective-permute-start | bytes 540680 | tf_op jit(solution)/shard_map/ppermute | solution.py:18
  33.2 1.7 %collective-permute-start.9 = (bf16[32,2816]{1,0:T(8,128)(2,1)S(1)}, bf16[32,2816]{1,0:T(8,128)(2,1)S(1)}, u32[]{:S(2)}, u32[]{:S(2)}) collective-permute-start(bf16[32,2816]{1,0:T(8,128)(2,1)S(1)} %get-tuple-element.116), channel_id=1, source_target_pairs={{0,1},{1,0},{2,3},{3,2},{4,5},{5,4},{6,7},{7,6},{8,9},{9,8},{10,11... | collective-permute-start | bytes 540680 | tf_op jit(solution)/shard_map/ppermute | solution.py:18
  34.6 1.4 %collective-permute-start.15 = (bf16[32,2816]{1,0:T(8,128)(2,1)S(1)}, bf16[32,2816]{1,0:T(8,128)(2,1)S(1)}, u32[]{:S(2)}, u32[]{:S(2)}) collective-permute-start(bf16[32,2816]{1,0:T(8,128)(2,1)S(1)} %get-tuple-element.111), channel_id=1, source_target_pairs={{0,1},{1,0},{2,3},{3,2},{4,5},{5,4},{6,7},{7,6},{8,9},{9,8},{10,11... | collective-permute-start | bytes 540680 | tf_op jit(solution)/shard_map/ppermute | solution.py:18
  34.8 1.4 %collective-permute-start.14 = (bf16[32,2816]{1,0:T(8,128)(2,1)S(1)}, bf16[32,2816]{1,0:T(8,128)(2,1)S(1)}, u32[]{:S(2)}, u32[]{:S(2)}) collective-permute-start(bf16[32,2816]{1,0:T(8,128)(2,1)S(1)} %get-tuple-element.112), channel_id=1, source_target_pairs={{0,1},{1,0},{2,3},{3,2},{4,5},{5,4},{6,7},{7,6},{8,9},{9,8},{10,11... | collective-permute-start | bytes 540680 | tf_op jit(solution)/shard_map/ppermute | solution.py:18
  35.1 12.4 %collective-permute-start.7 = (bf16[64,2816]{1,0:T(8,128)(2,1)S(1)}, bf16[64,2816]{1,0:T(8,128)(2,1)S(1)}, u32[]{:S(2)}, u32[]{:S(2)}) collective-permute-start(bf16[64,2816]{1,0:T(8,128)(2,1)S(1)} %collective-permute-done.5.refs_0_), channel_id=1, source_target_pairs={{0,4},{4,8},{8,12},{12,0},{1,5},{5,9},{9,13},{13,1},{2,6},{6,10},{... | collective-permute-start | bytes 1081352 | tf_op jit(solution)/shard_map/ppermute | solution.py:18
  39.0 2.2 %collective-permute-start.17 = (bf16[32,2816]{1,0:T(8,128)(2,1)S(1)}, bf16[32,2816]{1,0:T(8,128)(2,1)S(1)}, u32[]{:S(2)}, u32[]{:S(2)}) collective-permute-start(bf16[32,2816]{1,0:T(8,128)(2,1)S(1)} %get-tuple-element.109), channel_id=1, source_target_pairs={{0,1},{1,0},{2,3},{3,2},{4,5},{5,4},{6,7},{7,6},{8,9},{9,8},{10,11... | collective-permute-start | bytes 540680 | tf_op jit(solution)/shard_map/ppermute | solution.py:18
  39.4 1.9 %collective-permute-start.16 = (bf16[32,2816]{1,0:T(8,128)(2,1)S(1)}, bf16[32,2816]{1,0:T(8,128)(2,1)S(1)}, u32[]{:S(2)}, u32[]{:S(2)}) collective-permute-start(bf16[32,2816]{1,0:T(8,128)(2,1)S(1)} %get-tuple-element.110), channel_id=1, source_target_pairs={{0,1},{1,0},{2,3},{3,2},{4,5},{5,4},{6,7},{7,6},{8,9},{9,8},{10,11... | collective-permute-start | bytes 540680 | tf_op jit(solution)/shard_map/ppermute | solution.py:18
  39.6 13.5 %collective-permute-start.24 = (bf16[2,128,768]{2,1,0:T(8,128)(2,1)S(1)}, bf16[2,128,768]{2,1,0:T(8,128)(2,1)S(1)}, u32[]{:S(2)}, u32[]{:S(2)}) collective-permute-start(bf16[2,128,768]{2,1,0:T(8,128)(2,1)S(1)} %get-tuple-element.79.refs_0_), channel_id=1, source_target_pairs={{0,2},{2,0},{1,3},{3,1},{4,6},{6,4},{5,7},{7,5},{8,10},{10,8},{9,1... | collective-permute-start | bytes 1179656 | tf_op jit(solution)/shard_map/ppermute | solution.py:18
  47.5 1.5 %collective-permute-start.21 = (bf16[32,2816]{1,0:T(8,128)(2,1)S(1)}, bf16[32,2816]{1,0:T(8,128)(2,1)S(1)}, u32[]{:S(2)}, u32[]{:S(2)}) collective-permute-start(bf16[32,2816]{1,0:T(8,128)(2,1)S(1)} %get-tuple-element.105), channel_id=1, source_target_pairs={{0,1},{1,0},{2,3},{3,2},{4,5},{5,4},{6,7},{7,6},{8,9},{9,8},{10,11... | collective-permute-start | bytes 540680 | tf_op jit(solution)/shard_map/ppermute | solution.py:18
  47.6 12.7 %collective-permute-start.28 = (bf16[2,128,768]{2,1,0:T(8,128)(2,1)S(1)}, bf16[2,128,768]{2,1,0:T(8,128)(2,1)S(1)}, u32[]{:S(2)}, u32[]{:S(2)}) collective-permute-start(bf16[2,128,768]{2,1,0:T(8,128)(2,1)S(1)} %get-tuple-element.87.refs_0_), channel_id=1, source_target_pairs={{0,2},{2,0},{1,3},{3,1},{4,6},{6,4},{5,7},{7,5},{8,10},{10,8},{9,1... | collective-permute-start | bytes 1179656 | tf_op jit(solution)/shard_map/ppermute | solution.py:18
  48.2 1.5 %collective-permute-start.20 = (bf16[32,2816]{1,0:T(8,128)(2,1)S(1)}, bf16[32,2816]{1,0:T(8,128)(2,1)S(1)}, u32[]{:S(2)}, u32[]{:S(2)}) collective-permute-start(bf16[32,2816]{1,0:T(8,128)(2,1)S(1)} %get-tuple-element.106), channel_id=1, source_target_pairs={{0,1},{1,0},{2,3},{3,2},{4,5},{5,4},{6,7},{7,6},{8,9},{9,8},{10,11... | collective-permute-start | bytes 540680 | tf_op jit(solution)/shard_map/ppermute | solution.py:18
  48.4 1.5 %collective-permute-start.19 = (bf16[32,2816]{1,0:T(8,128)(2,1)S(1)}, bf16[32,2816]{1,0:T(8,128)(2,1)S(1)}, u32[]{:S(2)}, u32[]{:S(2)}) collective-permute-start(bf16[32,2816]{1,0:T(8,128)(2,1)S(1)} %get-tuple-element.107), channel_id=1, source_target_pairs={{0,1},{1,0},{2,3},{3,2},{4,5},{5,4},{6,7},{7,6},{8,9},{9,8},{10,11... | collective-permute-start | bytes 540680 | tf_op jit(solution)/shard_map/ppermute | solution.py:18
  49.0 1.4 %collective-permute-start.18 = (bf16[32,2816]{1,0:T(8,128)(2,1)S(1)}, bf16[32,2816]{1,0:T(8,128)(2,1)S(1)}, u32[]{:S(2)}, u32[]{:S(2)}) collective-permute-start(bf16[32,2816]{1,0:T(8,128)(2,1)S(1)} %get-tuple-element.108), channel_id=1, source_target_pairs={{0,1},{1,0},{2,3},{3,2},{4,5},{5,4},{6,7},{7,6},{8,9},{9,8},{10,11... | collective-permute-start | bytes 540680 | tf_op jit(solution)/shard_map/ppermute | solution.py:18
  57.1 1.9 %collective-permute-start.25 = (bf16[672,128]{1,0:T(8,128)(2,1)S(1)}, bf16[672,128]{1,0:T(8,128)(2,1)S(1)}, u32[]{:S(2)}, u32[]{:S(2)}) collective-permute-start(bf16[672,128]{1,0:T(8,128)(2,1)S(1)} %get-tuple-element.84), channel_id=1, source_target_pairs={{0,1},{1,0},{2,3},{3,2},{4,5},{5,4},{6,7},{7,6},{8,9},{9,8},{10,11... | collective-permute-start | bytes 516104 | tf_op jit(solution)/shard_map/ppermute | solution.py:18
  57.3 1.7 %collective-permute-start.26 = (bf16[672,128]{1,0:T(8,128)(2,1)S(1)}, bf16[672,128]{1,0:T(8,128)(2,1)S(1)}, u32[]{:S(2)}, u32[]{:S(2)}) collective-permute-start(bf16[672,128]{1,0:T(8,128)(2,1)S(1)} %get-tuple-element.85), channel_id=1, source_target_pairs={{0,1},{1,0},{2,3},{3,2},{4,5},{5,4},{6,7},{7,6},{8,9},{9,8},{10,11... | collective-permute-start | bytes 516104 | tf_op jit(solution)/shard_map/ppermute | solution.py:18
  57.6 11.7 %collective-permute-start.23 = (bf16[2,128,768]{2,1,0:T(8,128)(2,1)S(1)}, bf16[2,128,768]{2,1,0:T(8,128)(2,1)S(1)}, u32[]{:S(2)}, u32[]{:S(2)}) collective-permute-start(bf16[2,128,768]{2,1,0:T(8,128)(2,1)S(1)} %get-tuple-element.78.refs_0_), channel_id=1, source_target_pairs={{0,2},{2,0},{1,3},{3,1},{4,6},{6,4},{5,7},{7,5},{8,10},{10,8},{9,1... | collective-permute-start | bytes 1179656 | tf_op jit(solution)/shard_map/ppermute | solution.py:18
  59.0 10.3 %collective-permute-start.27 = (bf16[1344,128]{1,0:T(8,128)(2,1)S(1)}, bf16[1344,128]{1,0:T(8,128)(2,1)S(1)}, u32[]{:S(2)}, u32[]{:S(2)}) collective-permute-start(bf16[1344,128]{1,0:T(8,128)(2,1)S(1)} %add.4), channel_id=1, source_target_pairs={{0,12},{4,0},{8,4},{12,8},{1,13},{5,1},{9,5},{13,9},{2,14},{6,2},{... | collective-permute-start | bytes 1032200 | tf_op jit(solution)/shard_map/ppermute | solution.py:18
  64.2 1.5 %collective-permute-start.29 = (bf16[672,128]{1,0:T(8,128)(2,1)S(1)}, bf16[672,128]{1,0:T(8,128)(2,1)S(1)}, u32[]{:S(2)}, u32[]{:S(2)}) collective-permute-start(bf16[672,128]{1,0:T(8,128)(2,1)S(1)} %get-tuple-element.91), channel_id=1, source_target_pairs={{0,1},{1,0},{2,3},{3,2},{4,5},{5,4},{6,7},{7,6},{8,9},{9,8},{10,11... | collective-permute-start | bytes 516104 | tf_op jit(solution)/shard_map/ppermute | solution.py:18
  64.2 1.6 %collective-permute-start.30 = (bf16[672,128]{1,0:T(8,128)(2,1)S(1)}, bf16[672,128]{1,0:T(8,128)(2,1)S(1)}, u32[]{:S(2)}, u32[]{:S(2)}) collective-permute-start(bf16[672,128]{1,0:T(8,128)(2,1)S(1)} %get-tuple-element.92), channel_id=1, source_target_pairs={{0,1},{1,0},{2,3},{3,2},{4,5},{5,4},{6,7},{7,6},{8,9},{9,8},{10,11... | collective-permute-start | bytes 516104 | tf_op jit(solution)/shard_map/ppermute | solution.py:18
  65.9 12.1 %collective-permute-start.33 = (bf16[1344,128]{1,0:T(8,128)(2,1)S(1)}, bf16[1344,128]{1,0:T(8,128)(2,1)S(1)}, u32[]{:S(2)}, u32[]{:S(2)}) collective-permute-start(bf16[1344,128]{1,0:T(8,128)(2,1)S(1)} %add.5), channel_id=1, source_target_pairs={{0,4},{4,8},{8,12},{12,0},{1,5},{5,9},{9,13},{13,1},{2,6},{6,10},{... | collective-permute-start | bytes 1032200 | tf_op jit(solution)/shard_map/ppermute | solution.py:18
  67.1 11.1 %collective-permute-start.22 = (bf16[2,128,768]{2,1,0:T(8,128)(2,1)S(1)}, bf16[2,128,768]{2,1,0:T(8,128)(2,1)S(1)}, u32[]{:S(2)}, u32[]{:S(2)}) collective-permute-start(bf16[2,128,768]{2,1,0:T(8,128)(2,1)S(1)} %get-tuple-element.77.refs_0_), channel_id=1, source_target_pairs={{0,2},{2,0},{1,3},{3,1},{4,6},{6,4},{5,7},{7,5},{8,10},{10,8},{9,1... | collective-permute-start | bytes 1179656 | tf_op jit(solution)/shard_map/ppermute | solution.py:18
  73.3 1.5 %collective-permute-start.31 = (bf16[672,128]{1,0:T(8,128)(2,1)S(1)}, bf16[672,128]{1,0:T(8,128)(2,1)S(1)}, u32[]{:S(2)}, u32[]{:S(2)}) collective-permute-start(bf16[672,128]{1,0:T(8,128)(2,1)S(1)} %get-tuple-element.98), channel_id=1, source_target_pairs={{0,1},{1,0},{2,3},{3,2},{4,5},{5,4},{6,7},{7,6},{8,9},{9,8},{10,11... | collective-permute-start | bytes 516104 | tf_op jit(solution)/shard_map/ppermute | solution.py:18
  73.3 1.6 %collective-permute-start.32 = (bf16[672,128]{1,0:T(8,128)(2,1)S(1)}, bf16[672,128]{1,0:T(8,128)(2,1)S(1)}, u32[]{:S(2)}, u32[]{:S(2)}) collective-permute-start(bf16[672,128]{1,0:T(8,128)(2,1)S(1)} %get-tuple-element.99), channel_id=1, source_target_pairs={{0,1},{1,0},{2,3},{3,2},{4,5},{5,4},{6,7},{7,6},{8,9},{9,8},{10,11... | collective-permute-start | bytes 516104 | tf_op jit(solution)/shard_map/ppermute | solution.py:18
  78.1 11.3 %collective-permute-start.36 = (bf16[1344,128]{1,0:T(8,128)(2,1)S(1)}, bf16[1344,128]{1,0:T(8,128)(2,1)S(1)}, u32[]{:S(2)}, u32[]{:S(2)}) collective-permute-start(bf16[1344,128]{1,0:T(8,128)(2,1)S(1)} %add.6), channel_id=1, source_target_pairs={{0,4},{4,8},{8,12},{12,0},{1,5},{5,9},{9,13},{13,1},{2,6},{6,10},{... | collective-permute-start | bytes 1032200 | tf_op jit(solution)/shard_map/ppermute | solution.py:18
  82.1 1.5 %collective-permute-start.34 = (bf16[672,128]{1,0:T(8,128)(2,1)S(1)}, bf16[672,128]{1,0:T(8,128)(2,1)S(1)}, u32[]{:S(2)}, u32[]{:S(2)}) collective-permute-start(bf16[672,128]{1,0:T(8,128)(2,1)S(1)} %get-tuple-element.103), channel_id=1, source_target_pairs={{0,1},{1,0},{2,3},{3,2},{4,5},{5,4},{6,7},{7,6},{8,9},{9,8},{10,11... | collective-permute-start | bytes 516104 | tf_op jit(solution)/shard_map/ppermute | solution.py:18
  82.2 1.6 %collective-permute-start.35 = (bf16[672,128]{1,0:T(8,128)(2,1)S(1)}, bf16[672,128]{1,0:T(8,128)(2,1)S(1)}, u32[]{:S(2)}, u32[]{:S(2)}) collective-permute-start(bf16[672,128]{1,0:T(8,128)(2,1)S(1)} %get-tuple-element.104), channel_id=1, source_target_pairs={{0,1},{1,0},{2,3},{3,2},{4,5},{5,4},{6,7},{7,6},{8,9},{9,8},{10,11... | collective-permute-start | bytes 516104 | tf_op jit(solution)/shard_map/ppermute | solution.py:18

commit v4 on v3

--- a/solution.py
+++ b/solution.py
@@ -62,7 +62,7 @@
     line = iota((width, count), 0)
     expert = lax.rem(line, experts_all)
     after_it = (iota((count, count), 0) < iota((count, count), 1)).astype(jnp.bfloat16)
-    row = iota((width, factors), 0) - 3 * experts_all
+    row = iota((width, factors), 0) - 2 * experts_all
     pick = (row >= 0) & (row < 2 * factors) & (lax.rem(row, factors) == iota((width, factors), 1))
     for copy in copies[:2]:
         copy.wait()
@@ -82,11 +82,9 @@
     ).astype(jnp.bfloat16)
     copies[3].wait()
     low_rank = lax.dot_general(left, rows_in[...], NT, preferred_element_type=jnp.float32)
-    value = jnp.where(line < 3 * experts_all, gate, low_rank)
+    value = jnp.where(line < 2 * experts_all, gate, low_rank)
     high = value.astype(jnp.bfloat16).astype(jnp.float32)
-    is_low = ((line >= 2 * experts_all) & (line < 3 * experts_all)) | (
-        line >= 3 * experts_all + factors
-    )
+    is_low = line >= 2 * experts_all + factors
     value = jnp.where(is_low, value - high, high)
     info[...] = jnp.where(line < experts_all, slot, value).T.astype(jnp.bfloat16)
     for j, piece in enumerate(pieces):
@@ -97,15 +95,13 @@
         copy.wait()
 
 
-def up_kernel(first, load, experts_all, parts, cores, splits, capacity, factors, *refs):
-    count = parts * (1 + (cores - 1) * splits)
+def up_kernel(first, load, count, rows, experts_all, parts, cores, capacity, factors, *refs):
     pieces = refs[:count]
     tiles_first, weight, right, seeds_in, *rest = refs[count:-5]
     down_weight = rest.pop(0) if load else None
     hidden, gate_out, *tiles_rest = rest
     down_tiles = tiles_rest.pop() if load else None
     block, slots, right_in, seeds, sems = refs[-5:]
-    rows = pieces[0].shape[0]
     tok_count = rows * parts
     tiles_rest = tiles_rest[0] if first else weight
     local_experts, _, hid = hidden.shape
@@ -145,14 +141,12 @@
     for copy in tables + copies + loads:
         copy.start()
 
-    column = iota((width, 2 * slot_count), 0)
-    slot = iota((width, 2 * slot_count), 1)
-    owner = first_expert(local_experts) + lax.rem(slot, slot_count) // expert_rows
+    column = iota((width, slot_count), 0)
+    slot = iota((width, slot_count), 1)
+    owner = first_expert(local_experts) + slot // expert_rows
     place_of = (column == owner).astype(jnp.bfloat16)
-    gate_of = (
-        column == owner + jnp.where(slot < slot_count, experts_all, 2 * experts_all)
-    ).astype(jnp.bfloat16)
-    lane = iota((tok_count, 2 * slot_count), 1)
+    gate_of = (column == owner + experts_all).astype(jnp.bfloat16)
+    lane = iota((tok_count, slot_count), 1)
     wanted = lax.rem(lane, capacity).astype(jnp.float32)
     base = 0
     for piece in pieces:
@@ -171,7 +165,7 @@
             gate_out[pl.ds(pl.multiple_of(base + at, rows), rows), :] = gate[
                 j * rows : (j + 1) * rows, :
             ]
-        choosers.append(here[:, :slot_count].astype(jnp.bfloat16))
+        choosers.append(here.astype(jnp.bfloat16))
     slots[...] = lax.dot_general(
         jnp.concatenate(choosers, axis=0), block[...], TN, preferred_element_type=jnp.float32
     ).astype(jnp.bfloat16)
@@ -182,7 +176,7 @@
     for l in range(local_experts):
         mine = slice(l * expert_rows, (l + 1) * expert_rows)
         extra = slots[mine, model_width:].astype(jnp.float32)
-        at = iota(extra.shape, 1) - 3 * experts_all
+        at = iota(extra.shape, 1) - 2 * experts_all
         low_rank = jnp.sum(
             jnp.where((at == seeds[l, 0]) | (at == factors + seeds[l, 0]), extra, 0.0),
             axis=1,
@@ -254,9 +248,7 @@
                 right_in[:, here], chosen, TN, preferred_element_type=jnp.float32
             )
             result = (result + right_column * rank).astype(jnp.bfloat16)
-            for half in range(2):
-                at = half * slot_count + l * expert_rows
-                results[here, at : at + expert_rows] = result
+            results[here, l * expert_rows : (l + 1) * expert_rows] = result
     summed = lax.dot_general(results[...], gate[...], NT, preferred_element_type=jnp.float32)
     own[...] = summed[:, :tok_count]
     step = summed.shape[0] // pieces_out
@@ -287,7 +279,7 @@
     factors = up_left.shape[0]
     capacity = 4 * tok_count * top_count // (3 * experts_all)
     rows = tok_count // parts
-    width = -(-(3 * experts_all + 2 * factors) // LANES) * LANES
+    width = -(-2 * (experts_all + factors) // LANES) * LANES
     packed = model_width + width
     expert_rows = cores * capacity
     slot_count = local_experts * expert_rows
@@ -322,18 +314,18 @@
     down_steps = 3 if out_width % 48 == 0 else 1
     down_tiles = (local_experts * down_steps, out_width // down_steps, hid_all)
 
-    def up(first, load):
+    def up(first, load, count):
         return pl.pallas_call(
             functools.partial(
-                up_kernel, first, load, experts_all, parts, cores, splits, capacity, factors
+                up_kernel, first, load, count, rows, experts_all, parts, cores, capacity, factors
             ),
             out_shape=[
                 jax.ShapeDtypeStruct((local_experts, expert_rows, hid), jnp.bfloat16),
-                jax.ShapeDtypeStruct((all_tokens, 2 * slot_count), jnp.bfloat16),
+                jax.ShapeDtypeStruct((all_tokens, slot_count), jnp.bfloat16),
             ]
             + [jax.ShapeDtypeStruct(up_rest, jnp.bfloat16)] * first
             + [jax.ShapeDtypeStruct(down_tiles, jnp.bfloat16)] * load,
-            in_specs=[vmem] * (parts * (1 + (cores - 1) * splits))
+            in_specs=[vmem] * count
             + [vmem, hbm if first else vmem, hbm, hbm]
             + [hbm] * load,
             out_specs=[vmem] * (2 + first + load),
@@ -359,7 +351,7 @@
         in_specs=[vmem] * (hidden_parts + 1) + [hbm, hbm, hbm, vmem],
         out_specs=[vmem] * (1 + (cores - 1) * r_splits),
         scratch_shapes=[
-            pltpu.VMEM((out_width, 2 * slot_count), jnp.bfloat16),
+            pltpu.VMEM((out_width, slot_count), jnp.bfloat16),
             pltpu.VMEM(down_left.shape, jnp.bfloat16),
             pltpu.VMEM(down_right.shape, jnp.bfloat16),
             pltpu.SMEM(factor_seeds.shape, jnp.int32),
@@ -386,22 +378,22 @@
         last[0] = after(value, last[0])
         return last[0]
 
-    def over_cores(piece):
+    def halves_of(piece):
         step = rows // splits
-        return [
-            [shift(piece[i * step : (i + 1) * step], "tp", b) for i in range(splits)]
-            for b in range(1, cores)
-        ]
+        return [piece[i * step : (i + 1) * step] for i in range(splits)]
+
+    def over_cores(halves):
+        return [[shift(half, "tp", b) for half in halves] for b in range(1, cores)]
 
     def over_exp(value):
         return [shift(value, "exp", j) for j in range(1, parts)]
 
     def up_only(here, there, load=False):
-        blocks = here + [
-            there[j][b][i] for b in range(cores - 1) for j in range(parts) for i in range(splits)
-        ]
+        blocks = [half for halves in here for half in halves]
+        for b in range(cores - 1):
+            blocks += [half for others in there for half in others[b]]
         first = "up" not in kept
-        hidden, gate, *tiles = up(first, load)(
+        hidden, gate, *tiles = up(first, load, len(blocks))(
             order(blocks[0]),
             *blocks[1:],
             tiles_first,
@@ -481,30 +473,44 @@
         return [shift(after(piece, earlier), "ctx", -1) for piece in pieces[1:]]
 
     arriving = shift(pieces[0], "ctx", 1)
-    direct = [shift(piece, "ctx", -1) for piece in pieces[1:]]
-    hidden_own, gate_own = up_only(pieces, [over_cores(piece) for piece in pieces], load=True)
+    direct = [halves_of(piece) for piece in pieces[1:]]
+    direct = [[shift(halves[0], "ctx", -1)] + halves[1:] for halves in direct]
+    hidden_own, gate_own = up_only(
+        [[piece] for piece in pieces],
+        [over_cores(halves_of(piece)) for piece in pieces],
+        load=True,
+    )
     arriving = order(arriving)
-    direct = [order(piece) for piece in direct]
-    mine_there = over_cores(arriving)
+    direct = [[order(halves[0])] + halves[1:] for halves in direct]
+    mine_there = over_cores(halves_of(arriving))
     work = [None]
     for k in range(1, chips):
-        here = [arriving] + (over_exp(arriving) if k < chips - 1 else direct)
+        if k == max(1, chips - 2):
+            direct = [
+                halves[:1] + [shift(after(half, arriving), "ctx", -1) for half in halves[1:]]
+                for halves in direct
+            ]
+        if k < chips - 1:
+            here = [[piece] for piece in [arriving] + over_exp(arriving)]
+        else:
+            here = [[arriving]] + direct
         there = [mine_there]
         if k < chips - 1:
             arriving = shift(arriving, "ctx", 1)
         if k == 1:
             arriving = order(arriving)
-        here[1:] = [order(piece) for piece in here[1:]]
-        there += [over_cores(piece) for piece in here[1:]]
+        here[1:] = [halves[:-1] + [order(halves[-1])] for halves in here[1:]]
+        there += [
+            over_cores(halves_of(halves[0]) if len(halves) == 1 else halves) for halves in here[1:]
+        ]
         if k < chips - 2:
-            mine_there = over_cores(arriving)
-            mine_there = [[order(half) for half in halves] for halves in mine_there]
+            mine_there = over_cores(halves_of(arriving))
         hidden, gate = up_only(here, there)
         work.append((exchanged(hidden), gate))
         if 1 < k < chips - 1:
             arriving = order(arriving)
             if k == chips - 2:
-                mine_there = over_cores(arriving)
+                mine_there = over_cores(halves_of(arriving))
     hidden_own = after(hidden_own, gate)
     work[0] = (exchanged(hidden_own), gate_own)
     for k in range(1, chips):

time: 90.8 us -> 88.1 us (0.970)
  waiting for transfers between devices: 35.3 us -> 32.5 us
  starting transfers between devices: 21.8 us -> 22.8 us
    ppermute x37 -> x38, waiting for transfers between devices: 35.3 us -> 32.5 us  [shift(): lax.ppermute(value, axis, [(i, (i + by) % size) for i in range(size)])]
    ppermute x37 -> x38, starting transfers between devices: 21.8 us -> 22.8 us  [shift(): lax.ppermute(value, axis, [(i, (i + by) % size) for i in range(size)])]
  transfers between devices with their start and end apart: 37 -> 38, of which waited for: 23 -> 21; matrix products, arithmetic and copies ran while one was open for 0% -> 0% of each run, Pallas kernels for 32% -> 32%
where the time goes in v4:
time: 88.1 us; the launch traced here: 87.5 us
  waiting for transfers between devices  32.5 us (37%)
  Pallas kernels  31.8 us (36%)
  starting transfers between devices  22.8 us (26%)
    ppermute x38, waiting for transfers between devices, shift(): lax.ppermute(value, axis, [(i, (i + by) % size) for i in range(size)])  32.5 us
    ppermute x38, starting transfers between devices, shift(): lax.ppermute(value, axis, [(i, (i + by) % size) for i in range(size)])  22.8 us
    pallas_call x4, Pallas kernels, run_down(): down(*hiddens[:-1], order(hiddens[-1]), kept['down'], down_left, down_rig...  14.9 us
    pallas_call x4, Pallas kernels, up_only(): up(first, load, len(blocks))  13.2 us
    pallas_call x1, Pallas kernels, on_device(): *pieces, tiles_first = prep(*in_hbm[:5])  2.55 us
  transfers between devices with their start and end apart: 38, of which 21 were waited for; matrix products, arithmetic and copies ran while one was open for 0% of the time, Pallas kernels for 32%

profile of v4, /device:TPU:0, one launch (start us, length us, event | category | flops | bytes accessed | tf_op | source)
XLA Modules:
  0.0 87.5 jit_solution(12228686289835408447)
XLA Ops:
  0.0 2.6 %pack_tokens.1 = (bf16[64,2816]{1,0:T(8,128)(2,1)S(1)}, bf16[64,2816]{1,0:T(8,128)(2,1)S(1)}, bf16[3,2688,256]{2,1,0:T(8,128)(2,1)S(1)}) custom-call(s32[6,128]{1,0:T(8,128)} %bitcast.5, f32[6,128]{1,0:T(8,128)} %bitcast.6, bf16[128,2688]{1,0:T(8,128)(2,1)} %tokens.1, bf16[16,2688]{1,0:T(8,128)(2,1)} %up_left.1, bf16[2,2688,768]{2,1,0:T(8,128)(2,1)} %refs_7_.1), custom_call_target="tpu_custom_call" | custom-call | tf_op jit(solution)/shard_map/pack_tokens/pallas_call | solution.py:372
  2.6 3.1 %collective-permute-start.4 = (bf16[64,2816]{1,0:T(8,128)(2,1)S(1)}, bf16[64,2816]{1,0:T(8,128)(2,1)S(1)}, u32[]{:S(2)}, u32[]{:S(2)}) collective-permute-start(bf16[64,2816]{1,0:T(8,128)(2,1)S(1)} %get-tuple-element.55.refs_0_), channel_id=1, source_target_pairs={{0,4},{4,8},{8,12},{12,0},{1,5},{5,9},{9,13},{13,1},{2,6},{6,10},{... | collective-permute-start | bytes 1081352 | tf_op jit(solution)/shard_map/ppermute | solution.py:18
  5.7 0.5 collective-permute-start.1
  6.3 0.1 collective-permute-start.2
  6.4 0.4 collective-permute-start.3
  6.8 0.3 collective-permute-done.refs_2_
  7.1 2.0 %collective-permute-start.6 = (bf16[32,2816]{1,0:T(8,128)(2,1)S(1)}, bf16[32,2816]{1,0:T(8,128)(2,1)S(1)}, u32[]{:S(2)}, u32[]{:S(2)}) collective-permute-start(bf16[32,2816]{1,0:T(8,128)(2,1)S(1)} %get-tuple-element.114), channel_id=1, source_target_pairs={{0,12},{4,0},{8,4},{12,8},{1,13},{5,1},{9,5},{13,9},{2,14},{6,2},{... | collective-permute-start | bytes 540680 | tf_op jit(solution)/shard_map/ppermute | solution.py:18
  9.2 5.2 %up.4 = (bf16[2,128,768]{2,1,0:T(8,128)(2,1)S(1)}, bf16[256,256]{1,0:T(8,128)(2,1)S(1)}, bf16[3,2688,256]{2,1,0:T(8,128)(2,1)S(1)}, bf16[6,448,1536]{2,1,0:T(8,128)(2,1)S(1)}) custom-call(bf16[64,2816]{1,0:T(8,128)(2,1)S(1)} %get-tuple-element.55.refs_0_, bf16[64,2816]{1,0:T(8,128)(2,1)S(1)} %get-tuple-element.56.refs_1_, ...), custom_call_target="tpu_custom_call" | custom-call | tf_op jit(solution)/shard_map/up/pallas_call | solution.py:396
  14.4 2.5 %collective-permute-done.4.refs_0_ = bf16[64,2816]{1,0:T(8,128)(2,1)S(1)} collective-permute-done((bf16[64,2816]{1,0:T(8,128)(2,1)S(1)}, bf16[64,2816]{1,0:T(8,128)(2,1)S(1)}, u32[]{:S(2)}, u32[]{:S(2)}) %collective-permute-start.4) | collective-permute-done | bytes 360480 | tf_op jit(solution)/shard_map/ppermute | solution.py:18
  16.9 1.7 %collective-permute-start.9 = (bf16[64,2816]{1,0:T(8,128)(2,1)S(1)}, bf16[64,2816]{1,0:T(8,128)(2,1)S(1)}, u32[]{:S(2)}, u32[]{:S(2)}) collective-permute-start(bf16[64,2816]{1,0:T(8,128)(2,1)S(1)} %collective-permute-done.4.refs_0_), channel_id=1, source_target_pairs={{0,2},{2,0},{1,3},{3,1},{4,6},{6,4},{5,7},{7,5},{8,10},{10,8},{9,1... | collective-permute-start | bytes 1081352 | tf_op jit(solution)/shard_map/ppermute | solution.py:18
  18.7 1.3 %collective-permute-done.6.refs_1_ = bf16[32,2816]{1,0:T(8,128)(2,1)S(1)} collective-permute-done((bf16[32,2816]{1,0:T(8,128)(2,1)S(1)}, bf16[32,2816]{1,0:T(8,128)(2,1)S(1)}, u32[]{:S(2)}, u32[]{:S(2)}) %collective-permute-start.6) | collective-permute-done | bytes 180256 | tf_op jit(solution)/shard_map/ppermute | solution.py:18
  20.0 0.1 collective-permute-start.10
  20.1 0.5 collective-permute-start.11
  20.6 7.1 %collective-permute-done.5.refs_0_ = bf16[64,2816]{1,0:T(8,128)(2,1)S(1)} collective-permute-done((bf16[64,2816]{1,0:T(8,128)(2,1)S(1)}, bf16[64,2816]{1,0:T(8,128)(2,1)S(1)}, u32[]{:S(2)}, u32[]{:S(2)}) %collective-permute-start.5) | collective-permute-done | bytes 360480 | tf_op jit(solution)/shard_map/ppermute | solution.py:18
  27.7 1.5 %collective-permute-start.8 = (bf16[64,2816]{1,0:T(8,128)(2,1)S(1)}, bf16[64,2816]{1,0:T(8,128)(2,1)S(1)}, u32[]{:S(2)}, u32[]{:S(2)}) collective-permute-start(bf16[64,2816]{1,0:T(8,128)(2,1)S(1)} %collective-permute-done.5.refs_0_), channel_id=1, source_target_pairs={{0,2},{2,0},{1,3},{3,1},{4,6},{6,4},{5,7},{7,5},{8,10},{10,8},{9,1... | collective-permute-start | bytes 1081352 | tf_op jit(solution)/shard_map/ppermute | solution.py:18
  29.2 0.1 collective-permute-start.12
  29.3 0.5 collective-permute-start.13
  29.9 0.1 collective-permute-start.14
  30.1 0.6 collective-permute-done.12.refs_4_
  30.7 0.1 collective-permute-start.15
  30.9 0.1 collective-permute-done.13.refs_5_
  31.0 2.7 %up.5 = (bf16[2,128,768]{2,1,0:T(8,128)(2,1)S(1)}, bf16[256,256]{1,0:T(8,128)(2,1)S(1)}) custom-call(bf16[64,2816]{1,0:T(8,128)(2,1)S(1)} %collective-permute-done.4.refs_0_, bf16[64,2816]{1,0:T(8,128)(2,1)S(1)} %collective-permute-done.9.refs_1_, bf16[32,2816]{1,0:T(8,128)(2,1)S(1)} %collective-permute-done.10.refs_2_, ...), custom_call_target="tpu_custom_call" | custom-call | tf_op jit(solution)/shard_map/up/pallas_call | solution.py:396
  33.7 2.1 %collective-permute-done.8.refs_1_ = bf16[64,2816]{1,0:T(8,128)(2,1)S(1)} collective-permute-done((bf16[64,2816]{1,0:T(8,128)(2,1)S(1)}, bf16[64,2816]{1,0:T(8,128)(2,1)S(1)}, u32[]{:S(2)}, u32[]{:S(2)}) %collective-permute-start.8) | collective-permute-done | bytes 360480 | tf_op jit(solution)/shard_map/ppermute | solution.py:18
  35.8 0.1 collective-permute-start.16
  35.8 0.5 collective-permute-start.17
  36.3 0.1 collective-permute-start.21
  36.4 1.6 %collective-permute-start.18 = (bf16[32,2816]{1,0:T(8,128)(2,1)S(1)}, bf16[32,2816]{1,0:T(8,128)(2,1)S(1)}, u32[]{:S(2)}, u32[]{:S(2)}) collective-permute-start(bf16[32,2816]{1,0:T(8,128)(2,1)S(1)} %get-tuple-element.71), channel_id=1, source_target_pairs={{0,12},{4,0},{8,4},{12,8},{1,13},{5,1},{9,5},{13,9},{2,14},{6,2},{... | collective-permute-start | bytes 540680 | tf_op jit(solution)/shard_map/ppermute | solution.py:18
  38.0 1.5 %collective-permute-start.25 = (bf16[2,128,768]{2,1,0:T(8,128)(2,1)S(1)}, bf16[2,128,768]{2,1,0:T(8,128)(2,1)S(1)}, u32[]{:S(2)}, u32[]{:S(2)}) collective-permute-start(bf16[2,128,768]{2,1,0:T(8,128)(2,1)S(1)} %get-tuple-element.77.refs_0_), channel_id=1, source_target_pairs={{0,2},{2,0},{1,3},{3,1},{4,6},{6,4},{5,7},{7,5},{8,10},{10,8},{9,1... | collective-permute-start | bytes 1179656 | tf_op jit(solution)/shard_map/ppermute | solution.py:18
  39.5 2.7 %up.6 = (bf16[2,128,768]{2,1,0:T(8,128)(2,1)S(1)}, bf16[256,256]{1,0:T(8,128)(2,1)S(1)}) custom-call(bf16[64,2816]{1,0:T(8,128)(2,1)S(1)} %collective-permute-done.5.refs_0_, bf16[64,2816]{1,0:T(8,128)(2,1)S(1)} %collective-permute-done.8.refs_1_, bf16[32,2816]{1,0:T(8,128)(2,1)S(1)} %collective-permute-done.14.refs_2_, ...), custom_call_target="tpu_custom_call" | custom-call | tf_op jit(solution)/shard_map/up/pallas_call | solution.py:396
  42.2 0.8 collective-permute-done.7.refs_0_
  43.0 0.5 collective-permute-start.29
  43.5 0.1 collective-permute-start.19
  43.6 2.3 %collective-permute-done.18.refs_2_ = bf16[32,2816]{1,0:T(8,128)(2,1)S(1)} collective-permute-done((bf16[32,2816]{1,0:T(8,128)(2,1)S(1)}, bf16[32,2816]{1,0:T(8,128)(2,1)S(1)}, u32[]{:S(2)}, u32[]{:S(2)}) %collective-permute-start.18) | collective-permute-done | bytes 180256 | tf_op jit(solution)/shard_map/ppermute | solution.py:18
  46.0 0.5 collective-permute-start.22
  46.5 0.9 %collective-permute-done.20.refs_4_ = bf16[32,2816]{1,0:T(8,128)(2,1)S(1)} collective-permute-done((bf16[32,2816]{1,0:T(8,128)(2,1)S(1)}, bf16[32,2816]{1,0:T(8,128)(2,1)S(1)}, u32[]{:S(2)}, u32[]{:S(2)}) %collective-permute-start.20) | collective-permute-done | bytes 180256 | tf_op jit(solution)/shard_map/ppermute | solution.py:18
  47.4 0.3 collective-permute-done.22.refs_6_
  47.6 2.7 %up.7 = (bf16[2,128,768]{2,1,0:T(8,128)(2,1)S(1)}, bf16[256,256]{1,0:T(8,128)(2,1)S(1)}) custom-call(bf16[64,2816]{1,0:T(8,128)(2,1)S(1)} %collective-permute-done.7.refs_0_, bf16[32,2816]{1,0:T(8,128)(2,1)S(1)} %collective-permute-done.6.refs_1_, bf16[32,2816]{1,0:T(8,128)(2,1)S(1)} %collective-permute-done.18.refs_2_, ...), custom_call_target="tpu_custom_call" | custom-call | tf_op jit(solution)/shard_map/up/pallas_call | solution.py:396
  50.3 3.7 %down.4 = (f32[1344,128]{1,0:T(8,128)S(1)}, bf16[672,128]{1,0:T(8,128)(2,1)S(1)}, bf16[672,128]{1,0:T(8,128)(2,1)S(1)}) custom-call(bf16[2,128,768]{2,1,0:T(8,128)(2,1)S(1)} %get-tuple-element.77.refs_0_, bf16[2,128,768]{2,1,0:T(8,128)(2,1)S(1)} %collective-permute-done.25.refs_1_, bf16[6,448,1536]{2,1,0:T(8,128)(2,1)S(1)} %get-tuple-element.79.refs_2_, ...), custom_call_target="tpu_custom_call" | custom-call | tf_op jit(solution)/shard_map/down/pallas_call | solution.py:418
  54.1 0.3 collective-permute-start.26
  54.4 0.3 collective-permute-start.27
  54.6 1.2 %collective-permute-start.24 = (bf16[2,128,768]{2,1,0:T(8,128)(2,1)S(1)}, bf16[2,128,768]{2,1,0:T(8,128)(2,1)S(1)}, u32[]{:S(2)}, u32[]{:S(2)}) collective-permute-start(bf16[2,128,768]{2,1,0:T(8,128)(2,1)S(1)} %get-tuple-element.76.refs_0_), channel_id=1, source_target_pairs={{0,2},{2,0},{1,3},{3,1},{4,6},{6,4},{5,7},{7,5},{8,10},{10,8},{9,1... | collective-permute-start | bytes 1179656 | tf_op jit(solution)/shard_map/ppermute | solution.py:18
  55.9 1.0 %collective-permute-start.28 = (bf16[1344,128]{1,0:T(8,128)(2,1)S(1)}, bf16[1344,128]{1,0:T(8,128)(2,1)S(1)}, u32[]{:S(2)}, u32[]{:S(2)}) collective-permute-start(bf16[1344,128]{1,0:T(8,128)(2,1)S(1)} %add.4), channel_id=1, source_target_pairs={{0,12},{4,0},{8,4},{12,8},{1,13},{5,1},{9,5},{13,9},{2,14},{6,2},{... | collective-permute-start | bytes 1032200 | tf_op jit(solution)/shard_map/ppermute | solution.py:18
  56.8 0.6 collective-permute-done.29.refs_1_
  57.5 3.7 %down.5 = (f32[1344,128]{1,0:T(8,128)S(1)}, bf16[672,128]{1,0:T(8,128)(2,1)S(1)}, bf16[672,128]{1,0:T(8,128)(2,1)S(1)}) custom-call(bf16[2,128,768]{2,1,0:T(8,128)(2,1)S(1)} %get-tuple-element.85.refs_0_, bf16[2,128,768]{2,1,0:T(8,128)(2,1)S(1)} %collective-permute-done.29.refs_1_, bf16[6,448,1536]{2,1,0:T(8,128)(2,1)S(1)} %get-tuple-element.79.refs_2_, ...), custom_call_target="tpu_custom_call" | custom-call | tf_op jit(solution)/shard_map/down/pallas_call | solution.py:418
  61.3 0.5 collective-permute-start.31
  61.8 0.9 %collective-permute-done.30.refs_0_ = bf16[672,128]{1,0:T(8,128)(2,1)S(1)} collective-permute-done((bf16[672,128]{1,0:T(8,128)(2,1)S(1)}, bf16[672,128]{1,0:T(8,128)(2,1)S(1)}, u32[]{:S(2)}, u32[]{:S(2)}) %collective-permute-start.30) | collective-permute-done | bytes 172064 | tf_op jit(solution)/shard_map/ppermute | solution.py:18
  62.7 0.2 collective-permute-done.31.refs_1_
  63.0 0.9 collective-permute-start.34
  63.9 1.6 %collective-permute-start.23 = (bf16[2,128,768]{2,1,0:T(8,128)(2,1)S(1)}, bf16[2,128,768]{2,1,0:T(8,128)(2,1)S(1)}, u32[]{:S(2)}, u32[]{:S(2)}) collective-permute-start(bf16[2,128,768]{2,1,0:T(8,128)(2,1)S(1)} %get-tuple-element.75.refs_0_), channel_id=1, source_target_pairs={{0,2},{2,0},{1,3},{3,1},{4,6},{6,4},{5,7},{7,5},{8,10},{10,8},{9,1... | collective-permute-start | bytes 1179656 | tf_op jit(solution)/shard_map/ppermute | solution.py:18
  65.5 0.6 collective-permute-done.28.refs_2_
  66.1 3.7 %down.6 = (f32[1344,128]{1,0:T(8,128)S(1)}, bf16[672,128]{1,0:T(8,128)(2,1)S(1)}, bf16[672,128]{1,0:T(8,128)(2,1)S(1)}) custom-call(bf16[2,128,768]{2,1,0:T(8,128)(2,1)S(1)} %get-tuple-element.76.refs_0_, bf16[2,128,768]{2,1,0:T(8,128)(2,1)S(1)} %collective-permute-done.24.refs_1_, bf16[6,448,1536]{2,1,0:T(8,128)(2,1)S(1)} %get-tuple-element.79.refs_2_, ...), custom_call_target="tpu_custom_call" | custom-call | tf_op jit(solution)/shard_map/down/pallas_call | solution.py:418
  69.9 0.1 collective-permute-start.32
  70.0 0.5 collective-permute-start.33
  70.5 0.9 %collective-permute-done.32.refs_0_ = bf16[672,128]{1,0:T(8,128)(2,1)S(1)} collective-permute-done((bf16[672,128]{1,0:T(8,128)(2,1)S(1)}, bf16[672,128]{1,0:T(8,128)(2,1)S(1)}, u32[]{:S(2)}, u32[]{:S(2)}) %collective-permute-start.32) | collective-permute-done | bytes 172064 | tf_op jit(solution)/shard_map/ppermute | solution.py:18
  71.4 0.2 collective-permute-done.33.refs_1_
  71.6 3.7 %collective-permute-done.34.refs_2_ = bf16[1344,128]{1,0:T(8,128)(2,1)S(1)} collective-permute-done((bf16[1344,128]{1,0:T(8,128)(2,1)S(1)}, bf16[1344,128]{1,0:T(8,128)(2,1)S(1)}, u32[]{:S(2)}, u32[]{:S(2)}) %collective-permute-start.34) | collective-permute-done | bytes 344096 | tf_op jit(solution)/shard_map/ppermute | solution.py:18
  75.3 0.1 add.6
  75.5 3.7 %down.7 = (f32[1344,128]{1,0:T(8,128)S(1)}, bf16[672,128]{1,0:T(8,128)(2,1)S(1)}, bf16[672,128]{1,0:T(8,128)(2,1)S(1)}) custom-call(bf16[2,128,768]{2,1,0:T(8,128)(2,1)S(1)} %get-tuple-element.75.refs_0_, bf16[2,128,768]{2,1,0:T(8,128)(2,1)S(1)} %collective-permute-done.23.refs_1_, bf16[6,448,1536]{2,1,0:T(8,128)(2,1)S(1)} %get-tuple-element.79.refs_2_, ...), custom_call_target="tpu_custom_call" | custom-call | tf_op jit(solution)/shard_map/down/pallas_call | solution.py:418
  79.2 0.1 collective-permute-start.35
  79.3 0.5 collective-permute-start.36
  79.8 0.9 %collective-permute-done.35.refs_0_ = bf16[672,128]{1,0:T(8,128)(2,1)S(1)} collective-permute-done((bf16[672,128]{1,0:T(8,128)(2,1)S(1)}, bf16[672,128]{1,0:T(8,128)(2,1)S(1)}, u32[]{:S(2)}, u32[]{:S(2)}) %collective-permute-start.35) | collective-permute-done | bytes 172064 | tf_op jit(solution)/shard_map/ppermute | solution.py:18
  80.7 0.2 collective-permute-done.36.refs_1_
  80.9 5.7 %collective-permute-done.37.refs_3_ = bf16[1344,128]{1,0:T(8,128)(2,1)S(1)} collective-permute-done((bf16[1344,128]{1,0:T(8,128)(2,1)S(1)}, bf16[1344,128]{1,0:T(8,128)(2,1)S(1)}, u32[]{:S(2)}, u32[]{:S(2)}) %collective-permute-start.37) | collective-permute-done | bytes 344096 | tf_op jit(solution)/shard_map/ppermute | solution.py:18
  86.7 0.9 %add.7 = bf16[1344,128]{1,0:T(8,128)(2,1)} custom-call(f32[1344,128]{1,0:T(8,128)S(1)} %get-tuple-element.100.own, bf16[672,128]{1,0:T(8,128)(2,1)S(1)} %collective-permute-done.35.refs_0_, bf16[672,128]{1,0:T(8,128)(2,1)S(1)} %collective-permute-done.36.refs_1_, bf16[1344,128]{1,0:T(8,128)(2,1)S(1)} %collective-permute-done.28.refs_2_, ...), custom_call_target="tpu_custom_call" | custom-call | flops 1 | bytes 1 | tf_op jit(solution)/shard_map/add/pallas_call | solution.py:451
  (32 shorter events, 0.6 us)
Async XLA Ops:
  2.6 14.4 %collective-permute-start.4 = (bf16[64,2816]{1,0:T(8,128)(2,1)S(1)}, bf16[64,2816]{1,0:T(8,128)(2,1)S(1)}, u32[]{:S(2)}, u32[]{:S(2)}) collective-permute-start(bf16[64,2816]{1,0:T(8,128)(2,1)S(1)} %get-tuple-element.55.refs_0_), channel_id=1, source_target_pairs={{0,4},{4,8},{8,12},{12,0},{1,5},{5,9},{9,13},{13,1},{2,6},{6,10},{... | collective-permute-start | bytes 1081352 | tf_op jit(solution)/shard_map/ppermute | solution.py:18
  5.7 1.5 %collective-permute-start = (bf16[32,2816]{1,0:T(8,128)(2,1)S(1)}, bf16[32,2816]{1,0:T(8,128)(2,1)S(1)}, u32[]{:S(2)}, u32[]{:S(2)}) collective-permute-start(bf16[32,2816]{1,0:T(8,128)(2,1)S(1)} %get-tuple-element.116), channel_id=1, source_target_pairs={{0,1},{1,0},{2,3},{3,2},{4,5},{5,4},{6,7},{7,6},{8,9},{9,8},{10,11... | collective-permute-start | bytes 540680 | tf_op jit(solution)/shard_map/ppermute | solution.py:18
  5.7 3.5 %collective-permute-start.1 = (bf16[32,2816]{1,0:T(8,128)(2,1)S(1)}, bf16[32,2816]{1,0:T(8,128)(2,1)S(1)}, u32[]{:S(2)}, u32[]{:S(2)}) collective-permute-start(bf16[32,2816]{1,0:T(8,128)(2,1)S(1)} %get-tuple-element.115), channel_id=1, source_target_pairs={{0,1},{1,0},{2,3},{3,2},{4,5},{5,4},{6,7},{7,6},{8,9},{9,8},{10,11... | collective-permute-start | bytes 540680 | tf_op jit(solution)/shard_map/ppermute | solution.py:18
  6.3 2.9 %collective-permute-start.2 = (bf16[32,2816]{1,0:T(8,128)(2,1)S(1)}, bf16[32,2816]{1,0:T(8,128)(2,1)S(1)}, u32[]{:S(2)}, u32[]{:S(2)}) collective-permute-start(bf16[32,2816]{1,0:T(8,128)(2,1)S(1)} %get-tuple-element.114), channel_id=1, source_target_pairs={{0,1},{1,0},{2,3},{3,2},{4,5},{5,4},{6,7},{7,6},{8,9},{9,8},{10,11... | collective-permute-start | bytes 540680 | tf_op jit(solution)/shard_map/ppermute | solution.py:18
  6.4 2.8 %collective-permute-start.3 = (bf16[32,2816]{1,0:T(8,128)(2,1)S(1)}, bf16[32,2816]{1,0:T(8,128)(2,1)S(1)}, u32[]{:S(2)}, u32[]{:S(2)}) collective-permute-start(bf16[32,2816]{1,0:T(8,128)(2,1)S(1)} %get-tuple-element.71), channel_id=1, source_target_pairs={{0,1},{1,0},{2,3},{3,2},{4,5},{5,4},{6,7},{7,6},{8,9},{9,8},{10,11... | collective-permute-start | bytes 540680 | tf_op jit(solution)/shard_map/ppermute | solution.py:18
  7.1 12.9 %collective-permute-start.6 = (bf16[32,2816]{1,0:T(8,128)(2,1)S(1)}, bf16[32,2816]{1,0:T(8,128)(2,1)S(1)}, u32[]{:S(2)}, u32[]{:S(2)}) collective-permute-start(bf16[32,2816]{1,0:T(8,128)(2,1)S(1)} %get-tuple-element.114), channel_id=1, source_target_pairs={{0,12},{4,0},{8,4},{12,8},{1,13},{5,1},{9,5},{13,9},{2,14},{6,2},{... | collective-permute-start | bytes 540680 | tf_op jit(solution)/shard_map/ppermute | solution.py:18
  16.9 10.8 %collective-permute-start.5 = (bf16[64,2816]{1,0:T(8,128)(2,1)S(1)}, bf16[64,2816]{1,0:T(8,128)(2,1)S(1)}, u32[]{:S(2)}, u32[]{:S(2)}) collective-permute-start(bf16[64,2816]{1,0:T(8,128)(2,1)S(1)} %collective-permute-done.4.refs_0_), channel_id=1, source_target_pairs={{0,4},{4,8},{8,12},{12,0},{1,5},{5,9},{9,13},{13,1},{2,6},{6,10},{... | collective-permute-start | bytes 1081352 | tf_op jit(solution)/shard_map/ppermute | solution.py:18
  16.9 12.2 %collective-permute-start.9 = (bf16[64,2816]{1,0:T(8,128)(2,1)S(1)}, bf16[64,2816]{1,0:T(8,128)(2,1)S(1)}, u32[]{:S(2)}, u32[]{:S(2)}) collective-permute-start(bf16[64,2816]{1,0:T(8,128)(2,1)S(1)} %collective-permute-done.4.refs_0_), channel_id=1, source_target_pairs={{0,2},{2,0},{1,3},{3,1},{4,6},{6,4},{5,7},{7,5},{8,10},{10,8},{9,1... | collective-permute-start | bytes 1081352 | tf_op jit(solution)/shard_map/ppermute | solution.py:18
  20.0 9.8 %collective-permute-start.10 = (bf16[32,2816]{1,0:T(8,128)(2,1)S(1)}, bf16[32,2816]{1,0:T(8,128)(2,1)S(1)}, u32[]{:S(2)}, u32[]{:S(2)}) collective-permute-start(bf16[32,2816]{1,0:T(8,128)(2,1)S(1)} %get-tuple-element.112), channel_id=1, source_target_pairs={{0,1},{1,0},{2,3},{3,2},{4,5},{5,4},{6,7},{7,6},{8,9},{9,8},{10,11... | collective-permute-start | bytes 540680 | tf_op jit(solution)/shard_map/ppermute | solution.py:18
  20.1 9.8 %collective-permute-start.11 = (bf16[32,2816]{1,0:T(8,128)(2,1)S(1)}, bf16[32,2816]{1,0:T(8,128)(2,1)S(1)}, u32[]{:S(2)}, u32[]{:S(2)}) collective-permute-start(bf16[32,2816]{1,0:T(8,128)(2,1)S(1)} %get-tuple-element.111), channel_id=1, source_target_pairs={{0,1},{1,0},{2,3},{3,2},{4,5},{5,4},{6,7},{7,6},{8,9},{9,8},{10,11... | collective-permute-start | bytes 540680 | tf_op jit(solution)/shard_map/ppermute | solution.py:18
  27.7 8.0 %collective-permute-start.8 = (bf16[64,2816]{1,0:T(8,128)(2,1)S(1)}, bf16[64,2816]{1,0:T(8,128)(2,1)S(1)}, u32[]{:S(2)}, u32[]{:S(2)}) collective-permute-start(bf16[64,2816]{1,0:T(8,128)(2,1)S(1)} %collective-permute-done.5.refs_0_), channel_id=1, source_target_pairs={{0,2},{2,0},{1,3},{3,1},{4,6},{6,4},{5,7},{7,5},{8,10},{10,8},{9,1... | collective-permute-start | bytes 1081352 | tf_op jit(solution)/shard_map/ppermute | solution.py:18
  29.2 1.5 %collective-permute-start.12 = (bf16[32,2816]{1,0:T(8,128)(2,1)S(1)}, bf16[32,2816]{1,0:T(8,128)(2,1)S(1)}, u32[]{:S(2)}, u32[]{:S(2)}) collective-permute-start(bf16[32,2816]{1,0:T(8,128)(2,1)S(1)} %get-tuple-element.110), channel_id=1, source_target_pairs={{0,1},{1,0},{2,3},{3,2},{4,5},{5,4},{6,7},{7,6},{8,9},{9,8},{10,11... | collective-permute-start | bytes 540680 | tf_op jit(solution)/shard_map/ppermute | solution.py:18
  29.3 1.7 %collective-permute-start.13 = (bf16[32,2816]{1,0:T(8,128)(2,1)S(1)}, bf16[32,2816]{1,0:T(8,128)(2,1)S(1)}, u32[]{:S(2)}, u32[]{:S(2)}) collective-permute-start(bf16[32,2816]{1,0:T(8,128)(2,1)S(1)} %get-tuple-element.109), channel_id=1, source_target_pairs={{0,1},{1,0},{2,3},{3,2},{4,5},{5,4},{6,7},{7,6},{8,9},{9,8},{10,11... | collective-permute-start | bytes 540680 | tf_op jit(solution)/shard_map/ppermute | solution.py:18
  29.8 13.1 %collective-permute-start.7 = (bf16[64,2816]{1,0:T(8,128)(2,1)S(1)}, bf16[64,2816]{1,0:T(8,128)(2,1)S(1)}, u32[]{:S(2)}, u32[]{:S(2)}) collective-permute-start(bf16[64,2816]{1,0:T(8,128)(2,1)S(1)} %collective-permute-done.5.refs_0_), channel_id=1, source_target_pairs={{0,4},{4,8},{8,12},{12,0},{1,5},{5,9},{9,13},{13,1},{2,6},{6,10},{... | collective-permute-start | bytes 1081352 | tf_op jit(solution)/shard_map/ppermute | solution.py:18
  29.9 6.4 %collective-permute-start.14 = (bf16[32,2816]{1,0:T(8,128)(2,1)S(1)}, bf16[32,2816]{1,0:T(8,128)(2,1)S(1)}, u32[]{:S(2)}, u32[]{:S(2)}) collective-permute-start(bf16[32,2816]{1,0:T(8,128)(2,1)S(1)} %get-tuple-element.108), channel_id=1, source_target_pairs={{0,1},{1,0},{2,3},{3,2},{4,5},{5,4},{6,7},{7,6},{8,9},{9,8},{10,11... | collective-permute-start | bytes 540680 | tf_op jit(solution)/shard_map/ppermute | solution.py:18
  30.7 5.7 %collective-permute-start.15 = (bf16[32,2816]{1,0:T(8,128)(2,1)S(1)}, bf16[32,2816]{1,0:T(8,128)(2,1)S(1)}, u32[]{:S(2)}, u32[]{:S(2)}) collective-permute-start(bf16[32,2816]{1,0:T(8,128)(2,1)S(1)} %get-tuple-element.107), channel_id=1, source_target_pairs={{0,1},{1,0},{2,3},{3,2},{4,5},{5,4},{6,7},{7,6},{8,9},{9,8},{10,11... | collective-permute-start | bytes 540680 | tf_op jit(solution)/shard_map/ppermute | solution.py:18
  35.8 2.3 %collective-permute-start.16 = (bf16[32,2816]{1,0:T(8,128)(2,1)S(1)}, bf16[32,2816]{1,0:T(8,128)(2,1)S(1)}, u32[]{:S(2)}, u32[]{:S(2)}) collective-permute-start(bf16[32,2816]{1,0:T(8,128)(2,1)S(1)} %get-tuple-element.106), channel_id=1, source_target_pairs={{0,1},{1,0},{2,3},{3,2},{4,5},{5,4},{6,7},{7,6},{8,9},{9,8},{10,11... | collective-permute-start | bytes 540680 | tf_op jit(solution)/shard_map/ppermute | solution.py:18
  35.8 3.7 %collective-permute-start.17 = (bf16[32,2816]{1,0:T(8,128)(2,1)S(1)}, bf16[32,2816]{1,0:T(8,128)(2,1)S(1)}, u32[]{:S(2)}, u32[]{:S(2)}) collective-permute-start(bf16[32,2816]{1,0:T(8,128)(2,1)S(1)} %get-tuple-element.105), channel_id=1, source_target_pairs={{0,1},{1,0},{2,3},{3,2},{4,5},{5,4},{6,7},{7,6},{8,9},{9,8},{10,11... | collective-permute-start | bytes 540680 | tf_op jit(solution)/shard_map/ppermute | solution.py:18
  36.3 9.7 %collective-permute-start.21 = (bf16[32,2816]{1,0:T(8,128)(2,1)S(1)}, bf16[32,2816]{1,0:T(8,128)(2,1)S(1)}, u32[]{:S(2)}, u32[]{:S(2)}) collective-permute-start(bf16[32,2816]{1,0:T(8,128)(2,1)S(1)} %collective-permute-done.6.refs_1_), channel_id=1, source_target_pairs={{0,1},{1,0},{2,3},{3,2},{4,5},{5,4},{6,7},{7,6},{8,9},{9,8},{10,11... | collective-permute-start | bytes 540680 | tf_op jit(solution)/shard_map/ppermute | solution.py:18
  36.4 9.5 %collective-permute-start.18 = (bf16[32,2816]{1,0:T(8,128)(2,1)S(1)}, bf16[32,2816]{1,0:T(8,128)(2,1)S(1)}, u32[]{:S(2)}, u32[]{:S(2)}) collective-permute-start(bf16[32,2816]{1,0:T(8,128)(2,1)S(1)} %get-tuple-element.71), channel_id=1, source_target_pairs={{0,12},{4,0},{8,4},{12,8},{1,13},{5,1},{9,5},{13,9},{2,14},{6,2},{... | collective-permute-start | bytes 540680 | tf_op jit(solution)/shard_map/ppermute | solution.py:18
  38.0 12.3 %collective-permute-start.25 = (bf16[2,128,768]{2,1,0:T(8,128)(2,1)S(1)}, bf16[2,128,768]{2,1,0:T(8,128)(2,1)S(1)}, u32[]{:S(2)}, u32[]{:S(2)}) collective-permute-start(bf16[2,128,768]{2,1,0:T(8,128)(2,1)S(1)} %get-tuple-element.77.refs_0_), channel_id=1, source_target_pairs={{0,2},{2,0},{1,3},{3,1},{4,6},{6,4},{5,7},{7,5},{8,10},{10,8},{9,1... | collective-permute-start | bytes 1179656 | tf_op jit(solution)/shard_map/ppermute | solution.py:18
  43.0 14.5 %collective-permute-start.29 = (bf16[2,128,768]{2,1,0:T(8,128)(2,1)S(1)}, bf16[2,128,768]{2,1,0:T(8,128)(2,1)S(1)}, u32[]{:S(2)}, u32[]{:S(2)}) collective-permute-start(bf16[2,128,768]{2,1,0:T(8,128)(2,1)S(1)} %get-tuple-element.85.refs_0_), channel_id=1, source_target_pairs={{0,2},{2,0},{1,3},{3,1},{4,6},{6,4},{5,7},{7,5},{8,10},{10,8},{9,1... | collective-permute-start | bytes 1179656 | tf_op jit(solution)/shard_map/ppermute | solution.py:18
  43.5 2.9 %collective-permute-start.19 = (bf16[32,2816]{1,0:T(8,128)(2,1)S(1)}, bf16[32,2816]{1,0:T(8,128)(2,1)S(1)}, u32[]{:S(2)}, u32[]{:S(2)}) collective-permute-start(bf16[32,2816]{1,0:T(8,128)(2,1)S(1)} %get-tuple-element.104), channel_id=1, source_target_pairs={{0,1},{1,0},{2,3},{3,2},{4,5},{5,4},{6,7},{7,6},{8,9},{9,8},{10,11... | collective-permute-start | bytes 540680 | tf_op jit(solution)/shard_map/ppermute | solution.py:18
  46.0 1.4 %collective-permute-start.20 = (bf16[32,2816]{1,0:T(8,128)(2,1)S(1)}, bf16[32,2816]{1,0:T(8,128)(2,1)S(1)}, u32[]{:S(2)}, u32[]{:S(2)}) collective-permute-start(bf16[32,2816]{1,0:T(8,128)(2,1)S(1)} %get-tuple-element.103), channel_id=1, source_target_pairs={{0,1},{1,0},{2,3},{3,2},{4,5},{5,4},{6,7},{7,6},{8,9},{9,8},{10,11... | collective-permute-start | bytes 540680 | tf_op jit(solution)/shard_map/ppermute | solution.py:18
  46.0 1.6 %collective-permute-start.22 = (bf16[32,2816]{1,0:T(8,128)(2,1)S(1)}, bf16[32,2816]{1,0:T(8,128)(2,1)S(1)}, u32[]{:S(2)}, u32[]{:S(2)}) collective-permute-start(bf16[32,2816]{1,0:T(8,128)(2,1)S(1)} %collective-permute-done.18.refs_2_), channel_id=1, source_target_pairs={{0,1},{1,0},{2,3},{3,2},{4,5},{5,4},{6,7},{7,6},{8,9},{9,8},{10,11... | collective-permute-start | bytes 540680 | tf_op jit(solution)/shard_map/ppermute | solution.py:18
  54.1 1.7 %collective-permute-start.26 = (bf16[672,128]{1,0:T(8,128)(2,1)S(1)}, bf16[672,128]{1,0:T(8,128)(2,1)S(1)}, u32[]{:S(2)}, u32[]{:S(2)}) collective-permute-start(bf16[672,128]{1,0:T(8,128)(2,1)S(1)} %get-tuple-element.82), channel_id=1, source_target_pairs={{0,1},{1,0},{2,3},{3,2},{4,5},{5,4},{6,7},{7,6},{8,9},{9,8},{10,11... | collective-permute-start | bytes 516104 | tf_op jit(solution)/shard_map/ppermute | solution.py:18
  54.4 1.4 %collective-permute-start.27 = (bf16[672,128]{1,0:T(8,128)(2,1)S(1)}, bf16[672,128]{1,0:T(8,128)(2,1)S(1)}, u32[]{:S(2)}, u32[]{:S(2)}) collective-permute-start(bf16[672,128]{1,0:T(8,128)(2,1)S(1)} %get-tuple-element.83), channel_id=1, source_target_pairs={{0,1},{1,0},{2,3},{3,2},{4,5},{5,4},{6,7},{7,6},{8,9},{9,8},{10,11... | collective-permute-start | bytes 516104 | tf_op jit(solution)/shard_map/ppermute | solution.py:18
  54.6 11.5 %collective-permute-start.24 = (bf16[2,128,768]{2,1,0:T(8,128)(2,1)S(1)}, bf16[2,128,768]{2,1,0:T(8,128)(2,1)S(1)}, u32[]{:S(2)}, u32[]{:S(2)}) collective-permute-start(bf16[2,128,768]{2,1,0:T(8,128)(2,1)S(1)} %get-tuple-element.76.refs_0_), channel_id=1, source_target_pairs={{0,2},{2,0},{1,3},{3,1},{4,6},{6,4},{5,7},{7,5},{8,10},{10,8},{9,1... | collective-permute-start | bytes 1179656 | tf_op jit(solution)/shard_map/ppermute | solution.py:18
  55.9 10.3 %collective-permute-start.28 = (bf16[1344,128]{1,0:T(8,128)(2,1)S(1)}, bf16[1344,128]{1,0:T(8,128)(2,1)S(1)}, u32[]{:S(2)}, u32[]{:S(2)}) collective-permute-start(bf16[1344,128]{1,0:T(8,128)(2,1)S(1)} %add.4), channel_id=1, source_target_pairs={{0,12},{4,0},{8,4},{12,8},{1,13},{5,1},{9,5},{13,9},{2,14},{6,2},{... | collective-permute-start | bytes 1032200 | tf_op jit(solution)/shard_map/ppermute | solution.py:18
  61.2 1.5 %collective-permute-start.30 = (bf16[672,128]{1,0:T(8,128)(2,1)S(1)}, bf16[672,128]{1,0:T(8,128)(2,1)S(1)}, u32[]{:S(2)}, u32[]{:S(2)}) collective-permute-start(bf16[672,128]{1,0:T(8,128)(2,1)S(1)} %get-tuple-element.89), channel_id=1, source_target_pairs={{0,1},{1,0},{2,3},{3,2},{4,5},{5,4},{6,7},{7,6},{8,9},{9,8},{10,11... | collective-permute-start | bytes 516104 | tf_op jit(solution)/shard_map/ppermute | solution.py:18
  61.3 1.6 %collective-permute-start.31 = (bf16[672,128]{1,0:T(8,128)(2,1)S(1)}, bf16[672,128]{1,0:T(8,128)(2,1)S(1)}, u32[]{:S(2)}, u32[]{:S(2)}) collective-permute-start(bf16[672,128]{1,0:T(8,128)(2,1)S(1)} %get-tuple-element.90), channel_id=1, source_target_pairs={{0,1},{1,0},{2,3},{3,2},{4,5},{5,4},{6,7},{7,6},{8,9},{9,8},{10,11... | collective-permute-start | bytes 516104 | tf_op jit(solution)/shard_map/ppermute | solution.py:18
  63.0 12.3 %collective-permute-start.34 = (bf16[1344,128]{1,0:T(8,128)(2,1)S(1)}, bf16[1344,128]{1,0:T(8,128)(2,1)S(1)}, u32[]{:S(2)}, u32[]{:S(2)}) collective-permute-start(bf16[1344,128]{1,0:T(8,128)(2,1)S(1)} %add.5), channel_id=1, source_target_pairs={{0,4},{4,8},{8,12},{12,0},{1,5},{5,9},{9,13},{13,1},{2,6},{6,10},{... | collective-permute-start | bytes 1032200 | tf_op jit(solution)/shard_map/ppermute | solution.py:18
  63.9 11.6 %collective-permute-start.23 = (bf16[2,128,768]{2,1,0:T(8,128)(2,1)S(1)}, bf16[2,128,768]{2,1,0:T(8,128)(2,1)S(1)}, u32[]{:S(2)}, u32[]{:S(2)}) collective-permute-start(bf16[2,128,768]{2,1,0:T(8,128)(2,1)S(1)} %get-tuple-element.75.refs_0_), channel_id=1, source_target_pairs={{0,2},{2,0},{1,3},{3,1},{4,6},{6,4},{5,7},{7,5},{8,10},{10,8},{9,1... | collective-permute-start | bytes 1179656 | tf_op jit(solution)/shard_map/ppermute | solution.py:18
  69.9 1.5 %collective-permute-start.32 = (bf16[672,128]{1,0:T(8,128)(2,1)S(1)}, bf16[672,128]{1,0:T(8,128)(2,1)S(1)}, u32[]{:S(2)}, u32[]{:S(2)}) collective-permute-start(bf16[672,128]{1,0:T(8,128)(2,1)S(1)} %get-tuple-element.96), channel_id=1, source_target_pairs={{0,1},{1,0},{2,3},{3,2},{4,5},{5,4},{6,7},{7,6},{8,9},{9,8},{10,11... | collective-permute-start | bytes 516104 | tf_op jit(solution)/shard_map/ppermute | solution.py:18
  70.0 1.6 %collective-permute-start.33 = (bf16[672,128]{1,0:T(8,128)(2,1)S(1)}, bf16[672,128]{1,0:T(8,128)(2,1)S(1)}, u32[]{:S(2)}, u32[]{:S(2)}) collective-permute-start(bf16[672,128]{1,0:T(8,128)(2,1)S(1)} %get-tuple-element.97), channel_id=1, source_target_pairs={{0,1},{1,0},{2,3},{3,2},{4,5},{5,4},{6,7},{7,6},{8,9},{9,8},{10,11... | collective-permute-start | bytes 516104 | tf_op jit(solution)/shard_map/ppermute | solution.py:18
  75.4 11.3 %collective-permute-start.37 = (bf16[1344,128]{1,0:T(8,128)(2,1)S(1)}, bf16[1344,128]{1,0:T(8,128)(2,1)S(1)}, u32[]{:S(2)}, u32[]{:S(2)}) collective-permute-start(bf16[1344,128]{1,0:T(8,128)(2,1)S(1)} %add.6), channel_id=1, source_target_pairs={{0,4},{4,8},{8,12},{12,0},{1,5},{5,9},{9,13},{13,1},{2,6},{6,10},{... | collective-permute-start | bytes 1032200 | tf_op jit(solution)/shard_map/ppermute | solution.py:18
  79.2 1.5 %collective-permute-start.35 = (bf16[672,128]{1,0:T(8,128)(2,1)S(1)}, bf16[672,128]{1,0:T(8,128)(2,1)S(1)}, u32[]{:S(2)}, u32[]{:S(2)}) collective-permute-start(bf16[672,128]{1,0:T(8,128)(2,1)S(1)} %get-tuple-element.101), channel_id=1, source_target_pairs={{0,1},{1,0},{2,3},{3,2},{4,5},{5,4},{6,7},{7,6},{8,9},{9,8},{10,11... | collective-permute-start | bytes 516104 | tf_op jit(solution)/shard_map/ppermute | solution.py:18
  79.3 1.6 %collective-permute-start.36 = (bf16[672,128]{1,0:T(8,128)(2,1)S(1)}, bf16[672,128]{1,0:T(8,128)(2,1)S(1)}, u32[]{:S(2)}, u32[]{:S(2)}) collective-permute-start(bf16[672,128]{1,0:T(8,128)(2,1)S(1)} %get-tuple-element.102), channel_id=1, source_target_pairs={{0,1},{1,0},{2,3},{3,2},{4,5},{5,4},{6,7},{7,6},{8,9},{9,8},{10,11... | collective-permute-start | bytes 516104 | tf_op jit(solution)/shard_map/ppermute | solution.py:18

commit v5 on v4

--- a/solution.py
+++ b/solution.py
@@ -37,9 +37,8 @@
     return (lax.axis_index("ctx") * lax.axis_size("tp") + lax.axis_index("tp")) * local_experts
 
 
-def prep_kernel(experts_all, parts, routes, gates, tokens, up_left, weight, *refs):
-    pieces, tiles = refs[:parts], refs[parts]
-    routes_in, gates_in, rows_in, table_in, info, sems = refs[parts + 1 :]
+def prep_kernel(experts_all, parts, routes, gates, tokens, up_left, *refs):
+    pieces, (routes_in, gates_in, rows_in, table_in, info, sems) = refs[:parts], refs[parts:]
     count, model_width = tokens.shape
     width = info.shape[1]
     factors = up_left.shape[0]
@@ -50,14 +49,7 @@
             ((routes, routes_in), (gates, gates_in), (up_left, table_in), (tokens, rows_in))
         )
     ]
-    steps, _, tile = tiles.shape
-    loads = [
-        pltpu.make_async_copy(
-            weight.at[0, :, pl.ds(n * tile, tile)], tiles.at[n], sems.at[len(copies) + n]
-        )
-        for n in range(steps)
-    ]
-    for copy in copies + loads:
+    for copy in copies:
         copy.start()
     line = iota((width, count), 0)
     expert = lax.rem(line, experts_all)
@@ -91,21 +83,20 @@
         at = pl.multiple_of(lax.rem(my_part() - j + parts, parts) * rows, rows)
         piece[:, :model_width] = rows_in[pl.ds(at, rows), :]
         piece[:, model_width:] = info[pl.ds(at, rows), :]
-    for copy in loads:
-        copy.wait()
 
 
 def up_kernel(first, load, count, rows, experts_all, parts, cores, capacity, factors, *refs):
     pieces = refs[:count]
-    tiles_first, weight, right, seeds_in, *rest = refs[count:-5]
+    weight, right, seeds_in, *rest = refs[count:-5]
     down_weight = rest.pop(0) if load else None
-    hidden, gate_out, *tiles_rest = rest
-    down_tiles = tiles_rest.pop() if load else None
+    hidden, gate_out, *tiles = rest
+    down_tiles = tiles.pop() if load else None
     block, slots, right_in, seeds, sems = refs[-5:]
     tok_count = rows * parts
-    tiles_rest = tiles_rest[0] if first else weight
+    tiles = tiles[0] if first else weight
     local_experts, _, hid = hidden.shape
-    steps, model_width, tile = tiles_first.shape
+    steps = tiles.shape[0] // local_experts
+    model_width, tile = tiles.shape[1:]
     width = block.shape[1] - model_width
     expert_rows = cores * capacity
     slot_count = local_experts * expert_rows
@@ -119,10 +110,10 @@
         copies = [
             pltpu.make_async_copy(
                 weight.at[l, :, pl.ds(n * tile, tile)],
-                tiles_rest.at[(l - 1) * steps + n],
-                sems.at[2 + (l - 1) * steps + n],
+                tiles.at[l * steps + n],
+                sems.at[2 + l * steps + n],
             )
-            for l in range(1, local_experts)
+            for l in range(local_experts)
             for n in range(steps)
         ]
     loads = []
@@ -186,11 +177,12 @@
             jnp.where(iota(table.shape, 0) == seeds[l, 1], table, 0.0), axis=0, keepdims=True
         )
         for n in range(steps):
-            if first and l > 0:
-                copies[(l - 1) * steps + n].wait()
-            tile_in = tiles_rest[(l - 1) * steps + n] if l > 0 else tiles_first[n]
+            if first:
+                copies[l * steps + n].wait()
             up_act = jnp.dot(
-                slots[mine, :model_width], tile_in, preferred_element_type=jnp.float32
+                slots[mine, :model_width],
+                tiles[l * steps + n],
+                preferred_element_type=jnp.float32,
             )
             here = slice(n * tile, (n + 1) * tile)
             up_act = jnp.maximum(up_act + low_rank * right_row[:, here], 0.0)
@@ -288,29 +280,26 @@
     params = pltpu.CompilerParams(vmem_limit_bytes=VMEM_LIMIT)
     vmem, hbm = (pl.BlockSpec(memory_space=space) for space in (pltpu.VMEM, pltpu.HBM))
     up_steps = 3 if hid % (3 * LANES) == 0 else 1
-    up_tiles = (up_steps, model_width, hid // up_steps)
+    up_tiles = (local_experts * up_steps, model_width, hid // up_steps)
 
     prep = pl.pallas_call(
         functools.partial(prep_kernel, experts_all, parts),
-        out_shape=[jax.ShapeDtypeStruct((rows, packed), jnp.bfloat16)] * parts
-        + [jax.ShapeDtypeStruct(up_tiles, jnp.bfloat16)],
-        in_specs=[hbm] * 5,
-        out_specs=[vmem] * (parts + 1),
+        out_shape=[jax.ShapeDtypeStruct((rows, packed), jnp.bfloat16)] * parts,
+        in_specs=[hbm] * 4,
+        out_specs=[vmem] * parts,
         scratch_shapes=[
             pltpu.VMEM((top_count, tok_count), jnp.int32),
             pltpu.VMEM((top_count, tok_count), jnp.float32),
             pltpu.VMEM(tokens.shape, jnp.bfloat16),
             pltpu.VMEM(up_left.shape, jnp.bfloat16),
             pltpu.VMEM((tok_count, width), jnp.bfloat16),
-            pltpu.SemaphoreType.DMA((4 + up_steps,)),
+            pltpu.SemaphoreType.DMA((4,)),
         ],
         compiler_params=params,
         name="pack_tokens",
     )
 
     splits = 2 if rows % 32 == 0 else 1
-    up_rest = ((local_experts - 1) * up_steps,) + up_tiles[1:]
-
     down_steps = 3 if out_width % 48 == 0 else 1
     down_tiles = (local_experts * down_steps, out_width // down_steps, hid_all)
 
@@ -323,10 +312,10 @@
                 jax.ShapeDtypeStruct((local_experts, expert_rows, hid), jnp.bfloat16),
                 jax.ShapeDtypeStruct((all_tokens, slot_count), jnp.bfloat16),
             ]
-            + [jax.ShapeDtypeStruct(up_rest, jnp.bfloat16)] * first
+            + [jax.ShapeDtypeStruct(up_tiles, jnp.bfloat16)] * first
             + [jax.ShapeDtypeStruct(down_tiles, jnp.bfloat16)] * load,
             in_specs=[vmem] * count
-            + [vmem, hbm if first else vmem, hbm, hbm]
+            + [hbm if first else vmem, hbm, hbm]
             + [hbm] * load,
             out_specs=[vmem] * (2 + first + load),
             scratch_shapes=[
@@ -334,7 +323,7 @@
                 pltpu.VMEM((slot_count, packed), jnp.bfloat16),
                 pltpu.VMEM(up_right.shape, jnp.bfloat16),
                 pltpu.SMEM(factor_seeds.shape, jnp.int32),
-                pltpu.SemaphoreType.DMA((2 + (local_experts - 1) * up_steps + down_tiles[0],)),
+                pltpu.SemaphoreType.DMA((2 + up_tiles[0] + down_tiles[0],)),
             ],
             compiler_params=params,
             name="up",
@@ -369,7 +358,7 @@
         )
     ]
     up_weight, up_right, down_turned, down_left, down_right, seeds = in_hbm[4:]
-    *pieces, tiles_first = prep(*in_hbm[:5])
+    pieces = list(prep(*in_hbm[:4]))
     kept = {}
 
     last = [pieces[0]]
@@ -396,7 +385,6 @@
         hidden, gate, *tiles = up(first, load, len(blocks))(
             order(blocks[0]),
             *blocks[1:],
-            tiles_first,
             up_weight if first else kept["up"],
             up_right,
             seeds,

time: 88.1 us -> 87.5 us (level)
  waiting for transfers between devices: 32.5 us -> 30.4 us
    ppermute x38, waiting for transfers between devices: 32.5 us -> 30.4 us  [shift(): lax.ppermute(value, axis, [(i, (i + by) % size) for i in range(size)])]
    pallas_call x4, Pallas kernels: 13.2 us -> 14.6 us  [up_only(): up(first, load, len(blocks))]
  transfers between devices with their start and end apart: 38 -> 38, of which waited for: 21 -> 21; matrix products, arithmetic and copies ran while one was open for 0% -> 0% of each run, Pallas kernels for 32% -> 34%
where the time goes in v5:
time: 87.5 us; the launch traced here: 87 us
  Pallas kernels  32.6 us (37%)
  waiting for transfers between devices  30.4 us (35%)
  starting transfers between devices  23.5 us (27%)
    ppermute x38, waiting for transfers between devices, shift(): lax.ppermute(value, axis, [(i, (i + by) % size) for i in range(size)])  30.4 us
    ppermute x38, starting transfers between devices, shift(): lax.ppermute(value, axis, [(i, (i + by) % size) for i in range(size)])  23.5 us
    pallas_call x4, Pallas kernels, run_down(): down(*hiddens[:-1], order(hiddens[-1]), kept['down'], down_left, down_rig...  14.9 us
    pallas_call x4, Pallas kernels, up_only(): up(first, load, len(blocks))  14.6 us
    pallas_call x1, Pallas kernels, on_device(): pieces = list(prep(*in_hbm[:4]))  1.97 us
  transfers between devices with their start and end apart: 38, of which 21 were waited for; matrix products, arithmetic and copies ran while one was open for 0% of the time, Pallas kernels for 34%

profile of v5, /device:TPU:0, one launch (start us, length us, event | category | flops | bytes accessed | tf_op | source)
XLA Modules:
  0.0 87.0 jit_solution(11618976613936080361)
XLA Ops:
  0.0 2.0 %pack_tokens.1 = (bf16[64,2816]{1,0:T(8,128)(2,1)S(1)}, bf16[64,2816]{1,0:T(8,128)(2,1)S(1)}) custom-call(s32[6,128]{1,0:T(8,128)} %bitcast.5, f32[6,128]{1,0:T(8,128)} %bitcast.6, bf16[128,2688]{1,0:T(8,128)(2,1)} %tokens.1, bf16[16,2688]{1,0:T(8,128)(2,1)} %up_left.1), custom_call_target="tpu_custom_call" | custom-call | tf_op jit(solution)/shard_map/pack_tokens/pallas_call | solution.py:361
  2.0 3.1 %collective-permute-start.4 = (bf16[64,2816]{1,0:T(8,128)(2,1)S(1)}, bf16[64,2816]{1,0:T(8,128)(2,1)S(1)}, u32[]{:S(2)}, u32[]{:S(2)}) collective-permute-start(bf16[64,2816]{1,0:T(8,128)(2,1)S(1)} %get-tuple-element.54.refs_0_), channel_id=1, source_target_pairs={{0,4},{4,8},{8,12},{12,0},{1,5},{5,9},{9,13},{13,1},{2,6},{6,10},{... | collective-permute-start | bytes 1081352 | tf_op jit(solution)/shard_map/ppermute | solution.py:18
  5.1 0.1 collective-permute-start
  5.2 0.5 collective-permute-start.1
  5.7 0.1 collective-permute-start.2
  5.8 0.4 collective-permute-start.3
  6.3 0.3 collective-permute-done.refs_2_
  6.6 2.0 %collective-permute-start.6 = (bf16[32,2816]{1,0:T(8,128)(2,1)S(1)}, bf16[32,2816]{1,0:T(8,128)(2,1)S(1)}, u32[]{:S(2)}, u32[]{:S(2)}) collective-permute-start(bf16[32,2816]{1,0:T(8,128)(2,1)S(1)} %get-tuple-element.112), channel_id=1, source_target_pairs={{0,12},{4,0},{8,4},{12,8},{1,13},{5,1},{9,5},{13,9},{2,14},{6,2},{... | collective-permute-start | bytes 540680 | tf_op jit(solution)/shard_map/ppermute | solution.py:18
  8.6 6.4 %up.4 = (bf16[2,128,768]{2,1,0:T(8,128)(2,1)S(1)}, bf16[256,256]{1,0:T(8,128)(2,1)S(1)}, bf16[6,2688,256]{2,1,0:T(8,128)(2,1)S(1)}, bf16[6,448,1536]{2,1,0:T(8,128)(2,1)S(1)}) custom-call(bf16[64,2816]{1,0:T(8,128)(2,1)S(1)} %get-tuple-element.54.refs_0_, bf16[64,2816]{1,0:T(8,128)(2,1)S(1)} %get-tuple-element.55.refs_1_, ...), custom_call_target="tpu_custom_call" | custom-call | tf_op jit(solution)/shard_map/up/pallas_call | solution.py:385
  15.1 1.3 %collective-permute-done.4.refs_0_ = bf16[64,2816]{1,0:T(8,128)(2,1)S(1)} collective-permute-done((bf16[64,2816]{1,0:T(8,128)(2,1)S(1)}, bf16[64,2816]{1,0:T(8,128)(2,1)S(1)}, u32[]{:S(2)}, u32[]{:S(2)}) %collective-permute-start.4) | collective-permute-done | bytes 360480 | tf_op jit(solution)/shard_map/ppermute | solution.py:18
  16.4 1.7 %collective-permute-start.9 = (bf16[64,2816]{1,0:T(8,128)(2,1)S(1)}, bf16[64,2816]{1,0:T(8,128)(2,1)S(1)}, u32[]{:S(2)}, u32[]{:S(2)}) collective-permute-start(bf16[64,2816]{1,0:T(8,128)(2,1)S(1)} %collective-permute-done.4.refs_0_), channel_id=1, source_target_pairs={{0,2},{2,0},{1,3},{3,1},{4,6},{6,4},{5,7},{7,5},{8,10},{10,8},{9,1... | collective-permute-start | bytes 1081352 | tf_op jit(solution)/shard_map/ppermute | solution.py:18
  18.1 1.2 %collective-permute-done.6.refs_1_ = bf16[32,2816]{1,0:T(8,128)(2,1)S(1)} collective-permute-done((bf16[32,2816]{1,0:T(8,128)(2,1)S(1)}, bf16[32,2816]{1,0:T(8,128)(2,1)S(1)}, u32[]{:S(2)}, u32[]{:S(2)}) %collective-permute-start.6) | collective-permute-done | bytes 180256 | tf_op jit(solution)/shard_map/ppermute | solution.py:18
  19.4 0.1 collective-permute-start.10
  19.5 0.5 collective-permute-start.11
  20.0 7.2 %collective-permute-done.5.refs_0_ = bf16[64,2816]{1,0:T(8,128)(2,1)S(1)} collective-permute-done((bf16[64,2816]{1,0:T(8,128)(2,1)S(1)}, bf16[64,2816]{1,0:T(8,128)(2,1)S(1)}, u32[]{:S(2)}, u32[]{:S(2)}) %collective-permute-start.5) | collective-permute-done | bytes 360480 | tf_op jit(solution)/shard_map/ppermute | solution.py:18
  27.1 1.7 %collective-permute-start.8 = (bf16[64,2816]{1,0:T(8,128)(2,1)S(1)}, bf16[64,2816]{1,0:T(8,128)(2,1)S(1)}, u32[]{:S(2)}, u32[]{:S(2)}) collective-permute-start(bf16[64,2816]{1,0:T(8,128)(2,1)S(1)} %collective-permute-done.5.refs_0_), channel_id=1, source_target_pairs={{0,2},{2,0},{1,3},{3,1},{4,6},{6,4},{5,7},{7,5},{8,10},{10,8},{9,1... | collective-permute-start | bytes 1081352 | tf_op jit(solution)/shard_map/ppermute | solution.py:18
  28.8 0.1 collective-permute-start.12
  28.9 0.5 collective-permute-start.13
  29.5 0.1 collective-permute-start.14
  29.7 0.6 collective-permute-done.12.refs_4_
  30.3 0.1 collective-permute-start.15
  30.5 0.1 collective-permute-done.13.refs_5_
  30.6 2.7 %up.5 = (bf16[2,128,768]{2,1,0:T(8,128)(2,1)S(1)}, bf16[256,256]{1,0:T(8,128)(2,1)S(1)}) custom-call(bf16[64,2816]{1,0:T(8,128)(2,1)S(1)} %collective-permute-done.4.refs_0_, bf16[64,2816]{1,0:T(8,128)(2,1)S(1)} %collective-permute-done.9.refs_1_, bf16[32,2816]{1,0:T(8,128)(2,1)S(1)} %collective-permute-done.10.refs_2_, ...), custom_call_target="tpu_custom_call" | custom-call | tf_op jit(solution)/shard_map/up/pallas_call | solution.py:385
  33.3 1.6 %collective-permute-done.8.refs_1_ = bf16[64,2816]{1,0:T(8,128)(2,1)S(1)} collective-permute-done((bf16[64,2816]{1,0:T(8,128)(2,1)S(1)}, bf16[64,2816]{1,0:T(8,128)(2,1)S(1)}, u32[]{:S(2)}, u32[]{:S(2)}) %collective-permute-start.8) | collective-permute-done | bytes 360480 | tf_op jit(solution)/shard_map/ppermute | solution.py:18
  34.9 0.1 collective-permute-start.16
  35.0 0.5 collective-permute-start.17
  35.5 0.1 collective-permute-start.21
  35.6 1.9 %collective-permute-start.18 = (bf16[32,2816]{1,0:T(8,128)(2,1)S(1)}, bf16[32,2816]{1,0:T(8,128)(2,1)S(1)}, u32[]{:S(2)}, u32[]{:S(2)}) collective-permute-start(bf16[32,2816]{1,0:T(8,128)(2,1)S(1)} %get-tuple-element.69), channel_id=1, source_target_pairs={{0,12},{4,0},{8,4},{12,8},{1,13},{5,1},{9,5},{13,9},{2,14},{6,2},{... | collective-permute-start | bytes 540680 | tf_op jit(solution)/shard_map/ppermute | solution.py:18
  37.4 1.7 %collective-permute-start.25 = (bf16[2,128,768]{2,1,0:T(8,128)(2,1)S(1)}, bf16[2,128,768]{2,1,0:T(8,128)(2,1)S(1)}, u32[]{:S(2)}, u32[]{:S(2)}) collective-permute-start(bf16[2,128,768]{2,1,0:T(8,128)(2,1)S(1)} %get-tuple-element.75.refs_0_), channel_id=1, source_target_pairs={{0,2},{2,0},{1,3},{3,1},{4,6},{6,4},{5,7},{7,5},{8,10},{10,8},{9,1... | collective-permute-start | bytes 1179656 | tf_op jit(solution)/shard_map/ppermute | solution.py:18
  39.1 2.7 %up.6 = (bf16[2,128,768]{2,1,0:T(8,128)(2,1)S(1)}, bf16[256,256]{1,0:T(8,128)(2,1)S(1)}) custom-call(bf16[64,2816]{1,0:T(8,128)(2,1)S(1)} %collective-permute-done.5.refs_0_, bf16[64,2816]{1,0:T(8,128)(2,1)S(1)} %collective-permute-done.8.refs_1_, bf16[32,2816]{1,0:T(8,128)(2,1)S(1)} %collective-permute-done.14.refs_2_, ...), custom_call_target="tpu_custom_call" | custom-call | tf_op jit(solution)/shard_map/up/pallas_call | solution.py:385
  41.8 0.7 collective-permute-done.7.refs_0_
  42.6 0.3 collective-permute-start.29
  42.9 0.1 collective-permute-start.19
  43.0 2.5 %collective-permute-done.18.refs_2_ = bf16[32,2816]{1,0:T(8,128)(2,1)S(1)} collective-permute-done((bf16[32,2816]{1,0:T(8,128)(2,1)S(1)}, bf16[32,2816]{1,0:T(8,128)(2,1)S(1)}, u32[]{:S(2)}, u32[]{:S(2)}) %collective-permute-start.18) | collective-permute-done | bytes 180256 | tf_op jit(solution)/shard_map/ppermute | solution.py:18
  45.6 0.5 collective-permute-start.22
  46.1 0.9 %collective-permute-done.20.refs_4_ = bf16[32,2816]{1,0:T(8,128)(2,1)S(1)} collective-permute-done((bf16[32,2816]{1,0:T(8,128)(2,1)S(1)}, bf16[32,2816]{1,0:T(8,128)(2,1)S(1)}, u32[]{:S(2)}, u32[]{:S(2)}) %collective-permute-start.20) | collective-permute-done | bytes 180256 | tf_op jit(solution)/shard_map/ppermute | solution.py:18
  47.0 0.3 collective-permute-done.22.refs_6_
  47.2 2.7 %up.7 = (bf16[2,128,768]{2,1,0:T(8,128)(2,1)S(1)}, bf16[256,256]{1,0:T(8,128)(2,1)S(1)}) custom-call(bf16[64,2816]{1,0:T(8,128)(2,1)S(1)} %collective-permute-done.7.refs_0_, bf16[32,2816]{1,0:T(8,128)(2,1)S(1)} %collective-permute-done.6.refs_1_, bf16[32,2816]{1,0:T(8,128)(2,1)S(1)} %collective-permute-done.18.refs_2_, ...), custom_call_target="tpu_custom_call" | custom-call | tf_op jit(solution)/shard_map/up/pallas_call | solution.py:385
  50.0 3.7 %down.4 = (f32[1344,128]{1,0:T(8,128)S(1)}, bf16[672,128]{1,0:T(8,128)(2,1)S(1)}, bf16[672,128]{1,0:T(8,128)(2,1)S(1)}) custom-call(bf16[2,128,768]{2,1,0:T(8,128)(2,1)S(1)} %get-tuple-element.75.refs_0_, bf16[2,128,768]{2,1,0:T(8,128)(2,1)S(1)} %collective-permute-done.25.refs_1_, bf16[6,448,1536]{2,1,0:T(8,128)(2,1)S(1)} %get-tuple-element.77.refs_2_, ...), custom_call_target="tpu_custom_call" | custom-call | tf_op jit(solution)/shard_map/down/pallas_call | solution.py:406
  53.7 0.3 collective-permute-start.26
  54.0 0.3 collective-permute-start.27
  54.3 1.1 %collective-permute-start.24 = (bf16[2,128,768]{2,1,0:T(8,128)(2,1)S(1)}, bf16[2,128,768]{2,1,0:T(8,128)(2,1)S(1)}, u32[]{:S(2)}, u32[]{:S(2)}) collective-permute-start(bf16[2,128,768]{2,1,0:T(8,128)(2,1)S(1)} %get-tuple-element.74.refs_0_), channel_id=1, source_target_pairs={{0,2},{2,0},{1,3},{3,1},{4,6},{6,4},{5,7},{7,5},{8,10},{10,8},{9,1... | collective-permute-start | bytes 1179656 | tf_op jit(solution)/shard_map/ppermute | solution.py:18
  55.5 1.0 %collective-permute-start.28 = (bf16[1344,128]{1,0:T(8,128)(2,1)S(1)}, bf16[1344,128]{1,0:T(8,128)(2,1)S(1)}, u32[]{:S(2)}, u32[]{:S(2)}) collective-permute-start(bf16[1344,128]{1,0:T(8,128)(2,1)S(1)} %add.4), channel_id=1, source_target_pairs={{0,12},{4,0},{8,4},{12,8},{1,13},{5,1},{9,5},{13,9},{2,14},{6,2},{... | collective-permute-start | bytes 1032200 | tf_op jit(solution)/shard_map/ppermute | solution.py:18
  56.5 0.3 collective-permute-done.29.refs_1_
  56.9 3.7 %down.5 = (f32[1344,128]{1,0:T(8,128)S(1)}, bf16[672,128]{1,0:T(8,128)(2,1)S(1)}, bf16[672,128]{1,0:T(8,128)(2,1)S(1)}) custom-call(bf16[2,128,768]{2,1,0:T(8,128)(2,1)S(1)} %get-tuple-element.83.refs_0_, bf16[2,128,768]{2,1,0:T(8,128)(2,1)S(1)} %collective-permute-done.29.refs_1_, bf16[6,448,1536]{2,1,0:T(8,128)(2,1)S(1)} %get-tuple-element.77.refs_2_, ...), custom_call_target="tpu_custom_call" | custom-call | tf_op jit(solution)/shard_map/down/pallas_call | solution.py:406
  60.7 0.5 collective-permute-start.31
  61.2 0.9 %collective-permute-done.30.refs_0_ = bf16[672,128]{1,0:T(8,128)(2,1)S(1)} collective-permute-done((bf16[672,128]{1,0:T(8,128)(2,1)S(1)}, bf16[672,128]{1,0:T(8,128)(2,1)S(1)}, u32[]{:S(2)}, u32[]{:S(2)}) %collective-permute-start.30) | collective-permute-done | bytes 172064 | tf_op jit(solution)/shard_map/ppermute | solution.py:18
  62.1 0.2 collective-permute-done.31.refs_1_
  62.4 1.0 %collective-permute-start.34 = (bf16[1344,128]{1,0:T(8,128)(2,1)S(1)}, bf16[1344,128]{1,0:T(8,128)(2,1)S(1)}, u32[]{:S(2)}, u32[]{:S(2)}) collective-permute-start(bf16[1344,128]{1,0:T(8,128)(2,1)S(1)} %add.5), channel_id=1, source_target_pairs={{0,4},{4,8},{8,12},{12,0},{1,5},{5,9},{9,13},{13,1},{2,6},{6,10},{... | collective-permute-start | bytes 1032200 | tf_op jit(solution)/shard_map/ppermute | solution.py:18
  63.4 1.8 %collective-permute-start.23 = (bf16[2,128,768]{2,1,0:T(8,128)(2,1)S(1)}, bf16[2,128,768]{2,1,0:T(8,128)(2,1)S(1)}, u32[]{:S(2)}, u32[]{:S(2)}) collective-permute-start(bf16[2,128,768]{2,1,0:T(8,128)(2,1)S(1)} %get-tuple-element.73.refs_0_), channel_id=1, source_target_pairs={{0,2},{2,0},{1,3},{3,1},{4,6},{6,4},{5,7},{7,5},{8,10},{10,8},{9,1... | collective-permute-start | bytes 1179656 | tf_op jit(solution)/shard_map/ppermute | solution.py:18
  65.1 0.6 collective-permute-done.28.refs_2_
  65.8 3.7 %down.6 = (f32[1344,128]{1,0:T(8,128)S(1)}, bf16[672,128]{1,0:T(8,128)(2,1)S(1)}, bf16[672,128]{1,0:T(8,128)(2,1)S(1)}) custom-call(bf16[2,128,768]{2,1,0:T(8,128)(2,1)S(1)} %get-tuple-element.74.refs_0_, bf16[2,128,768]{2,1,0:T(8,128)(2,1)S(1)} %collective-permute-done.24.refs_1_, bf16[6,448,1536]{2,1,0:T(8,128)(2,1)S(1)} %get-tuple-element.77.refs_2_, ...), custom_call_target="tpu_custom_call" | custom-call | tf_op jit(solution)/shard_map/down/pallas_call | solution.py:406
  69.6 0.5 collective-permute-start.33
  70.1 0.9 %collective-permute-done.32.refs_0_ = bf16[672,128]{1,0:T(8,128)(2,1)S(1)} collective-permute-done((bf16[672,128]{1,0:T(8,128)(2,1)S(1)}, bf16[672,128]{1,0:T(8,128)(2,1)S(1)}, u32[]{:S(2)}, u32[]{:S(2)}) %collective-permute-start.32) | collective-permute-done | bytes 172064 | tf_op jit(solution)/shard_map/ppermute | solution.py:18
  71.0 0.2 collective-permute-done.33.refs_1_
  71.2 3.5 %collective-permute-done.34.refs_2_ = bf16[1344,128]{1,0:T(8,128)(2,1)S(1)} collective-permute-done((bf16[1344,128]{1,0:T(8,128)(2,1)S(1)}, bf16[1344,128]{1,0:T(8,128)(2,1)S(1)}, u32[]{:S(2)}, u32[]{:S(2)}) %collective-permute-start.34) | collective-permute-done | bytes 344096 | tf_op jit(solution)/shard_map/ppermute | solution.py:18
  74.7 0.1 add.6
  74.9 3.7 %down.7 = (f32[1344,128]{1,0:T(8,128)S(1)}, bf16[672,128]{1,0:T(8,128)(2,1)S(1)}, bf16[672,128]{1,0:T(8,128)(2,1)S(1)}) custom-call(bf16[2,128,768]{2,1,0:T(8,128)(2,1)S(1)} %get-tuple-element.73.refs_0_, bf16[2,128,768]{2,1,0:T(8,128)(2,1)S(1)} %collective-permute-done.23.refs_1_, bf16[6,448,1536]{2,1,0:T(8,128)(2,1)S(1)} %get-tuple-element.77.refs_2_, ...), custom_call_target="tpu_custom_call" | custom-call | tf_op jit(solution)/shard_map/down/pallas_call | solution.py:406
  78.6 0.1 collective-permute-start.35
  78.7 0.5 collective-permute-start.36
  79.2 0.9 %collective-permute-done.35.refs_0_ = bf16[672,128]{1,0:T(8,128)(2,1)S(1)} collective-permute-done((bf16[672,128]{1,0:T(8,128)(2,1)S(1)}, bf16[672,128]{1,0:T(8,128)(2,1)S(1)}, u32[]{:S(2)}, u32[]{:S(2)}) %collective-permute-start.35) | collective-permute-done | bytes 172064 | tf_op jit(solution)/shard_map/ppermute | solution.py:18
  80.1 0.2 collective-permute-done.36.refs_1_
  80.4 5.7 %collective-permute-done.37.refs_3_ = bf16[1344,128]{1,0:T(8,128)(2,1)S(1)} collective-permute-done((bf16[1344,128]{1,0:T(8,128)(2,1)S(1)}, bf16[1344,128]{1,0:T(8,128)(2,1)S(1)}, u32[]{:S(2)}, u32[]{:S(2)}) %collective-permute-start.37) | collective-permute-done | bytes 344096 | tf_op jit(solution)/shard_map/ppermute | solution.py:18
  86.1 0.9 %add.7 = bf16[1344,128]{1,0:T(8,128)(2,1)} custom-call(f32[1344,128]{1,0:T(8,128)S(1)} %get-tuple-element.98.own, bf16[672,128]{1,0:T(8,128)(2,1)S(1)} %collective-permute-done.35.refs_0_, bf16[672,128]{1,0:T(8,128)(2,1)S(1)} %collective-permute-done.36.refs_1_, bf16[1344,128]{1,0:T(8,128)(2,1)S(1)} %collective-permute-done.28.refs_2_, ...), custom_call_target="tpu_custom_call" | custom-call | flops 1 | bytes 1 | tf_op jit(solution)/shard_map/add/pallas_call | solution.py:439
  (32 shorter events, 0.7 us)
Async XLA Ops:
  2.0 14.4 %collective-permute-start.4 = (bf16[64,2816]{1,0:T(8,128)(2,1)S(1)}, bf16[64,2816]{1,0:T(8,128)(2,1)S(1)}, u32[]{:S(2)}, u32[]{:S(2)}) collective-permute-start(bf16[64,2816]{1,0:T(8,128)(2,1)S(1)} %get-tuple-element.54.refs_0_), channel_id=1, source_target_pairs={{0,4},{4,8},{8,12},{12,0},{1,5},{5,9},{9,13},{13,1},{2,6},{6,10},{... | collective-permute-start | bytes 1081352 | tf_op jit(solution)/shard_map/ppermute | solution.py:18
  5.1 1.5 %collective-permute-start = (bf16[32,2816]{1,0:T(8,128)(2,1)S(1)}, bf16[32,2816]{1,0:T(8,128)(2,1)S(1)}, u32[]{:S(2)}, u32[]{:S(2)}) collective-permute-start(bf16[32,2816]{1,0:T(8,128)(2,1)S(1)} %get-tuple-element.114), channel_id=1, source_target_pairs={{0,1},{1,0},{2,3},{3,2},{4,5},{5,4},{6,7},{7,6},{8,9},{9,8},{10,11... | collective-permute-start | bytes 540680 | tf_op jit(solution)/shard_map/ppermute | solution.py:18
  5.2 3.5 %collective-permute-start.1 = (bf16[32,2816]{1,0:T(8,128)(2,1)S(1)}, bf16[32,2816]{1,0:T(8,128)(2,1)S(1)}, u32[]{:S(2)}, u32[]{:S(2)}) collective-permute-start(bf16[32,2816]{1,0:T(8,128)(2,1)S(1)} %get-tuple-element.113), channel_id=1, source_target_pairs={{0,1},{1,0},{2,3},{3,2},{4,5},{5,4},{6,7},{7,6},{8,9},{9,8},{10,11... | collective-permute-start | bytes 540680 | tf_op jit(solution)/shard_map/ppermute | solution.py:18
  5.7 2.9 %collective-permute-start.2 = (bf16[32,2816]{1,0:T(8,128)(2,1)S(1)}, bf16[32,2816]{1,0:T(8,128)(2,1)S(1)}, u32[]{:S(2)}, u32[]{:S(2)}) collective-permute-start(bf16[32,2816]{1,0:T(8,128)(2,1)S(1)} %get-tuple-element.112), channel_id=1, source_target_pairs={{0,1},{1,0},{2,3},{3,2},{4,5},{5,4},{6,7},{7,6},{8,9},{9,8},{10,11... | collective-permute-start | bytes 540680 | tf_op jit(solution)/shard_map/ppermute | solution.py:18
  5.8 2.8 %collective-permute-start.3 = (bf16[32,2816]{1,0:T(8,128)(2,1)S(1)}, bf16[32,2816]{1,0:T(8,128)(2,1)S(1)}, u32[]{:S(2)}, u32[]{:S(2)}) collective-permute-start(bf16[32,2816]{1,0:T(8,128)(2,1)S(1)} %get-tuple-element.69), channel_id=1, source_target_pairs={{0,1},{1,0},{2,3},{3,2},{4,5},{5,4},{6,7},{7,6},{8,9},{9,8},{10,11... | collective-permute-start | bytes 540680 | tf_op jit(solution)/shard_map/ppermute | solution.py:18
  6.6 12.8 %collective-permute-start.6 = (bf16[32,2816]{1,0:T(8,128)(2,1)S(1)}, bf16[32,2816]{1,0:T(8,128)(2,1)S(1)}, u32[]{:S(2)}, u32[]{:S(2)}) collective-permute-start(bf16[32,2816]{1,0:T(8,128)(2,1)S(1)} %get-tuple-element.112), channel_id=1, source_target_pairs={{0,12},{4,0},{8,4},{12,8},{1,13},{5,1},{9,5},{13,9},{2,14},{6,2},{... | collective-permute-start | bytes 540680 | tf_op jit(solution)/shard_map/ppermute | solution.py:18
  16.4 10.8 %collective-permute-start.5 = (bf16[64,2816]{1,0:T(8,128)(2,1)S(1)}, bf16[64,2816]{1,0:T(8,128)(2,1)S(1)}, u32[]{:S(2)}, u32[]{:S(2)}) collective-permute-start(bf16[64,2816]{1,0:T(8,128)(2,1)S(1)} %collective-permute-done.4.refs_0_), channel_id=1, source_target_pairs={{0,4},{4,8},{8,12},{12,0},{1,5},{5,9},{9,13},{13,1},{2,6},{6,10},{... | collective-permute-start | bytes 1081352 | tf_op jit(solution)/shard_map/ppermute | solution.py:18
  16.4 12.4 %collective-permute-start.9 = (bf16[64,2816]{1,0:T(8,128)(2,1)S(1)}, bf16[64,2816]{1,0:T(8,128)(2,1)S(1)}, u32[]{:S(2)}, u32[]{:S(2)}) collective-permute-start(bf16[64,2816]{1,0:T(8,128)(2,1)S(1)} %collective-permute-done.4.refs_0_), channel_id=1, source_target_pairs={{0,2},{2,0},{1,3},{3,1},{4,6},{6,4},{5,7},{7,5},{8,10},{10,8},{9,1... | collective-permute-start | bytes 1081352 | tf_op jit(solution)/shard_map/ppermute | solution.py:18
  19.4 10.1 %collective-permute-start.10 = (bf16[32,2816]{1,0:T(8,128)(2,1)S(1)}, bf16[32,2816]{1,0:T(8,128)(2,1)S(1)}, u32[]{:S(2)}, u32[]{:S(2)}) collective-permute-start(bf16[32,2816]{1,0:T(8,128)(2,1)S(1)} %get-tuple-element.110), channel_id=1, source_target_pairs={{0,1},{1,0},{2,3},{3,2},{4,5},{5,4},{6,7},{7,6},{8,9},{9,8},{10,11... | collective-permute-start | bytes 540680 | tf_op jit(solution)/shard_map/ppermute | solution.py:18
  19.5 10.0 %collective-permute-start.11 = (bf16[32,2816]{1,0:T(8,128)(2,1)S(1)}, bf16[32,2816]{1,0:T(8,128)(2,1)S(1)}, u32[]{:S(2)}, u32[]{:S(2)}) collective-permute-start(bf16[32,2816]{1,0:T(8,128)(2,1)S(1)} %get-tuple-element.109), channel_id=1, source_target_pairs={{0,1},{1,0},{2,3},{3,2},{4,5},{5,4},{6,7},{7,6},{8,9},{9,8},{10,11... | collective-permute-start | bytes 540680 | tf_op jit(solution)/shard_map/ppermute | solution.py:18
  27.1 7.8 %collective-permute-start.8 = (bf16[64,2816]{1,0:T(8,128)(2,1)S(1)}, bf16[64,2816]{1,0:T(8,128)(2,1)S(1)}, u32[]{:S(2)}, u32[]{:S(2)}) collective-permute-start(bf16[64,2816]{1,0:T(8,128)(2,1)S(1)} %collective-permute-done.5.refs_0_), channel_id=1, source_target_pairs={{0,2},{2,0},{1,3},{3,1},{4,6},{6,4},{5,7},{7,5},{8,10},{10,8},{9,1... | collective-permute-start | bytes 1081352 | tf_op jit(solution)/shard_map/ppermute | solution.py:18
  28.8 1.5 %collective-permute-start.12 = (bf16[32,2816]{1,0:T(8,128)(2,1)S(1)}, bf16[32,2816]{1,0:T(8,128)(2,1)S(1)}, u32[]{:S(2)}, u32[]{:S(2)}) collective-permute-start(bf16[32,2816]{1,0:T(8,128)(2,1)S(1)} %get-tuple-element.108), channel_id=1, source_target_pairs={{0,1},{1,0},{2,3},{3,2},{4,5},{5,4},{6,7},{7,6},{8,9},{9,8},{10,11... | collective-permute-start | bytes 540680 | tf_op jit(solution)/shard_map/ppermute | solution.py:18
  28.9 1.7 %collective-permute-start.13 = (bf16[32,2816]{1,0:T(8,128)(2,1)S(1)}, bf16[32,2816]{1,0:T(8,128)(2,1)S(1)}, u32[]{:S(2)}, u32[]{:S(2)}) collective-permute-start(bf16[32,2816]{1,0:T(8,128)(2,1)S(1)} %get-tuple-element.107), channel_id=1, source_target_pairs={{0,1},{1,0},{2,3},{3,2},{4,5},{5,4},{6,7},{7,6},{8,9},{9,8},{10,11... | collective-permute-start | bytes 540680 | tf_op jit(solution)/shard_map/ppermute | solution.py:18
  29.5 13.1 %collective-permute-start.7 = (bf16[64,2816]{1,0:T(8,128)(2,1)S(1)}, bf16[64,2816]{1,0:T(8,128)(2,1)S(1)}, u32[]{:S(2)}, u32[]{:S(2)}) collective-permute-start(bf16[64,2816]{1,0:T(8,128)(2,1)S(1)} %collective-permute-done.5.refs_0_), channel_id=1, source_target_pairs={{0,4},{4,8},{8,12},{12,0},{1,5},{5,9},{9,13},{13,1},{2,6},{6,10},{... | collective-permute-start | bytes 1081352 | tf_op jit(solution)/shard_map/ppermute | solution.py:18
  29.5 6.0 %collective-permute-start.14 = (bf16[32,2816]{1,0:T(8,128)(2,1)S(1)}, bf16[32,2816]{1,0:T(8,128)(2,1)S(1)}, u32[]{:S(2)}, u32[]{:S(2)}) collective-permute-start(bf16[32,2816]{1,0:T(8,128)(2,1)S(1)} %get-tuple-element.106), channel_id=1, source_target_pairs={{0,1},{1,0},{2,3},{3,2},{4,5},{5,4},{6,7},{7,6},{8,9},{9,8},{10,11... | collective-permute-start | bytes 540680 | tf_op jit(solution)/shard_map/ppermute | solution.py:18
  30.3 5.3 %collective-permute-start.15 = (bf16[32,2816]{1,0:T(8,128)(2,1)S(1)}, bf16[32,2816]{1,0:T(8,128)(2,1)S(1)}, u32[]{:S(2)}, u32[]{:S(2)}) collective-permute-start(bf16[32,2816]{1,0:T(8,128)(2,1)S(1)} %get-tuple-element.105), channel_id=1, source_target_pairs={{0,1},{1,0},{2,3},{3,2},{4,5},{5,4},{6,7},{7,6},{8,9},{9,8},{10,11... | collective-permute-start | bytes 540680 | tf_op jit(solution)/shard_map/ppermute | solution.py:18
  34.9 2.5 %collective-permute-start.16 = (bf16[32,2816]{1,0:T(8,128)(2,1)S(1)}, bf16[32,2816]{1,0:T(8,128)(2,1)S(1)}, u32[]{:S(2)}, u32[]{:S(2)}) collective-permute-start(bf16[32,2816]{1,0:T(8,128)(2,1)S(1)} %get-tuple-element.104), channel_id=1, source_target_pairs={{0,1},{1,0},{2,3},{3,2},{4,5},{5,4},{6,7},{7,6},{8,9},{9,8},{10,11... | collective-permute-start | bytes 540680 | tf_op jit(solution)/shard_map/ppermute | solution.py:18
  35.0 4.1 %collective-permute-start.17 = (bf16[32,2816]{1,0:T(8,128)(2,1)S(1)}, bf16[32,2816]{1,0:T(8,128)(2,1)S(1)}, u32[]{:S(2)}, u32[]{:S(2)}) collective-permute-start(bf16[32,2816]{1,0:T(8,128)(2,1)S(1)} %get-tuple-element.103), channel_id=1, source_target_pairs={{0,1},{1,0},{2,3},{3,2},{4,5},{5,4},{6,7},{7,6},{8,9},{9,8},{10,11... | collective-permute-start | bytes 540680 | tf_op jit(solution)/shard_map/ppermute | solution.py:18
  35.5 10.1 %collective-permute-start.21 = (bf16[32,2816]{1,0:T(8,128)(2,1)S(1)}, bf16[32,2816]{1,0:T(8,128)(2,1)S(1)}, u32[]{:S(2)}, u32[]{:S(2)}) collective-permute-start(bf16[32,2816]{1,0:T(8,128)(2,1)S(1)} %collective-permute-done.6.refs_1_), channel_id=1, source_target_pairs={{0,1},{1,0},{2,3},{3,2},{4,5},{5,4},{6,7},{7,6},{8,9},{9,8},{10,11... | collective-permute-start | bytes 540680 | tf_op jit(solution)/shard_map/ppermute | solution.py:18
  35.6 10.0 %collective-permute-start.18 = (bf16[32,2816]{1,0:T(8,128)(2,1)S(1)}, bf16[32,2816]{1,0:T(8,128)(2,1)S(1)}, u32[]{:S(2)}, u32[]{:S(2)}) collective-permute-start(bf16[32,2816]{1,0:T(8,128)(2,1)S(1)} %get-tuple-element.69), channel_id=1, source_target_pairs={{0,12},{4,0},{8,4},{12,8},{1,13},{5,1},{9,5},{13,9},{2,14},{6,2},{... | collective-permute-start | bytes 540680 | tf_op jit(solution)/shard_map/ppermute | solution.py:18
  37.4 12.5 %collective-permute-start.25 = (bf16[2,128,768]{2,1,0:T(8,128)(2,1)S(1)}, bf16[2,128,768]{2,1,0:T(8,128)(2,1)S(1)}, u32[]{:S(2)}, u32[]{:S(2)}) collective-permute-start(bf16[2,128,768]{2,1,0:T(8,128)(2,1)S(1)} %get-tuple-element.75.refs_0_), channel_id=1, source_target_pairs={{0,2},{2,0},{1,3},{3,1},{4,6},{6,4},{5,7},{7,5},{8,10},{10,8},{9,1... | collective-permute-start | bytes 1179656 | tf_op jit(solution)/shard_map/ppermute | solution.py:18
  42.6 14.3 %collective-permute-start.29 = (bf16[2,128,768]{2,1,0:T(8,128)(2,1)S(1)}, bf16[2,128,768]{2,1,0:T(8,128)(2,1)S(1)}, u32[]{:S(2)}, u32[]{:S(2)}) collective-permute-start(bf16[2,128,768]{2,1,0:T(8,128)(2,1)S(1)} %get-tuple-element.83.refs_0_), channel_id=1, source_target_pairs={{0,2},{2,0},{1,3},{3,1},{4,6},{6,4},{5,7},{7,5},{8,10},{10,8},{9,1... | collective-permute-start | bytes 1179656 | tf_op jit(solution)/shard_map/ppermute | solution.py:18
  42.9 3.1 %collective-permute-start.19 = (bf16[32,2816]{1,0:T(8,128)(2,1)S(1)}, bf16[32,2816]{1,0:T(8,128)(2,1)S(1)}, u32[]{:S(2)}, u32[]{:S(2)}) collective-permute-start(bf16[32,2816]{1,0:T(8,128)(2,1)S(1)} %get-tuple-element.102), channel_id=1, source_target_pairs={{0,1},{1,0},{2,3},{3,2},{4,5},{5,4},{6,7},{7,6},{8,9},{9,8},{10,11... | collective-permute-start | bytes 540680 | tf_op jit(solution)/shard_map/ppermute | solution.py:18
  45.6 1.4 %collective-permute-start.20 = (bf16[32,2816]{1,0:T(8,128)(2,1)S(1)}, bf16[32,2816]{1,0:T(8,128)(2,1)S(1)}, u32[]{:S(2)}, u32[]{:S(2)}) collective-permute-start(bf16[32,2816]{1,0:T(8,128)(2,1)S(1)} %get-tuple-element.101), channel_id=1, source_target_pairs={{0,1},{1,0},{2,3},{3,2},{4,5},{5,4},{6,7},{7,6},{8,9},{9,8},{10,11... | collective-permute-start | bytes 540680 | tf_op jit(solution)/shard_map/ppermute | solution.py:18
  45.6 1.6 %collective-permute-start.22 = (bf16[32,2816]{1,0:T(8,128)(2,1)S(1)}, bf16[32,2816]{1,0:T(8,128)(2,1)S(1)}, u32[]{:S(2)}, u32[]{:S(2)}) collective-permute-start(bf16[32,2816]{1,0:T(8,128)(2,1)S(1)} %collective-permute-done.18.refs_2_), channel_id=1, source_target_pairs={{0,1},{1,0},{2,3},{3,2},{4,5},{5,4},{6,7},{7,6},{8,9},{9,8},{10,11... | collective-permute-start | bytes 540680 | tf_op jit(solution)/shard_map/ppermute | solution.py:18
  53.7 1.7 %collective-permute-start.26 = (bf16[672,128]{1,0:T(8,128)(2,1)S(1)}, bf16[672,128]{1,0:T(8,128)(2,1)S(1)}, u32[]{:S(2)}, u32[]{:S(2)}) collective-permute-start(bf16[672,128]{1,0:T(8,128)(2,1)S(1)} %get-tuple-element.80), channel_id=1, source_target_pairs={{0,1},{1,0},{2,3},{3,2},{4,5},{5,4},{6,7},{7,6},{8,9},{9,8},{10,11... | collective-permute-start | bytes 516104 | tf_op jit(solution)/shard_map/ppermute | solution.py:18
  54.0 1.4 %collective-permute-start.27 = (bf16[672,128]{1,0:T(8,128)(2,1)S(1)}, bf16[672,128]{1,0:T(8,128)(2,1)S(1)}, u32[]{:S(2)}, u32[]{:S(2)}) collective-permute-start(bf16[672,128]{1,0:T(8,128)(2,1)S(1)} %get-tuple-element.81), channel_id=1, source_target_pairs={{0,1},{1,0},{2,3},{3,2},{4,5},{5,4},{6,7},{7,6},{8,9},{9,8},{10,11... | collective-permute-start | bytes 516104 | tf_op jit(solution)/shard_map/ppermute | solution.py:18
  54.3 11.5 %collective-permute-start.24 = (bf16[2,128,768]{2,1,0:T(8,128)(2,1)S(1)}, bf16[2,128,768]{2,1,0:T(8,128)(2,1)S(1)}, u32[]{:S(2)}, u32[]{:S(2)}) collective-permute-start(bf16[2,128,768]{2,1,0:T(8,128)(2,1)S(1)} %get-tuple-element.74.refs_0_), channel_id=1, source_target_pairs={{0,2},{2,0},{1,3},{3,1},{4,6},{6,4},{5,7},{7,5},{8,10},{10,8},{9,1... | collective-permute-start | bytes 1179656 | tf_op jit(solution)/shard_map/ppermute | solution.py:18
  55.5 10.3 %collective-permute-start.28 = (bf16[1344,128]{1,0:T(8,128)(2,1)S(1)}, bf16[1344,128]{1,0:T(8,128)(2,1)S(1)}, u32[]{:S(2)}, u32[]{:S(2)}) collective-permute-start(bf16[1344,128]{1,0:T(8,128)(2,1)S(1)} %add.4), channel_id=1, source_target_pairs={{0,12},{4,0},{8,4},{12,8},{1,13},{5,1},{9,5},{13,9},{2,14},{6,2},{... | collective-permute-start | bytes 1032200 | tf_op jit(solution)/shard_map/ppermute | solution.py:18
  60.6 1.5 %collective-permute-start.30 = (bf16[672,128]{1,0:T(8,128)(2,1)S(1)}, bf16[672,128]{1,0:T(8,128)(2,1)S(1)}, u32[]{:S(2)}, u32[]{:S(2)}) collective-permute-start(bf16[672,128]{1,0:T(8,128)(2,1)S(1)} %get-tuple-element.87), channel_id=1, source_target_pairs={{0,1},{1,0},{2,3},{3,2},{4,5},{5,4},{6,7},{7,6},{8,9},{9,8},{10,11... | collective-permute-start | bytes 516104 | tf_op jit(solution)/shard_map/ppermute | solution.py:18
  60.7 1.6 %collective-permute-start.31 = (bf16[672,128]{1,0:T(8,128)(2,1)S(1)}, bf16[672,128]{1,0:T(8,128)(2,1)S(1)}, u32[]{:S(2)}, u32[]{:S(2)}) collective-permute-start(bf16[672,128]{1,0:T(8,128)(2,1)S(1)} %get-tuple-element.88), channel_id=1, source_target_pairs={{0,1},{1,0},{2,3},{3,2},{4,5},{5,4},{6,7},{7,6},{8,9},{9,8},{10,11... | collective-permute-start | bytes 516104 | tf_op jit(solution)/shard_map/ppermute | solution.py:18
  62.4 12.3 %collective-permute-start.34 = (bf16[1344,128]{1,0:T(8,128)(2,1)S(1)}, bf16[1344,128]{1,0:T(8,128)(2,1)S(1)}, u32[]{:S(2)}, u32[]{:S(2)}) collective-permute-start(bf16[1344,128]{1,0:T(8,128)(2,1)S(1)} %add.5), channel_id=1, source_target_pairs={{0,4},{4,8},{8,12},{12,0},{1,5},{5,9},{9,13},{13,1},{2,6},{6,10},{... | collective-permute-start | bytes 1032200 | tf_op jit(solution)/shard_map/ppermute | solution.py:18
  63.4 11.5 %collective-permute-start.23 = (bf16[2,128,768]{2,1,0:T(8,128)(2,1)S(1)}, bf16[2,128,768]{2,1,0:T(8,128)(2,1)S(1)}, u32[]{:S(2)}, u32[]{:S(2)}) collective-permute-start(bf16[2,128,768]{2,1,0:T(8,128)(2,1)S(1)} %get-tuple-element.73.refs_0_), channel_id=1, source_target_pairs={{0,2},{2,0},{1,3},{3,1},{4,6},{6,4},{5,7},{7,5},{8,10},{10,8},{9,1... | collective-permute-start | bytes 1179656 | tf_op jit(solution)/shard_map/ppermute | solution.py:18
  69.5 1.5 %collective-permute-start.32 = (bf16[672,128]{1,0:T(8,128)(2,1)S(1)}, bf16[672,128]{1,0:T(8,128)(2,1)S(1)}, u32[]{:S(2)}, u32[]{:S(2)}) collective-permute-start(bf16[672,128]{1,0:T(8,128)(2,1)S(1)} %get-tuple-element.94), channel_id=1, source_target_pairs={{0,1},{1,0},{2,3},{3,2},{4,5},{5,4},{6,7},{7,6},{8,9},{9,8},{10,11... | collective-permute-start | bytes 516104 | tf_op jit(solution)/shard_map/ppermute | solution.py:18
  69.6 1.6 %collective-permute-start.33 = (bf16[672,128]{1,0:T(8,128)(2,1)S(1)}, bf16[672,128]{1,0:T(8,128)(2,1)S(1)}, u32[]{:S(2)}, u32[]{:S(2)}) collective-permute-start(bf16[672,128]{1,0:T(8,128)(2,1)S(1)} %get-tuple-element.95), channel_id=1, source_target_pairs={{0,1},{1,0},{2,3},{3,2},{4,5},{5,4},{6,7},{7,6},{8,9},{9,8},{10,11... | collective-permute-start | bytes 516104 | tf_op jit(solution)/shard_map/ppermute | solution.py:18
  74.8 11.3 %collective-permute-start.37 = (bf16[1344,128]{1,0:T(8,128)(2,1)S(1)}, bf16[1344,128]{1,0:T(8,128)(2,1)S(1)}, u32[]{:S(2)}, u32[]{:S(2)}) collective-permute-start(bf16[1344,128]{1,0:T(8,128)(2,1)S(1)} %add.6), channel_id=1, source_target_pairs={{0,4},{4,8},{8,12},{12,0},{1,5},{5,9},{9,13},{13,1},{2,6},{6,10},{... | collective-permute-start | bytes 1032200 | tf_op jit(solution)/shard_map/ppermute | solution.py:18
  78.6 1.5 %collective-permute-start.35 = (bf16[672,128]{1,0:T(8,128)(2,1)S(1)}, bf16[672,128]{1,0:T(8,128)(2,1)S(1)}, u32[]{:S(2)}, u32[]{:S(2)}) collective-permute-start(bf16[672,128]{1,0:T(8,128)(2,1)S(1)} %get-tuple-element.99), channel_id=1, source_target_pairs={{0,1},{1,0},{2,3},{3,2},{4,5},{5,4},{6,7},{7,6},{8,9},{9,8},{10,11... | collective-permute-start | bytes 516104 | tf_op jit(solution)/shard_map/ppermute | solution.py:18
  78.7 1.6 %collective-permute-start.36 = (bf16[672,128]{1,0:T(8,128)(2,1)S(1)}, bf16[672,128]{1,0:T(8,128)(2,1)S(1)}, u32[]{:S(2)}, u32[]{:S(2)}) collective-permute-start(bf16[672,128]{1,0:T(8,128)(2,1)S(1)} %get-tuple-element.100), channel_id=1, source_target_pairs={{0,1},{1,0},{2,3},{3,2},{4,5},{5,4},{6,7},{7,6},{8,9},{9,8},{10,11... | collective-permute-start | bytes 516104 | tf_op jit(solution)/shard_map/ppermute | solution.py:18

commit v6 on v5

--- a/solution.py
+++ b/solution.py
@@ -137,29 +137,26 @@
     owner = first_expert(local_experts) + slot // expert_rows
     place_of = (column == owner).astype(jnp.bfloat16)
     gate_of = (column == owner + experts_all).astype(jnp.bfloat16)
-    lane = iota((tok_count, slot_count), 1)
+    lane = iota((cores * tok_count, slot_count), 1)
     wanted = lax.rem(lane, capacity).astype(jnp.float32)
+    same_core = lax.rem(lane, expert_rows) // capacity == iota(lane.shape, 0) // tok_count
     base = 0
     for piece in pieces:
         block[base : base + piece.shape[0], :] = piece[...]
         base += piece.shape[0]
-    choosers = []
+    info = block[:, model_width:]
+    slot_of = jnp.dot(info, place_of, preferred_element_type=jnp.float32)
+    here = (slot_of == wanted) & same_core
+    slots[...] = lax.dot_general(
+        here.astype(jnp.bfloat16), block[...], TN, preferred_element_type=jnp.float32
+    ).astype(jnp.bfloat16)
+    gate = jnp.dot(info, gate_of, preferred_element_type=jnp.float32)
+    gate = jnp.where(here, gate, 0.0).astype(jnp.bfloat16)
     for b in range(cores):
-        base = b * tok_count
-        info = block[base : base + tok_count, model_width:]
-        slot_of = jnp.dot(info, place_of, preferred_element_type=jnp.float32)
-        gate = jnp.dot(info, gate_of, preferred_element_type=jnp.float32)
-        here = (slot_of == wanted) & (lax.rem(lane, expert_rows) // capacity == b)
-        gate = jnp.where(here, gate, 0.0).astype(jnp.bfloat16)
         for j in range(parts):
-            at = lax.rem(my_part() - j + parts, parts) * rows
-            gate_out[pl.ds(pl.multiple_of(base + at, rows), rows), :] = gate[
-                j * rows : (j + 1) * rows, :
-            ]
-        choosers.append(here.astype(jnp.bfloat16))
-    slots[...] = lax.dot_general(
-        jnp.concatenate(choosers, axis=0), block[...], TN, preferred_element_type=jnp.float32
-    ).astype(jnp.bfloat16)
+            base = b * tok_count + j * rows
+            at = b * tok_count + lax.rem(my_part() - j + parts, parts) * rows
+            gate_out[pl.ds(pl.multiple_of(at, rows), rows), :] = gate[base : base + rows, :]
 
     for copy in tables:
         copy.wait()

time: 87.5 us -> 87.5 us (level)
  no operation moved by 1% of the time
where the time goes in v6:
time: 87.5 us; the launch traced here: 87 us
  Pallas kernels  32.5 us (37%)
  waiting for transfers between devices  30.5 us (35%)
  starting transfers between devices  23.6 us (27%)
    ppermute x38, waiting for transfers between devices, shift(): lax.ppermute(value, axis, [(i, (i + by) % size) for i in range(size)])  30.5 us
    ppermute x38, starting transfers between devices, shift(): lax.ppermute(value, axis, [(i, (i + by) % size) for i in range(size)])  23.6 us
    pallas_call x4, Pallas kernels, run_down(): down(*hiddens[:-1], order(hiddens[-1]), kept['down'], down_left, down_rig...  14.9 us
    pallas_call x4, Pallas kernels, up_only(): up(first, load, len(blocks))  14.5 us
    pallas_call x1, Pallas kernels, on_device(): pieces = list(prep(*in_hbm[:4]))  1.97 us
  transfers between devices with their start and end apart: 38, of which 21 were waited for; matrix products, arithmetic and copies ran while one was open for 0% of the time, Pallas kernels for 34%

profile of v6, /device:TPU:0, one launch (start us, length us, event | category | flops | bytes accessed | tf_op | source)
XLA Modules:
  0.0 87.0 jit_solution(8696756515985663815)
XLA Ops:
  0.0 2.0 %pack_tokens.1 = (bf16[64,2816]{1,0:T(8,128)(2,1)S(1)}, bf16[64,2816]{1,0:T(8,128)(2,1)S(1)}) custom-call(s32[6,128]{1,0:T(8,128)} %bitcast.5, f32[6,128]{1,0:T(8,128)} %bitcast.6, bf16[128,2688]{1,0:T(8,128)(2,1)} %tokens.1, bf16[16,2688]{1,0:T(8,128)(2,1)} %up_left.1), custom_call_target="tpu_custom_call" | custom-call | tf_op jit(solution)/shard_map/pack_tokens/pallas_call | solution.py:358
  2.0 3.1 %collective-permute-start.4 = (bf16[64,2816]{1,0:T(8,128)(2,1)S(1)}, bf16[64,2816]{1,0:T(8,128)(2,1)S(1)}, u32[]{:S(2)}, u32[]{:S(2)}) collective-permute-start(bf16[64,2816]{1,0:T(8,128)(2,1)S(1)} %get-tuple-element.54.refs_0_), channel_id=1, source_target_pairs={{0,4},{4,8},{8,12},{12,0},{1,5},{5,9},{9,13},{13,1},{2,6},{6,10},{... | collective-permute-start | bytes 1081352 | tf_op jit(solution)/shard_map/ppermute | solution.py:18
  5.1 0.1 collective-permute-start
  5.2 0.5 collective-permute-start.1
  5.7 0.1 collective-permute-start.2
  5.8 0.4 collective-permute-start.3
  6.3 0.3 collective-permute-done.refs_2_
  6.6 2.0 %collective-permute-start.6 = (bf16[32,2816]{1,0:T(8,128)(2,1)S(1)}, bf16[32,2816]{1,0:T(8,128)(2,1)S(1)}, u32[]{:S(2)}, u32[]{:S(2)}) collective-permute-start(bf16[32,2816]{1,0:T(8,128)(2,1)S(1)} %get-tuple-element.112), channel_id=1, source_target_pairs={{0,12},{4,0},{8,4},{12,8},{1,13},{5,1},{9,5},{13,9},{2,14},{6,2},{... | collective-permute-start | bytes 540680 | tf_op jit(solution)/shard_map/ppermute | solution.py:18
  8.6 6.4 %up.4 = (bf16[2,128,768]{2,1,0:T(8,128)(2,1)S(1)}, bf16[256,256]{1,0:T(8,128)(2,1)S(1)}, bf16[6,2688,256]{2,1,0:T(8,128)(2,1)S(1)}, bf16[6,448,1536]{2,1,0:T(8,128)(2,1)S(1)}) custom-call(bf16[64,2816]{1,0:T(8,128)(2,1)S(1)} %get-tuple-element.54.refs_0_, bf16[64,2816]{1,0:T(8,128)(2,1)S(1)} %get-tuple-element.55.refs_1_, ...), custom_call_target="tpu_custom_call" | custom-call | tf_op jit(solution)/shard_map/up/pallas_call | solution.py:382
  15.1 1.3 %collective-permute-done.4.refs_0_ = bf16[64,2816]{1,0:T(8,128)(2,1)S(1)} collective-permute-done((bf16[64,2816]{1,0:T(8,128)(2,1)S(1)}, bf16[64,2816]{1,0:T(8,128)(2,1)S(1)}, u32[]{:S(2)}, u32[]{:S(2)}) %collective-permute-start.4) | collective-permute-done | bytes 360480 | tf_op jit(solution)/shard_map/ppermute | solution.py:18
  16.4 1.7 %collective-permute-start.9 = (bf16[64,2816]{1,0:T(8,128)(2,1)S(1)}, bf16[64,2816]{1,0:T(8,128)(2,1)S(1)}, u32[]{:S(2)}, u32[]{:S(2)}) collective-permute-start(bf16[64,2816]{1,0:T(8,128)(2,1)S(1)} %collective-permute-done.4.refs_0_), channel_id=1, source_target_pairs={{0,2},{2,0},{1,3},{3,1},{4,6},{6,4},{5,7},{7,5},{8,10},{10,8},{9,1... | collective-permute-start | bytes 1081352 | tf_op jit(solution)/shard_map/ppermute | solution.py:18
  18.1 1.2 %collective-permute-done.6.refs_1_ = bf16[32,2816]{1,0:T(8,128)(2,1)S(1)} collective-permute-done((bf16[32,2816]{1,0:T(8,128)(2,1)S(1)}, bf16[32,2816]{1,0:T(8,128)(2,1)S(1)}, u32[]{:S(2)}, u32[]{:S(2)}) %collective-permute-start.6) | collective-permute-done | bytes 180256 | tf_op jit(solution)/shard_map/ppermute | solution.py:18
  19.4 0.1 collective-permute-start.10
  19.5 0.5 collective-permute-start.11
  20.0 7.2 %collective-permute-done.5.refs_0_ = bf16[64,2816]{1,0:T(8,128)(2,1)S(1)} collective-permute-done((bf16[64,2816]{1,0:T(8,128)(2,1)S(1)}, bf16[64,2816]{1,0:T(8,128)(2,1)S(1)}, u32[]{:S(2)}, u32[]{:S(2)}) %collective-permute-start.5) | collective-permute-done | bytes 360480 | tf_op jit(solution)/shard_map/ppermute | solution.py:18
  27.1 1.7 %collective-permute-start.8 = (bf16[64,2816]{1,0:T(8,128)(2,1)S(1)}, bf16[64,2816]{1,0:T(8,128)(2,1)S(1)}, u32[]{:S(2)}, u32[]{:S(2)}) collective-permute-start(bf16[64,2816]{1,0:T(8,128)(2,1)S(1)} %collective-permute-done.5.refs_0_), channel_id=1, source_target_pairs={{0,2},{2,0},{1,3},{3,1},{4,6},{6,4},{5,7},{7,5},{8,10},{10,8},{9,1... | collective-permute-start | bytes 1081352 | tf_op jit(solution)/shard_map/ppermute | solution.py:18
  28.8 0.1 collective-permute-start.12
  28.9 0.5 collective-permute-start.13
  29.5 0.1 collective-permute-start.14
  29.7 0.6 collective-permute-done.12.refs_4_
  30.3 0.1 collective-permute-start.15
  30.5 0.1 collective-permute-done.13.refs_5_
  30.6 2.7 %up.5 = (bf16[2,128,768]{2,1,0:T(8,128)(2,1)S(1)}, bf16[256,256]{1,0:T(8,128)(2,1)S(1)}) custom-call(bf16[64,2816]{1,0:T(8,128)(2,1)S(1)} %collective-permute-done.4.refs_0_, bf16[64,2816]{1,0:T(8,128)(2,1)S(1)} %collective-permute-done.9.refs_1_, bf16[32,2816]{1,0:T(8,128)(2,1)S(1)} %collective-permute-done.10.refs_2_, ...), custom_call_target="tpu_custom_call" | custom-call | tf_op jit(solution)/shard_map/up/pallas_call | solution.py:382
  33.3 1.6 %collective-permute-done.8.refs_1_ = bf16[64,2816]{1,0:T(8,128)(2,1)S(1)} collective-permute-done((bf16[64,2816]{1,0:T(8,128)(2,1)S(1)}, bf16[64,2816]{1,0:T(8,128)(2,1)S(1)}, u32[]{:S(2)}, u32[]{:S(2)}) %collective-permute-start.8) | collective-permute-done | bytes 360480 | tf_op jit(solution)/shard_map/ppermute | solution.py:18
  34.9 0.1 collective-permute-start.16
  35.0 0.5 collective-permute-start.17
  35.5 0.1 collective-permute-start.21
  35.6 1.8 %collective-permute-start.18 = (bf16[32,2816]{1,0:T(8,128)(2,1)S(1)}, bf16[32,2816]{1,0:T(8,128)(2,1)S(1)}, u32[]{:S(2)}, u32[]{:S(2)}) collective-permute-start(bf16[32,2816]{1,0:T(8,128)(2,1)S(1)} %get-tuple-element.69), channel_id=1, source_target_pairs={{0,12},{4,0},{8,4},{12,8},{1,13},{5,1},{9,5},{13,9},{2,14},{6,2},{... | collective-permute-start | bytes 540680 | tf_op jit(solution)/shard_map/ppermute | solution.py:18
  37.4 1.7 %collective-permute-start.25 = (bf16[2,128,768]{2,1,0:T(8,128)(2,1)S(1)}, bf16[2,128,768]{2,1,0:T(8,128)(2,1)S(1)}, u32[]{:S(2)}, u32[]{:S(2)}) collective-permute-start(bf16[2,128,768]{2,1,0:T(8,128)(2,1)S(1)} %get-tuple-element.75.refs_0_), channel_id=1, source_target_pairs={{0,2},{2,0},{1,3},{3,1},{4,6},{6,4},{5,7},{7,5},{8,10},{10,8},{9,1... | collective-permute-start | bytes 1179656 | tf_op jit(solution)/shard_map/ppermute | solution.py:18
  39.1 2.7 %up.6 = (bf16[2,128,768]{2,1,0:T(8,128)(2,1)S(1)}, bf16[256,256]{1,0:T(8,128)(2,1)S(1)}) custom-call(bf16[64,2816]{1,0:T(8,128)(2,1)S(1)} %collective-permute-done.5.refs_0_, bf16[64,2816]{1,0:T(8,128)(2,1)S(1)} %collective-permute-done.8.refs_1_, bf16[32,2816]{1,0:T(8,128)(2,1)S(1)} %collective-permute-done.14.refs_2_, ...), custom_call_target="tpu_custom_call" | custom-call | tf_op jit(solution)/shard_map/up/pallas_call | solution.py:382
  41.8 0.7 collective-permute-done.7.refs_0_
  42.6 0.3 collective-permute-start.29
  43.0 2.5 %collective-permute-done.18.refs_2_ = bf16[32,2816]{1,0:T(8,128)(2,1)S(1)} collective-permute-done((bf16[32,2816]{1,0:T(8,128)(2,1)S(1)}, bf16[32,2816]{1,0:T(8,128)(2,1)S(1)}, u32[]{:S(2)}, u32[]{:S(2)}) %collective-permute-start.18) | collective-permute-done | bytes 180256 | tf_op jit(solution)/shard_map/ppermute | solution.py:18
  45.6 0.5 collective-permute-start.22
  46.1 0.9 %collective-permute-done.20.refs_4_ = bf16[32,2816]{1,0:T(8,128)(2,1)S(1)} collective-permute-done((bf16[32,2816]{1,0:T(8,128)(2,1)S(1)}, bf16[32,2816]{1,0:T(8,128)(2,1)S(1)}, u32[]{:S(2)}, u32[]{:S(2)}) %collective-permute-start.20) | collective-permute-done | bytes 180256 | tf_op jit(solution)/shard_map/ppermute | solution.py:18
  47.0 0.3 collective-permute-done.22.refs_6_
  47.2 2.7 %up.7 = (bf16[2,128,768]{2,1,0:T(8,128)(2,1)S(1)}, bf16[256,256]{1,0:T(8,128)(2,1)S(1)}) custom-call(bf16[64,2816]{1,0:T(8,128)(2,1)S(1)} %collective-permute-done.7.refs_0_, bf16[32,2816]{1,0:T(8,128)(2,1)S(1)} %collective-permute-done.6.refs_1_, bf16[32,2816]{1,0:T(8,128)(2,1)S(1)} %collective-permute-done.18.refs_2_, ...), custom_call_target="tpu_custom_call" | custom-call | tf_op jit(solution)/shard_map/up/pallas_call | solution.py:382
  49.9 3.7 %down.4 = (f32[1344,128]{1,0:T(8,128)S(1)}, bf16[672,128]{1,0:T(8,128)(2,1)S(1)}, bf16[672,128]{1,0:T(8,128)(2,1)S(1)}) custom-call(bf16[2,128,768]{2,1,0:T(8,128)(2,1)S(1)} %get-tuple-element.75.refs_0_, bf16[2,128,768]{2,1,0:T(8,128)(2,1)S(1)} %collective-permute-done.25.refs_1_, bf16[6,448,1536]{2,1,0:T(8,128)(2,1)S(1)} %get-tuple-element.77.refs_2_, ...), custom_call_target="tpu_custom_call" | custom-call | tf_op jit(solution)/shard_map/down/pallas_call | solution.py:403
  53.7 0.3 collective-permute-start.26
  54.0 0.3 collective-permute-start.27
  54.3 1.2 %collective-permute-start.24 = (bf16[2,128,768]{2,1,0:T(8,128)(2,1)S(1)}, bf16[2,128,768]{2,1,0:T(8,128)(2,1)S(1)}, u32[]{:S(2)}, u32[]{:S(2)}) collective-permute-start(bf16[2,128,768]{2,1,0:T(8,128)(2,1)S(1)} %get-tuple-element.74.refs_0_), channel_id=1, source_target_pairs={{0,2},{2,0},{1,3},{3,1},{4,6},{6,4},{5,7},{7,5},{8,10},{10,8},{9,1... | collective-permute-start | bytes 1179656 | tf_op jit(solution)/shard_map/ppermute | solution.py:18
  55.5 1.0 %collective-permute-start.28 = (bf16[1344,128]{1,0:T(8,128)(2,1)S(1)}, bf16[1344,128]{1,0:T(8,128)(2,1)S(1)}, u32[]{:S(2)}, u32[]{:S(2)}) collective-permute-start(bf16[1344,128]{1,0:T(8,128)(2,1)S(1)} %add.4), channel_id=1, source_target_pairs={{0,12},{4,0},{8,4},{12,8},{1,13},{5,1},{9,5},{13,9},{2,14},{6,2},{... | collective-permute-start | bytes 1032200 | tf_op jit(solution)/shard_map/ppermute | solution.py:18
  56.5 0.3 collective-permute-done.29.refs_1_
  56.9 3.7 %down.5 = (f32[1344,128]{1,0:T(8,128)S(1)}, bf16[672,128]{1,0:T(8,128)(2,1)S(1)}, bf16[672,128]{1,0:T(8,128)(2,1)S(1)}) custom-call(bf16[2,128,768]{2,1,0:T(8,128)(2,1)S(1)} %get-tuple-element.83.refs_0_, bf16[2,128,768]{2,1,0:T(8,128)(2,1)S(1)} %collective-permute-done.29.refs_1_, bf16[6,448,1536]{2,1,0:T(8,128)(2,1)S(1)} %get-tuple-element.77.refs_2_, ...), custom_call_target="tpu_custom_call" | custom-call | tf_op jit(solution)/shard_map/down/pallas_call | solution.py:403
  60.6 0.1 collective-permute-start.30
  60.7 0.5 collective-permute-start.31
  61.2 0.9 %collective-permute-done.30.refs_0_ = bf16[672,128]{1,0:T(8,128)(2,1)S(1)} collective-permute-done((bf16[672,128]{1,0:T(8,128)(2,1)S(1)}, bf16[672,128]{1,0:T(8,128)(2,1)S(1)}, u32[]{:S(2)}, u32[]{:S(2)}) %collective-permute-start.30) | collective-permute-done | bytes 172064 | tf_op jit(solution)/shard_map/ppermute | solution.py:18
  62.1 0.2 collective-permute-done.31.refs_1_
  62.4 1.0 %collective-permute-start.34 = (bf16[1344,128]{1,0:T(8,128)(2,1)S(1)}, bf16[1344,128]{1,0:T(8,128)(2,1)S(1)}, u32[]{:S(2)}, u32[]{:S(2)}) collective-permute-start(bf16[1344,128]{1,0:T(8,128)(2,1)S(1)} %add.5), channel_id=1, source_target_pairs={{0,4},{4,8},{8,12},{12,0},{1,5},{5,9},{9,13},{13,1},{2,6},{6,10},{... | collective-permute-start | bytes 1032200 | tf_op jit(solution)/shard_map/ppermute | solution.py:18
  63.4 1.8 %collective-permute-start.23 = (bf16[2,128,768]{2,1,0:T(8,128)(2,1)S(1)}, bf16[2,128,768]{2,1,0:T(8,128)(2,1)S(1)}, u32[]{:S(2)}, u32[]{:S(2)}) collective-permute-start(bf16[2,128,768]{2,1,0:T(8,128)(2,1)S(1)} %get-tuple-element.73.refs_0_), channel_id=1, source_target_pairs={{0,2},{2,0},{1,3},{3,1},{4,6},{6,4},{5,7},{7,5},{8,10},{10,8},{9,1... | collective-permute-start | bytes 1179656 | tf_op jit(solution)/shard_map/ppermute | solution.py:18
  65.1 0.6 collective-permute-done.28.refs_2_
  65.8 3.7 %down.6 = (f32[1344,128]{1,0:T(8,128)S(1)}, bf16[672,128]{1,0:T(8,128)(2,1)S(1)}, bf16[672,128]{1,0:T(8,128)(2,1)S(1)}) custom-call(bf16[2,128,768]{2,1,0:T(8,128)(2,1)S(1)} %get-tuple-element.74.refs_0_, bf16[2,128,768]{2,1,0:T(8,128)(2,1)S(1)} %collective-permute-done.24.refs_1_, bf16[6,448,1536]{2,1,0:T(8,128)(2,1)S(1)} %get-tuple-element.77.refs_2_, ...), custom_call_target="tpu_custom_call" | custom-call | tf_op jit(solution)/shard_map/down/pallas_call | solution.py:403
  69.5 0.1 collective-permute-start.32
  69.6 0.5 collective-permute-start.33
  70.1 0.9 %collective-permute-done.32.refs_0_ = bf16[672,128]{1,0:T(8,128)(2,1)S(1)} collective-permute-done((bf16[672,128]{1,0:T(8,128)(2,1)S(1)}, bf16[672,128]{1,0:T(8,128)(2,1)S(1)}, u32[]{:S(2)}, u32[]{:S(2)}) %collective-permute-start.32) | collective-permute-done | bytes 172064 | tf_op jit(solution)/shard_map/ppermute | solution.py:18
  71.0 0.2 collective-permute-done.33.refs_1_
  71.2 3.5 %collective-permute-done.34.refs_2_ = bf16[1344,128]{1,0:T(8,128)(2,1)S(1)} collective-permute-done((bf16[1344,128]{1,0:T(8,128)(2,1)S(1)}, bf16[1344,128]{1,0:T(8,128)(2,1)S(1)}, u32[]{:S(2)}, u32[]{:S(2)}) %collective-permute-start.34) | collective-permute-done | bytes 344096 | tf_op jit(solution)/shard_map/ppermute | solution.py:18
  74.7 0.1 add.6
  74.9 3.7 %down.7 = (f32[1344,128]{1,0:T(8,128)S(1)}, bf16[672,128]{1,0:T(8,128)(2,1)S(1)}, bf16[672,128]{1,0:T(8,128)(2,1)S(1)}) custom-call(bf16[2,128,768]{2,1,0:T(8,128)(2,1)S(1)} %get-tuple-element.73.refs_0_, bf16[2,128,768]{2,1,0:T(8,128)(2,1)S(1)} %collective-permute-done.23.refs_1_, bf16[6,448,1536]{2,1,0:T(8,128)(2,1)S(1)} %get-tuple-element.77.refs_2_, ...), custom_call_target="tpu_custom_call" | custom-call | tf_op jit(solution)/shard_map/down/pallas_call | solution.py:403
  78.7 0.5 collective-permute-start.36
  79.2 0.9 %collective-permute-done.35.refs_0_ = bf16[672,128]{1,0:T(8,128)(2,1)S(1)} collective-permute-done((bf16[672,128]{1,0:T(8,128)(2,1)S(1)}, bf16[672,128]{1,0:T(8,128)(2,1)S(1)}, u32[]{:S(2)}, u32[]{:S(2)}) %collective-permute-start.35) | collective-permute-done | bytes 172064 | tf_op jit(solution)/shard_map/ppermute | solution.py:18
  80.1 0.2 collective-permute-done.36.refs_1_
  80.3 5.7 %collective-permute-done.37.refs_3_ = bf16[1344,128]{1,0:T(8,128)(2,1)S(1)} collective-permute-done((bf16[1344,128]{1,0:T(8,128)(2,1)S(1)}, bf16[1344,128]{1,0:T(8,128)(2,1)S(1)}, u32[]{:S(2)}, u32[]{:S(2)}) %collective-permute-start.37) | collective-permute-done | bytes 344096 | tf_op jit(solution)/shard_map/ppermute | solution.py:18
  86.1 0.9 %add.7 = bf16[1344,128]{1,0:T(8,128)(2,1)} custom-call(f32[1344,128]{1,0:T(8,128)S(1)} %get-tuple-element.98.own, bf16[672,128]{1,0:T(8,128)(2,1)S(1)} %collective-permute-done.35.refs_0_, bf16[672,128]{1,0:T(8,128)(2,1)S(1)} %collective-permute-done.36.refs_1_, bf16[1344,128]{1,0:T(8,128)(2,1)S(1)} %collective-permute-done.28.refs_2_, ...), custom_call_target="tpu_custom_call" | custom-call | flops 1 | bytes 1 | tf_op jit(solution)/shard_map/add/pallas_call | solution.py:436
  (32 shorter events, 0.6 us)
Async XLA Ops:
  2.0 14.4 %collective-permute-start.4 = (bf16[64,2816]{1,0:T(8,128)(2,1)S(1)}, bf16[64,2816]{1,0:T(8,128)(2,1)S(1)}, u32[]{:S(2)}, u32[]{:S(2)}) collective-permute-start(bf16[64,2816]{1,0:T(8,128)(2,1)S(1)} %get-tuple-element.54.refs_0_), channel_id=1, source_target_pairs={{0,4},{4,8},{8,12},{12,0},{1,5},{5,9},{9,13},{13,1},{2,6},{6,10},{... | collective-permute-start | bytes 1081352 | tf_op jit(solution)/shard_map/ppermute | solution.py:18
  5.1 1.5 %collective-permute-start = (bf16[32,2816]{1,0:T(8,128)(2,1)S(1)}, bf16[32,2816]{1,0:T(8,128)(2,1)S(1)}, u32[]{:S(2)}, u32[]{:S(2)}) collective-permute-start(bf16[32,2816]{1,0:T(8,128)(2,1)S(1)} %get-tuple-element.114), channel_id=1, source_target_pairs={{0,1},{1,0},{2,3},{3,2},{4,5},{5,4},{6,7},{7,6},{8,9},{9,8},{10,11... | collective-permute-start | bytes 540680 | tf_op jit(solution)/shard_map/ppermute | solution.py:18
  5.2 3.5 %collective-permute-start.1 = (bf16[32,2816]{1,0:T(8,128)(2,1)S(1)}, bf16[32,2816]{1,0:T(8,128)(2,1)S(1)}, u32[]{:S(2)}, u32[]{:S(2)}) collective-permute-start(bf16[32,2816]{1,0:T(8,128)(2,1)S(1)} %get-tuple-element.113), channel_id=1, source_target_pairs={{0,1},{1,0},{2,3},{3,2},{4,5},{5,4},{6,7},{7,6},{8,9},{9,8},{10,11... | collective-permute-start | bytes 540680 | tf_op jit(solution)/shard_map/ppermute | solution.py:18
  5.7 2.9 %collective-permute-start.2 = (bf16[32,2816]{1,0:T(8,128)(2,1)S(1)}, bf16[32,2816]{1,0:T(8,128)(2,1)S(1)}, u32[]{:S(2)}, u32[]{:S(2)}) collective-permute-start(bf16[32,2816]{1,0:T(8,128)(2,1)S(1)} %get-tuple-element.112), channel_id=1, source_target_pairs={{0,1},{1,0},{2,3},{3,2},{4,5},{5,4},{6,7},{7,6},{8,9},{9,8},{10,11... | collective-permute-start | bytes 540680 | tf_op jit(solution)/shard_map/ppermute | solution.py:18
  5.8 2.8 %collective-permute-start.3 = (bf16[32,2816]{1,0:T(8,128)(2,1)S(1)}, bf16[32,2816]{1,0:T(8,128)(2,1)S(1)}, u32[]{:S(2)}, u32[]{:S(2)}) collective-permute-start(bf16[32,2816]{1,0:T(8,128)(2,1)S(1)} %get-tuple-element.69), channel_id=1, source_target_pairs={{0,1},{1,0},{2,3},{3,2},{4,5},{5,4},{6,7},{7,6},{8,9},{9,8},{10,11... | collective-permute-start | bytes 540680 | tf_op jit(solution)/shard_map/ppermute | solution.py:18
  6.6 12.8 %collective-permute-start.6 = (bf16[32,2816]{1,0:T(8,128)(2,1)S(1)}, bf16[32,2816]{1,0:T(8,128)(2,1)S(1)}, u32[]{:S(2)}, u32[]{:S(2)}) collective-permute-start(bf16[32,2816]{1,0:T(8,128)(2,1)S(1)} %get-tuple-element.112), channel_id=1, source_target_pairs={{0,12},{4,0},{8,4},{12,8},{1,13},{5,1},{9,5},{13,9},{2,14},{6,2},{... | collective-permute-start | bytes 540680 | tf_op jit(solution)/shard_map/ppermute | solution.py:18
  16.4 10.8 %collective-permute-start.5 = (bf16[64,2816]{1,0:T(8,128)(2,1)S(1)}, bf16[64,2816]{1,0:T(8,128)(2,1)S(1)}, u32[]{:S(2)}, u32[]{:S(2)}) collective-permute-start(bf16[64,2816]{1,0:T(8,128)(2,1)S(1)} %collective-permute-done.4.refs_0_), channel_id=1, source_target_pairs={{0,4},{4,8},{8,12},{12,0},{1,5},{5,9},{9,13},{13,1},{2,6},{6,10},{... | collective-permute-start | bytes 1081352 | tf_op jit(solution)/shard_map/ppermute | solution.py:18
  16.4 12.4 %collective-permute-start.9 = (bf16[64,2816]{1,0:T(8,128)(2,1)S(1)}, bf16[64,2816]{1,0:T(8,128)(2,1)S(1)}, u32[]{:S(2)}, u32[]{:S(2)}) collective-permute-start(bf16[64,2816]{1,0:T(8,128)(2,1)S(1)} %collective-permute-done.4.refs_0_), channel_id=1, source_target_pairs={{0,2},{2,0},{1,3},{3,1},{4,6},{6,4},{5,7},{7,5},{8,10},{10,8},{9,1... | collective-permute-start | bytes 1081352 | tf_op jit(solution)/shard_map/ppermute | solution.py:18
  19.4 10.1 %collective-permute-start.10 = (bf16[32,2816]{1,0:T(8,128)(2,1)S(1)}, bf16[32,2816]{1,0:T(8,128)(2,1)S(1)}, u32[]{:S(2)}, u32[]{:S(2)}) collective-permute-start(bf16[32,2816]{1,0:T(8,128)(2,1)S(1)} %get-tuple-element.110), channel_id=1, source_target_pairs={{0,1},{1,0},{2,3},{3,2},{4,5},{5,4},{6,7},{7,6},{8,9},{9,8},{10,11... | collective-permute-start | bytes 540680 | tf_op jit(solution)/shard_map/ppermute | solution.py:18
  19.5 10.0 %collective-permute-start.11 = (bf16[32,2816]{1,0:T(8,128)(2,1)S(1)}, bf16[32,2816]{1,0:T(8,128)(2,1)S(1)}, u32[]{:S(2)}, u32[]{:S(2)}) collective-permute-start(bf16[32,2816]{1,0:T(8,128)(2,1)S(1)} %get-tuple-element.109), channel_id=1, source_target_pairs={{0,1},{1,0},{2,3},{3,2},{4,5},{5,4},{6,7},{7,6},{8,9},{9,8},{10,11... | collective-permute-start | bytes 540680 | tf_op jit(solution)/shard_map/ppermute | solution.py:18
  27.1 7.8 %collective-permute-start.8 = (bf16[64,2816]{1,0:T(8,128)(2,1)S(1)}, bf16[64,2816]{1,0:T(8,128)(2,1)S(1)}, u32[]{:S(2)}, u32[]{:S(2)}) collective-permute-start(bf16[64,2816]{1,0:T(8,128)(2,1)S(1)} %collective-permute-done.5.refs_0_), channel_id=1, source_target_pairs={{0,2},{2,0},{1,3},{3,1},{4,6},{6,4},{5,7},{7,5},{8,10},{10,8},{9,1... | collective-permute-start | bytes 1081352 | tf_op jit(solution)/shard_map/ppermute | solution.py:18
  28.8 1.5 %collective-permute-start.12 = (bf16[32,2816]{1,0:T(8,128)(2,1)S(1)}, bf16[32,2816]{1,0:T(8,128)(2,1)S(1)}, u32[]{:S(2)}, u32[]{:S(2)}) collective-permute-start(bf16[32,2816]{1,0:T(8,128)(2,1)S(1)} %get-tuple-element.108), channel_id=1, source_target_pairs={{0,1},{1,0},{2,3},{3,2},{4,5},{5,4},{6,7},{7,6},{8,9},{9,8},{10,11... | collective-permute-start | bytes 540680 | tf_op jit(solution)/shard_map/ppermute | solution.py:18
  28.9 1.7 %collective-permute-start.13 = (bf16[32,2816]{1,0:T(8,128)(2,1)S(1)}, bf16[32,2816]{1,0:T(8,128)(2,1)S(1)}, u32[]{:S(2)}, u32[]{:S(2)}) collective-permute-start(bf16[32,2816]{1,0:T(8,128)(2,1)S(1)} %get-tuple-element.107), channel_id=1, source_target_pairs={{0,1},{1,0},{2,3},{3,2},{4,5},{5,4},{6,7},{7,6},{8,9},{9,8},{10,11... | collective-permute-start | bytes 540680 | tf_op jit(solution)/shard_map/ppermute | solution.py:18
  29.4 13.1 %collective-permute-start.7 = (bf16[64,2816]{1,0:T(8,128)(2,1)S(1)}, bf16[64,2816]{1,0:T(8,128)(2,1)S(1)}, u32[]{:S(2)}, u32[]{:S(2)}) collective-permute-start(bf16[64,2816]{1,0:T(8,128)(2,1)S(1)} %collective-permute-done.5.refs_0_), channel_id=1, source_target_pairs={{0,4},{4,8},{8,12},{12,0},{1,5},{5,9},{9,13},{13,1},{2,6},{6,10},{... | collective-permute-start | bytes 1081352 | tf_op jit(solution)/shard_map/ppermute | solution.py:18
  29.5 6.0 %collective-permute-start.14 = (bf16[32,2816]{1,0:T(8,128)(2,1)S(1)}, bf16[32,2816]{1,0:T(8,128)(2,1)S(1)}, u32[]{:S(2)}, u32[]{:S(2)}) collective-permute-start(bf16[32,2816]{1,0:T(8,128)(2,1)S(1)} %get-tuple-element.106), channel_id=1, source_target_pairs={{0,1},{1,0},{2,3},{3,2},{4,5},{5,4},{6,7},{7,6},{8,9},{9,8},{10,11... | collective-permute-start | bytes 540680 | tf_op jit(solution)/shard_map/ppermute | solution.py:18
  30.3 5.3 %collective-permute-start.15 = (bf16[32,2816]{1,0:T(8,128)(2,1)S(1)}, bf16[32,2816]{1,0:T(8,128)(2,1)S(1)}, u32[]{:S(2)}, u32[]{:S(2)}) collective-permute-start(bf16[32,2816]{1,0:T(8,128)(2,1)S(1)} %get-tuple-element.105), channel_id=1, source_target_pairs={{0,1},{1,0},{2,3},{3,2},{4,5},{5,4},{6,7},{7,6},{8,9},{9,8},{10,11... | collective-permute-start | bytes 540680 | tf_op jit(solution)/shard_map/ppermute | solution.py:18
  34.9 2.5 %collective-permute-start.16 = (bf16[32,2816]{1,0:T(8,128)(2,1)S(1)}, bf16[32,2816]{1,0:T(8,128)(2,1)S(1)}, u32[]{:S(2)}, u32[]{:S(2)}) collective-permute-start(bf16[32,2816]{1,0:T(8,128)(2,1)S(1)} %get-tuple-element.104), channel_id=1, source_target_pairs={{0,1},{1,0},{2,3},{3,2},{4,5},{5,4},{6,7},{7,6},{8,9},{9,8},{10,11... | collective-permute-start | bytes 540680 | tf_op jit(solution)/shard_map/ppermute | solution.py:18
  35.0 4.1 %collective-permute-start.17 = (bf16[32,2816]{1,0:T(8,128)(2,1)S(1)}, bf16[32,2816]{1,0:T(8,128)(2,1)S(1)}, u32[]{:S(2)}, u32[]{:S(2)}) collective-permute-start(bf16[32,2816]{1,0:T(8,128)(2,1)S(1)} %get-tuple-element.103), channel_id=1, source_target_pairs={{0,1},{1,0},{2,3},{3,2},{4,5},{5,4},{6,7},{7,6},{8,9},{9,8},{10,11... | collective-permute-start | bytes 540680 | tf_op jit(solution)/shard_map/ppermute | solution.py:18
  35.5 10.1 %collective-permute-start.21 = (bf16[32,2816]{1,0:T(8,128)(2,1)S(1)}, bf16[32,2816]{1,0:T(8,128)(2,1)S(1)}, u32[]{:S(2)}, u32[]{:S(2)}) collective-permute-start(bf16[32,2816]{1,0:T(8,128)(2,1)S(1)} %collective-permute-done.6.refs_1_), channel_id=1, source_target_pairs={{0,1},{1,0},{2,3},{3,2},{4,5},{5,4},{6,7},{7,6},{8,9},{9,8},{10,11... | collective-permute-start | bytes 540680 | tf_op jit(solution)/shard_map/ppermute | solution.py:18
  35.6 10.0 %collective-permute-start.18 = (bf16[32,2816]{1,0:T(8,128)(2,1)S(1)}, bf16[32,2816]{1,0:T(8,128)(2,1)S(1)}, u32[]{:S(2)}, u32[]{:S(2)}) collective-permute-start(bf16[32,2816]{1,0:T(8,128)(2,1)S(1)} %get-tuple-element.69), channel_id=1, source_target_pairs={{0,12},{4,0},{8,4},{12,8},{1,13},{5,1},{9,5},{13,9},{2,14},{6,2},{... | collective-permute-start | bytes 540680 | tf_op jit(solution)/shard_map/ppermute | solution.py:18
  37.4 12.5 %collective-permute-start.25 = (bf16[2,128,768]{2,1,0:T(8,128)(2,1)S(1)}, bf16[2,128,768]{2,1,0:T(8,128)(2,1)S(1)}, u32[]{:S(2)}, u32[]{:S(2)}) collective-permute-start(bf16[2,128,768]{2,1,0:T(8,128)(2,1)S(1)} %get-tuple-element.75.refs_0_), channel_id=1, source_target_pairs={{0,2},{2,0},{1,3},{3,1},{4,6},{6,4},{5,7},{7,5},{8,10},{10,8},{9,1... | collective-permute-start | bytes 1179656 | tf_op jit(solution)/shard_map/ppermute | solution.py:18
  42.6 14.3 %collective-permute-start.29 = (bf16[2,128,768]{2,1,0:T(8,128)(2,1)S(1)}, bf16[2,128,768]{2,1,0:T(8,128)(2,1)S(1)}, u32[]{:S(2)}, u32[]{:S(2)}) collective-permute-start(bf16[2,128,768]{2,1,0:T(8,128)(2,1)S(1)} %get-tuple-element.83.refs_0_), channel_id=1, source_target_pairs={{0,2},{2,0},{1,3},{3,1},{4,6},{6,4},{5,7},{7,5},{8,10},{10,8},{9,1... | collective-permute-start | bytes 1179656 | tf_op jit(solution)/shard_map/ppermute | solution.py:18
  42.9 3.1 %collective-permute-start.19 = (bf16[32,2816]{1,0:T(8,128)(2,1)S(1)}, bf16[32,2816]{1,0:T(8,128)(2,1)S(1)}, u32[]{:S(2)}, u32[]{:S(2)}) collective-permute-start(bf16[32,2816]{1,0:T(8,128)(2,1)S(1)} %get-tuple-element.102), channel_id=1, source_target_pairs={{0,1},{1,0},{2,3},{3,2},{4,5},{5,4},{6,7},{7,6},{8,9},{9,8},{10,11... | collective-permute-start | bytes 540680 | tf_op jit(solution)/shard_map/ppermute | solution.py:18
  45.6 1.4 %collective-permute-start.20 = (bf16[32,2816]{1,0:T(8,128)(2,1)S(1)}, bf16[32,2816]{1,0:T(8,128)(2,1)S(1)}, u32[]{:S(2)}, u32[]{:S(2)}) collective-permute-start(bf16[32,2816]{1,0:T(8,128)(2,1)S(1)} %get-tuple-element.101), channel_id=1, source_target_pairs={{0,1},{1,0},{2,3},{3,2},{4,5},{5,4},{6,7},{7,6},{8,9},{9,8},{10,11... | collective-permute-start | bytes 540680 | tf_op jit(solution)/shard_map/ppermute | solution.py:18
  45.6 1.6 %collective-permute-start.22 = (bf16[32,2816]{1,0:T(8,128)(2,1)S(1)}, bf16[32,2816]{1,0:T(8,128)(2,1)S(1)}, u32[]{:S(2)}, u32[]{:S(2)}) collective-permute-start(bf16[32,2816]{1,0:T(8,128)(2,1)S(1)} %collective-permute-done.18.refs_2_), channel_id=1, source_target_pairs={{0,1},{1,0},{2,3},{3,2},{4,5},{5,4},{6,7},{7,6},{8,9},{9,8},{10,11... | collective-permute-start | bytes 540680 | tf_op jit(solution)/shard_map/ppermute | solution.py:18
  53.7 1.7 %collective-permute-start.26 = (bf16[672,128]{1,0:T(8,128)(2,1)S(1)}, bf16[672,128]{1,0:T(8,128)(2,1)S(1)}, u32[]{:S(2)}, u32[]{:S(2)}) collective-permute-start(bf16[672,128]{1,0:T(8,128)(2,1)S(1)} %get-tuple-element.80), channel_id=1, source_target_pairs={{0,1},{1,0},{2,3},{3,2},{4,5},{5,4},{6,7},{7,6},{8,9},{9,8},{10,11... | collective-permute-start | bytes 516104 | tf_op jit(solution)/shard_map/ppermute | solution.py:18
  54.0 1.4 %collective-permute-start.27 = (bf16[672,128]{1,0:T(8,128)(2,1)S(1)}, bf16[672,128]{1,0:T(8,128)(2,1)S(1)}, u32[]{:S(2)}, u32[]{:S(2)}) collective-permute-start(bf16[672,128]{1,0:T(8,128)(2,1)S(1)} %get-tuple-element.81), channel_id=1, source_target_pairs={{0,1},{1,0},{2,3},{3,2},{4,5},{5,4},{6,7},{7,6},{8,9},{9,8},{10,11... | collective-permute-start | bytes 516104 | tf_op jit(solution)/shard_map/ppermute | solution.py:18
  54.3 11.5 %collective-permute-start.24 = (bf16[2,128,768]{2,1,0:T(8,128)(2,1)S(1)}, bf16[2,128,768]{2,1,0:T(8,128)(2,1)S(1)}, u32[]{:S(2)}, u32[]{:S(2)}) collective-permute-start(bf16[2,128,768]{2,1,0:T(8,128)(2,1)S(1)} %get-tuple-element.74.refs_0_), channel_id=1, source_target_pairs={{0,2},{2,0},{1,3},{3,1},{4,6},{6,4},{5,7},{7,5},{8,10},{10,8},{9,1... | collective-permute-start | bytes 1179656 | tf_op jit(solution)/shard_map/ppermute | solution.py:18
  55.5 10.3 %collective-permute-start.28 = (bf16[1344,128]{1,0:T(8,128)(2,1)S(1)}, bf16[1344,128]{1,0:T(8,128)(2,1)S(1)}, u32[]{:S(2)}, u32[]{:S(2)}) collective-permute-start(bf16[1344,128]{1,0:T(8,128)(2,1)S(1)} %add.4), channel_id=1, source_target_pairs={{0,12},{4,0},{8,4},{12,8},{1,13},{5,1},{9,5},{13,9},{2,14},{6,2},{... | collective-permute-start | bytes 1032200 | tf_op jit(solution)/shard_map/ppermute | solution.py:18
  60.6 1.5 %collective-permute-start.30 = (bf16[672,128]{1,0:T(8,128)(2,1)S(1)}, bf16[672,128]{1,0:T(8,128)(2,1)S(1)}, u32[]{:S(2)}, u32[]{:S(2)}) collective-permute-start(bf16[672,128]{1,0:T(8,128)(2,1)S(1)} %get-tuple-element.87), channel_id=1, source_target_pairs={{0,1},{1,0},{2,3},{3,2},{4,5},{5,4},{6,7},{7,6},{8,9},{9,8},{10,11... | collective-permute-start | bytes 516104 | tf_op jit(solution)/shard_map/ppermute | solution.py:18
  60.7 1.6 %collective-permute-start.31 = (bf16[672,128]{1,0:T(8,128)(2,1)S(1)}, bf16[672,128]{1,0:T(8,128)(2,1)S(1)}, u32[]{:S(2)}, u32[]{:S(2)}) collective-permute-start(bf16[672,128]{1,0:T(8,128)(2,1)S(1)} %get-tuple-element.88), channel_id=1, source_target_pairs={{0,1},{1,0},{2,3},{3,2},{4,5},{5,4},{6,7},{7,6},{8,9},{9,8},{10,11... | collective-permute-start | bytes 516104 | tf_op jit(solution)/shard_map/ppermute | solution.py:18
  62.4 12.3 %collective-permute-start.34 = (bf16[1344,128]{1,0:T(8,128)(2,1)S(1)}, bf16[1344,128]{1,0:T(8,128)(2,1)S(1)}, u32[]{:S(2)}, u32[]{:S(2)}) collective-permute-start(bf16[1344,128]{1,0:T(8,128)(2,1)S(1)} %add.5), channel_id=1, source_target_pairs={{0,4},{4,8},{8,12},{12,0},{1,5},{5,9},{9,13},{13,1},{2,6},{6,10},{... | collective-permute-start | bytes 1032200 | tf_op jit(solution)/shard_map/ppermute | solution.py:18
  63.4 11.5 %collective-permute-start.23 = (bf16[2,128,768]{2,1,0:T(8,128)(2,1)S(1)}, bf16[2,128,768]{2,1,0:T(8,128)(2,1)S(1)}, u32[]{:S(2)}, u32[]{:S(2)}) collective-permute-start(bf16[2,128,768]{2,1,0:T(8,128)(2,1)S(1)} %get-tuple-element.73.refs_0_), channel_id=1, source_target_pairs={{0,2},{2,0},{1,3},{3,1},{4,6},{6,4},{5,7},{7,5},{8,10},{10,8},{9,1... | collective-permute-start | bytes 1179656 | tf_op jit(solution)/shard_map/ppermute | solution.py:18
  69.5 1.5 %collective-permute-start.32 = (bf16[672,128]{1,0:T(8,128)(2,1)S(1)}, bf16[672,128]{1,0:T(8,128)(2,1)S(1)}, u32[]{:S(2)}, u32[]{:S(2)}) collective-permute-start(bf16[672,128]{1,0:T(8,128)(2,1)S(1)} %get-tuple-element.94), channel_id=1, source_target_pairs={{0,1},{1,0},{2,3},{3,2},{4,5},{5,4},{6,7},{7,6},{8,9},{9,8},{10,11... | collective-permute-start | bytes 516104 | tf_op jit(solution)/shard_map/ppermute | solution.py:18
  69.6 1.6 %collective-permute-start.33 = (bf16[672,128]{1,0:T(8,128)(2,1)S(1)}, bf16[672,128]{1,0:T(8,128)(2,1)S(1)}, u32[]{:S(2)}, u32[]{:S(2)}) collective-permute-start(bf16[672,128]{1,0:T(8,128)(2,1)S(1)} %get-tuple-element.95), channel_id=1, source_target_pairs={{0,1},{1,0},{2,3},{3,2},{4,5},{5,4},{6,7},{7,6},{8,9},{9,8},{10,11... | collective-permute-start | bytes 516104 | tf_op jit(solution)/shard_map/ppermute | solution.py:18
  74.8 11.3 %collective-permute-start.37 = (bf16[1344,128]{1,0:T(8,128)(2,1)S(1)}, bf16[1344,128]{1,0:T(8,128)(2,1)S(1)}, u32[]{:S(2)}, u32[]{:S(2)}) collective-permute-start(bf16[1344,128]{1,0:T(8,128)(2,1)S(1)} %add.6), channel_id=1, source_target_pairs={{0,4},{4,8},{8,12},{12,0},{1,5},{5,9},{9,13},{13,1},{2,6},{6,10},{... | collective-permute-start | bytes 1032200 | tf_op jit(solution)/shard_map/ppermute | solution.py:18
  78.6 1.5 %collective-permute-start.35 = (bf16[672,128]{1,0:T(8,128)(2,1)S(1)}, bf16[672,128]{1,0:T(8,128)(2,1)S(1)}, u32[]{:S(2)}, u32[]{:S(2)}) collective-permute-start(bf16[672,128]{1,0:T(8,128)(2,1)S(1)} %get-tuple-element.99), channel_id=1, source_target_pairs={{0,1},{1,0},{2,3},{3,2},{4,5},{5,4},{6,7},{7,6},{8,9},{9,8},{10,11... | collective-permute-start | bytes 516104 | tf_op jit(solution)/shard_map/ppermute | solution.py:18
  78.7 1.6 %collective-permute-start.36 = (bf16[672,128]{1,0:T(8,128)(2,1)S(1)}, bf16[672,128]{1,0:T(8,128)(2,1)S(1)}, u32[]{:S(2)}, u32[]{:S(2)}) collective-permute-start(bf16[672,128]{1,0:T(8,128)(2,1)S(1)} %get-tuple-element.100), channel_id=1, source_target_pairs={{0,1},{1,0},{2,3},{3,2},{4,5},{5,4},{6,7},{7,6},{8,9},{9,8},{10,11... | collective-permute-start | bytes 516104 | tf_op jit(solution)/shard_map/ppermute | solution.py:18
